TPU v7x, 32 devices: a whole 2x2x4 slice. The times are simulated.
32 devices in a mesh: batch: 2 (over y), freq: 8 (over z, x), elem: 2 (over core).
Axes of the slice: x: 2, y: 2, z: 4, core: 2. Of those that a mesh axis runs over, the one named last changes fastest.
Arguments:
- flaw_cells: int32 [512], P('batch'), parts along dimension 0, may hold values from 0 to 255, each once
- flaw_blocks: int32 [16], P('batch'), parts along dimension 0, may hold values from 0 to 7, each once
- element_channel: int32 [256], P('elem'), may hold values from 0 to 255, each once
- focal_delay: float32 [256, 256], replicated, may hold values from 0 to 64
- beam_field: bfloat16 [128, 2, 256, 256], P('freq', None, 'elem'), may hold values from -0.125 to 0.125
- flaw_size: float32 [4, 128], P('batch'), parts along dimension 0, may hold values from 0.5 to 4
- flaw_slope: float32 [4, 128], P('batch'), parts along dimension 0, may hold values from 0.2 to 1
- noise_level: float32 [4, 128], P(('batch', 'elem'), 'freq'), parts along dimension 0, may hold values from 0.5 to 5
Outputs:
- flaw_peak: float32 [4, 128], P(('batch', 'elem'), 'freq'), parts along dimension 0
- detection: float32 [4, 128], P(('batch', 'elem'), 'freq'), parts along dimension 0
There are 2 independent parts, one for each index of `batch`. A program takes and returns all parts, laid end to end along the dimension named above; an argument that names none is the same for every part. Nothing has to cross between parts.
Inputs may be any that keep to these rules, and one draw needn't show every extreme that they name: `flaw_cells`: every site holds exactly one flaw. `flaw_blocks`: every scan block belongs to exactly one flaw group. `element_channel`: every channel drives exactly one element.
All inputs are finite; a program needn't handle non-finite values.
Results may differ from a plain program's by a relative error of at most 0.0011.
Values may be sent and summed in bfloat16 or wider, within the bound.
No kernel may reach another device: no remote copies, remote signals or barrier semaphores. Data moves between devices by JAX's collectives and lax.ppermute only.
A program may use at most 64 MiB of HBM per device.

v0:
```python
import functools
import math

import jax
import jax.numpy as jnp
from jax import lax
from jax.experimental import pallas as pl
from jax.experimental.pallas import tpu as pltpu
from jax.sharding import PartitionSpec as P

W_DEV = 16
W_HALF = W_DEV // 2
FG = 128
NB = 4
SB = 32
T_CAP = 1024

EDGE = 0.6
STEEP = 3.0
EPS = 1e-05

ROWS = NB * SB
VMEM_BYTES = 48 * 1024 * 1024


def sin_half_turn(turns):
    angle = turns * math.pi
    square = angle * angle
    sine = 1.0 / 6227020800.0
    for factorial in (-39916800.0, 362880.0, -5040.0, 120.0, -6.0, 1.0):
        sine = sine * square + 1.0 / factorial
    cosine = 1.0 / 479001600.0
    for factorial in (-3628800.0, 40320.0, -720.0, 24.0, -2.0, 1.0):
        cosine = cosine * square + 1.0 / factorial
    return sine * angle, cosine


def sincos_turns(turns):
    rest = turns - jnp.floor(turns + 0.5)
    sine, cosine = sin_half_turn(rest)
    return 2.0 * sine * cosine, 1.0 - 2.0 * sine * sine


def dot(left, right, contract):
    return lax.dot_general(
        left, right, (contract, ((), ())), preferred_element_type=jnp.float32
    )


def slot_masks(slots):
    half = slots // 2
    between = (2, half, half + 1, 3, slots - 1)
    return (0, 1, *between, slots - 2), (0, slots - 2, *between, 1)


def partner(slots, slot):
    index = lax.axis_index("freq")
    inner = ((index * 2) ^ index) & (slots // 2) != 0
    outer_masks, inner_masks = slot_masks(slots)
    mask = jnp.zeros_like(slot)
    for s in range(1, slots):
        mask = jnp.where(slot == s, jnp.where(inner, inner_masks[s], outer_masks[s]), mask)
    return mask ^ index


def slot_order(slots):
    size = FG // slots
    row = lax.broadcasted_iota(jnp.int32, (FG, 1), 0)
    column = lax.broadcasted_iota(jnp.int32, (FG, FG), 1)
    if slots > 1:
        row = partner(slots, row // size) * size + row % size
    return row == column


def flaw_pick(order, which, cells_ref):
    cells = jnp.where(which == 0, cells_ref[:, :FG], cells_ref[:, FG:])
    cell_sel = lax.broadcasted_iota(jnp.int32, (cells_ref.shape[1], FG), 0) == cells
    return dot(
        order.astype(jnp.bfloat16), cell_sel.astype(jnp.bfloat16), ((1,), (1,))
    ).astype(jnp.bfloat16)


def delays_of(channel_ref, delay_ref, blocks_ref, groups, elements):
    lane = lax.broadcasted_iota(jnp.int32, (1, 2 * ROWS), 1)
    position = lane & (SB - 1)
    for j in range(2 * NB):
        block = blocks_ref[groups[j // NB] * NB + j % NB]
        position = position + jnp.where((lane >> 5) == j, block * SB, 0)
    channels, positions = delay_ref.shape
    scan_sel = (
        lax.broadcasted_iota(jnp.int32, (positions, 2 * ROWS), 0) == position
    ).astype(jnp.bfloat16)
    channel_sel = (
        (lax.broadcasted_iota(jnp.int32, (channels, elements), 0) == channel_ref[...])
        .astype(jnp.float32)
        .T.astype(jnp.bfloat16)
    )
    rest = delay_ref[...]
    pieces = []
    for _ in range(3):
        pieces.append(rest.astype(jnp.bfloat16))
        rest = rest - pieces[-1].astype(jnp.float32)
    moved = jnp.concatenate(
        [dot(channel_sel, piece, ((1,), (0,))).astype(jnp.bfloat16) for piece in pieces], axis=0
    )
    moved = dot(moved, scan_sel, ((1,), (0,)))
    return moved[:elements] + moved[elements : 2 * elements] + moved[2 * elements :]


def turned(law, step):
    return law[0] * step[0] - law[1] * step[1], law[1] * step[0] + law[0] * step[1]


def focal_base(freq_total, delays):
    first_freq = lax.axis_index("freq") * W_DEV
    phase = delays * (0.5 / freq_total)
    unit = sincos_turns(phase)[::-1]
    base = sincos_turns(phase * first_freq.astype(jnp.float32))[::-1]
    return base, turned(unit, unit), turned(base, unit)


def kirchhoff(freq_total, order, which, size_ref, slope_ref):
    first_freq = lax.axis_index("freq") * W_DEV
    size = size_ref[pl.ds(which, 1), :]
    turn = size * slope_ref[pl.ds(which, 1), :] * (1.0 / freq_total)
    size = jnp.sum(jnp.where(order, size, 0.0), axis=1, keepdims=True)
    turn = jnp.sum(jnp.where(order, turn, 0.0), axis=1, keepdims=True)
    freq = first_freq + lax.broadcasted_iota(jnp.int32, (FG, FG), 1)
    sine, cosine = sincos_turns(turn * freq.astype(jnp.float32))
    return size * (1.0 + EDGE) * cosine, size * (EDGE - 1.0) * sine


def store_law(law_ref, law, step):
    elements = law_ref.shape[1] // 2
    for w in range(W_HALF):
        c = law[0].astype(jnp.bfloat16)
        s = law[1].astype(jnp.bfloat16)
        law_ref[w, :elements, :ROWS] = c
        law_ref[w, :elements, ROWS:] = -s
        law_ref[w, elements:, :ROWS] = s
        law_ref[w, elements:, ROWS:] = c
        if w < W_HALF - 1:
            law = turned(law, step)


def pick_fields(parity, picks, field_ref, picked_refs):
    elements, sites = field_ref.shape[3:]
    for w in range(W_HALF):
        picked = dot(
            picks, field_ref[w, parity].reshape(2 * elements, sites), ((1,), (1,))
        ).astype(jnp.bfloat16)
        for i, ref in enumerate(picked_refs):
            ref[w] = picked[i * FG : (i + 1) * FG]


def store_spectra(parity, picked_ref, law_ref, k_real, k_imag, out_ref, first):
    for w in range(W_HALF):
        product = dot(picked_ref[w], law_ref[w], ((1,), (0,)))
        real_part = product[:, :ROWS]
        imag_part = product[:, ROWS:]
        kr = k_real[:, 2 * w + parity : 2 * w + parity + 1]
        ki = k_imag[:, 2 * w + parity : 2 * w + parity + 1]
        out_ref[first + 2 * w] = (kr * real_part - ki * imag_part).astype(jnp.bfloat16)
        out_ref[first + 2 * w + 1] = (kr * imag_part + ki * real_part).astype(jnp.bfloat16)


def other_even_kernel(freq_total, slots, *refs):
    field_hbm, *small_hbm = refs[:7]
    out_ref, own_picked_ref, field_ref, size_ref, slope_ref, *kept = refs[7:20]
    delay_ref, channel_ref, blocks_ref, cells_ref = refs[20:24]
    field_sem, small_sem, *scratch = refs[24:]
    small = (delay_ref, channel_ref, blocks_ref, cells_ref, size_ref, slope_ref)
    picked_ref, law_ref = scratch
    copies = [
        pltpu.make_async_copy(source, target, small_sem.at[i])
        for i, (source, target) in enumerate(zip(small_hbm, small))
    ]
    for copy in copies:
        copy.start()
    field_copies = [
        pltpu.make_async_copy(
            field_hbm.at[:, parity], field_ref.at[:, parity], field_sem.at[parity]
        )
        for parity in range(2)
    ]
    for copy in field_copies:
        copy.start()
    order = slot_order(slots)
    for copy in copies:
        copy.wait()
    group = lax.axis_index("elem")
    groups = (1 - group, group)
    picks = jnp.concatenate(
        [flaw_pick(order, which, cells_ref) for which in groups], axis=0
    )
    factors = kirchhoff(freq_total, order, groups[0], size_ref, slope_ref)
    delays = delays_of(channel_ref, delay_ref, blocks_ref, groups, field_ref.shape[3])
    even, step, odd = focal_base(freq_total, delays[:, :ROWS])
    values = (picks, *step, *odd, *factors, delays[:, ROWS:])
    for ref, value in zip(kept, values):
        ref[...] = value
    store_law(law_ref, even, step)

    field_copies[0].wait()
    pick_fields(0, picks, field_ref, (picked_ref, own_picked_ref))
    store_spectra(0, picked_ref, law_ref, *factors, out_ref, 0)
    field_copies[1].wait()


def other_odd_kernel(field_ref, picks_ref, *refs):
    step, odd, k_refs = refs[:2], refs[2:4], refs[4:6]
    out_ref, own_picked_ref, picked_ref, law_ref = refs[6:]
    store_law(law_ref, [ref[...] for ref in odd], [ref[...] for ref in step])
    pick_fields(1, picks_ref[...], field_ref, (picked_ref, own_picked_ref))
    store_spectra(1, picked_ref, law_ref, *k_refs, out_ref, 0)


def own_kernel(freq_total, slots, *refs):
    picked_refs, (delays_ref, size_ref, slope_ref, out_ref, law_ref) = refs[:2], refs[2:]
    even, step, odd = focal_base(freq_total, delays_ref[...])
    for parity, law in enumerate((even, odd)):
        store_law(law_ref.at[parity], law, step)
    group = lax.axis_index("elem")
    factors = kirchhoff(freq_total, slot_order(slots), group, size_ref, slope_ref)
    for parity in range(2):
        store_spectra(
            parity, picked_refs[parity], law_ref.at[parity], *factors, out_ref, parity * W_DEV
        )


def call(kernel, name, in_specs, out_shape, scratch):
    vmem = pl.BlockSpec(memory_space=pltpu.VMEM)
    return pl.pallas_call(
        kernel,
        in_specs=in_specs,
        out_specs=[vmem] * len(out_shape),
        out_shape=out_shape,
        scratch_shapes=scratch,
        compiler_params=pltpu.CompilerParams(vmem_limit_bytes=VMEM_BYTES),
        cost_estimate=pl.CostEstimate(flops=1000, bytes_accessed=1000, transcendentals=0),
        name=name,
    )


def partials(field, small, swap, freq_total, slots):
    elements, sites = field.shape[3:]
    vmem = pl.BlockSpec(memory_space=pltpu.VMEM)
    hbm = pl.BlockSpec(memory_space=pltpu.HBM)
    pinned = [pltpu.with_memory_space_constraint(a, pltpu.HBM) for a in (field, *small)]
    out = jax.ShapeDtypeStruct((W_DEV, FG, ROWS), jnp.bfloat16)
    picked = jax.ShapeDtypeStruct((W_HALF, FG, 2 * elements), jnp.bfloat16)
    law = (W_HALF, 2 * elements, 2 * ROWS)
    base = [jax.ShapeDtypeStruct((elements, ROWS), jnp.float32)] * 2
    factors = [jax.ShapeDtypeStruct((FG, FG), jnp.float32)] * 2
    kept = [jax.ShapeDtypeStruct((2 * FG, sites), jnp.bfloat16), *base, *base, *factors]
    copied = [jax.ShapeDtypeStruct(a.shape, a.dtype) for a in (field, *small[4:])]
    work = [pltpu.VMEM(picked.shape, picked.dtype), pltpu.VMEM(law, jnp.bfloat16)]
    even, even_picked, field, size, slope, *kept, delays = call(
        functools.partial(other_even_kernel, freq_total, slots),
        "other_even",
        [hbm] * len(pinned),
        [out, picked, *copied, *kept, base[0]],
        [
            pltpu.SMEM(a.shape, a.dtype) if a.ndim == 1 else pltpu.VMEM(a.shape, a.dtype)
            for a in small[:4]
        ]
        + [pltpu.SemaphoreType.DMA((2,)), pltpu.SemaphoreType.DMA((len(small),)), *work],
    )(*pinned)
    even = lax.ppermute(even, "elem", swap)
    odd, odd_picked = call(
        other_odd_kernel, "other_odd", [vmem] * 8, [out, picked], work
    )(field, *kept)
    odd = lax.ppermute(odd, "elem", swap)
    (own,) = call(
        functools.partial(own_kernel, freq_total, slots),
        "own",
        [vmem] * 5,
        [jax.ShapeDtypeStruct((2 * W_DEV, FG, ROWS), jnp.bfloat16)],
        [pltpu.VMEM((2, *law), jnp.bfloat16)],
    )(even_picked, odd_picked, delays, size, slope)
    return own, even, odd


def total(own_ref, moved_ref, parity, rows):
    own = own_ref[parity * W_DEV : (parity + 1) * W_DEV, rows]
    both = own.astype(jnp.float32) + moved_ref[:, rows].astype(jnp.float32)
    return jnp.swapaxes(both, 0, 1).astype(jnp.bfloat16)


def add_even_kernel(size, own_ref, even_ref, held_ref):
    for first in range(0, held_ref.shape[0], size):
        rows = pl.ds(first, size)
        held_ref[rows] = total(own_ref, even_ref, 0, rows)


def add_odd_kernel(own_ref, odd_ref, held_ref, *refs):
    size = refs[0].shape[0]
    for slot, ref in enumerate(refs):
        rows = pl.ds(slot * size, size)
        ref[:, :W_DEV] = held_ref[rows]
        ref[:, W_DEV:] = total(own_ref, odd_ref, 1, rows)


def add(own, even, odd, slots):
    vmem = pl.BlockSpec(memory_space=pltpu.VMEM)
    planes, flaws, rows = own.shape
    size = flaws // slots
    shape = jax.ShapeDtypeStruct((flaws, planes // 2, rows), own.dtype)
    kernel = functools.partial(add_even_kernel, min(size, 16))
    (held,) = call(kernel, "add_even", [vmem] * 2, [shape], [])(own, even)
    shapes = [jax.ShapeDtypeStruct((size, planes, rows), own.dtype)] * slots
    return call(add_odd_kernel, "add_odd", [vmem] * 3, shapes, [])(own, odd, held)


def table_kernel(freq_total, slots, table_ref):
    height, depth = table_ref.shape[2:]
    time_block = height // 2
    row = lax.broadcasted_iota(jnp.int32, (height, depth // 2), 0)
    column = lax.broadcasted_iota(jnp.int32, (height, depth // 2), 1)
    out_imag = (row >= time_block).astype(jnp.int32)
    time = pl.program_id(0) * time_block + row - out_imag * time_block
    for parity in range(2):
        freq = (column >> 1) * 2 + parity
        if slots > 1:
            lane = lax.broadcasted_iota(jnp.int32, (1, depth // 2), 1)
            lane = (lane >> 1) * 2 + parity
            freq = partner(slots, lane // W_DEV) * W_DEV + lane % W_DEV
        steps = freq * time + ((column & 1) - out_imag) * (freq_total // 2)
        steps = (steps + 2 * freq_total) & (2 * freq_total - 1)
        _, value = sincos_turns(steps.astype(jnp.float32) * (0.5 / freq_total))
        high = value.astype(jnp.bfloat16)
        table_ref[0, parity, :, : depth // 2] = high
        table_ref[0, parity, :, depth // 2 :] = (
            value - high.astype(jnp.float32)
        ).astype(jnp.bfloat16)


def table(freq_total, slots, times, time_block):
    blocks = times // time_block
    shape = (blocks, 2, 2 * time_block, 2 * freq_total)
    return pl.pallas_call(
        functools.partial(table_kernel, freq_total, slots),
        grid=(blocks,),
        out_specs=pl.BlockSpec((1, *shape[1:]), lambda i: (i, 0, 0, 0)),
        out_shape=jax.ShapeDtypeStruct(shape, jnp.bfloat16),
        compiler_params=pltpu.CompilerParams(vmem_limit_bytes=VMEM_BYTES),
        name="table",
    )()


def peak_kernel(freq_total, folded, sources, blocks, *refs):
    def first_step():
        return blocks == 1 or pl.program_id(0) == 0

    def last_step():
        return blocks == 1 or pl.program_id(0) == blocks - 1

    count = len(refs) - 5
    table_ref, noise_ref, peak_ref, found_ref, best_ref = refs[count:]
    columns = peak_ref.shape[1]
    time_block = table_ref.shape[2] // 2

    @pl.when(first_step())
    def _():
        best_ref[...] = jnp.zeros_like(best_ref)

    width = min(2, columns)
    for first in range(0, columns, width):
        parts = []
        for parity in range(2):
            planes = slice(parity * W_DEV, (parity + 1) * W_DEV)
            spectra = jnp.concatenate(
                [
                    jnp.concatenate(
                        [
                            refs[i][row + first + k, planes, :]
                            for i, row in sources
                        ]
                        * 2,
                        axis=0,
                    )
                    for k in range(width)
                ],
                axis=1,
            )
            parts.append(dot(table_ref[0, parity], spectra, ((1,), (0,))))
        powers = []
        for signal in [parts[0] + parts[1]] + [parts[0] - parts[1]] * folded:
            real_part = signal[:time_block]
            imag_part = signal[time_block:]
            powers.append(real_part * real_part + imag_part * imag_part)
        power = jnp.maximum(powers[0], powers[-1]) if folded else powers[0]
        power = jnp.max(power, axis=0, keepdims=True)
        for k in range(width):
            row = pl.ds(first + k, 1)
            best_ref[row, :] = jnp.maximum(
                best_ref[row, :], power[:, k * ROWS : (k + 1) * ROWS]
            )

    @pl.when(last_step())
    def _():
        largest = jnp.max(best_ref[...], axis=1, keepdims=True)
        shape = best_ref.shape
        diagonal = lax.broadcasted_iota(jnp.int32, shape, 0) == lax.broadcasted_iota(
            jnp.int32, shape, 1
        )
        largest = jnp.max(jnp.where(diagonal, largest, 0.0), axis=0, keepdims=True)
        peak = jnp.sqrt(largest[:, :columns]) * (1.0 / math.sqrt(freq_total))
        score = STEEP * (jnp.log(peak + EPS) - jnp.log(noise_ref[...]))
        peak_ref[...] = peak
        found_ref[...] = 1.0 / (1.0 + jnp.exp(-score))


def peaks(spectra, sources, twiddles, noise_level, freq_total, folded):
    columns = noise_level.shape[1]
    blocks = twiddles.shape[0]
    if blocks == 1:
        vmem = pl.BlockSpec(memory_space=pltpu.VMEM)
        grid, in_specs, out_spec = (), [vmem] * (len(spectra) + 2), vmem
    else:
        grid = (blocks,)
        out_spec = pl.BlockSpec((1, columns), lambda i: (0, 0))
        in_specs = [pl.BlockSpec(a.shape, lambda i: (0, 0, 0)) for a in spectra]
        in_specs += [
            pl.BlockSpec((1, *twiddles.shape[1:]), lambda i: (i, 0, 0, 0)),
            out_spec,
        ]
    return pl.pallas_call(
        functools.partial(peak_kernel, freq_total, folded, sources, blocks),
        grid=grid,
        in_specs=in_specs,
        out_specs=[out_spec, out_spec],
        out_shape=[jax.ShapeDtypeStruct((1, columns), jnp.float32)] * 2,
        scratch_shapes=[pltpu.VMEM((max(8, columns), ROWS), jnp.float32)],
        compiler_params=pltpu.CompilerParams(vmem_limit_bytes=VMEM_BYTES),
        name="peaks",
    )(*spectra, twiddles, noise_level)


def body(
    flaw_cells,
    flaw_blocks,
    element_channel,
    focal_delay,
    beam_field,
    flaw_size,
    flaw_slope,
    noise_level,
):
    freq_count = lax.axis_size("freq")
    freq_total = W_DEV * freq_count
    sample_count = min(T_CAP, 2 * freq_total)
    swap = [(0, 1), (1, 0)]
    direct = freq_count == 8
    slots = freq_count if direct else 1
    small = (
        focal_delay,
        element_channel.reshape(1, -1),
        flaw_blocks,
        flaw_cells.reshape(1, -1),
        flaw_size,
        flaw_slope,
    )
    folded = sample_count == 2 * freq_total
    times = sample_count // 2 if folded else sample_count
    twiddles = table(freq_total, slots, times, min(128, times))
    field = beam_field.reshape(W_HALF, 2, *beam_field.shape[1:])
    parts = add(*partials(field, small, swap, freq_total, slots), slots)
    if direct:
        half = slots // 2
        spectra = []
        for slot, masks in enumerate(zip(*slot_masks(slots))):
            pairs = [(a, a ^ masks[((2 * a) ^ a) & half != 0]) for a in range(slots)]
            spectra.append(lax.ppermute(parts[slot], "freq", pairs) if slot else parts[slot])
        spectra = [*spectra[1:], spectra[0]]
        sources = [((slot - 1) % slots, 0) for slot in range(slots)]
    else:
        spectra = [
            lax.all_to_all(parts[0], "freq", split_axis=0, concat_axis=0, tiled=True)
        ]
        sources = [(0, s * (FG // freq_count)) for s in range(freq_count)]
    return tuple(peaks(spectra, sources, twiddles, noise_level, freq_total, folded))


def solution(mesh):
    in_specs = (
        P("batch"),
        P("batch"),
        P("elem"),
        P(),
        P("freq", None, "elem", None),
        P("batch", None),
        P("batch", None),
        P(("batch", "elem"), "freq"),
    )
    out_specs = (P(("batch", "elem"), "freq"), P(("batch", "elem"), "freq"))
    return jax.shard_map(body, mesh=mesh, in_specs=in_specs, out_specs=out_specs, check_vma=False)
```

profile of v0, /device:TPU:0, one launch (start us, length us, event | category | flops | bytes accessed | tf_op | source)
XLA Modules:
  0.0 34.7 jit_solution(17171019974703624864)
XLA Ops:
  0.6 2.7 %other_even.1 = (bf16[16,128,128]{2,1,0:T(8,128)(2,1)S(1)}, bf16[8,128,256]{2,1,0:T(8,128)(2,1)S(1)}, bf16[8,2,2,128,256]{4,3,2,1,0:T(8,128)(2,1)S(1)}, f32[2,12...) custom-call(bf16[8,2,2,128,256]{4,3,2,1,0:T(8,128)(2,1)} %bitcast.3,, ...), custom_call_target="tpu_custom_call" | custom-call | flops 1000 | bytes 1000 | tf_op jit(solution)/shard_map/other_even/pallas_call | solution.py:258
  3.3 0.5 %collective-permute-start.1 = (bf16[16,128,128]{2,1,0:T(8,128)(2,1)S(1)}, bf16[16,128,128]{2,1,0:T(8,128)(2,1)S(1)}, u32[]{:S(2)}, u32[]{:S(2)}) collective-permute-start(bf16[16,128,128]{2,1,0:T(8,128)(2,1)S(1)} %get-tuple-element.39), channel_id=1, source_target_pairs={{0,1},{1,0},{2,3},{3,2},{4,5},{5,4},{6,7},{7,6},{8,9},{9,8},{10,11... | collective-permute-start | bytes 1572872 | tf_op jit(solution)/shard_map/ppermute | solution.py:269
  3.8 0.8 %other_odd.1 = (bf16[16,128,128]{2,1,0:T(8,128)(2,1)S(1)}, bf16[8,128,256]{2,1,0:T(8,128)(2,1)S(1)}) custom-call(bf16[8,2,2,128,256]{4,3,2,1,0:T(8,128)(2,1)S(1)} %get-tuple-element.26.field_ref, bf16[256,256]{1,0:T(8,128)(2,1)S(1)} %get-tuple-element.27.picks_ref, f32[128,128]{1,0:T(8,128)S(1)} %get-tuple-element.28.refs_0_, ...), custom_call_target="tpu_custom_call" | custom-call | flops 1000 | bytes 1000 | tf_op jit(solution)/shard_map/other_odd/pallas_call | solution.py:270
  4.6 0.1 collective-permute-start
  4.7 1.3 %own.1.own_ref = bf16[32,128,128]{2,1,0:T(8,128)(2,1)S(1)} custom-call(bf16[8,128,256]{2,1,0:T(8,128)(2,1)S(1)} %get-tuple-element.25.refs_0_, bf16[8,128,256]{2,1,0:T(8,128)(2,1)S(1)} %get-tuple-element.34.refs_1_, f32[128,128]{1,0:T(8,128)S(1)} %get-tuple-element.35.refs_2_, f32[2,128]{1,0:T(2,128)S(1)} %get-tuple-element.36.refs_3_, ...), custom_call_target="tpu_custom_call" | custom-call | flops 1000 | bytes 1000 | tf_op jit(solution)/shard_map/own/pallas_call | solution.py:274
  6.0 0.0 copy-start
  6.0 0.0 collective-permute-done.1.even_ref
  6.0 0.3 add_even.1.held_ref
  6.4 0.2 collective-permute-done.odd_ref
  6.6 0.3 add_odd.1
  6.9 2.8 %collective-permute-start.2 = (bf16[16,32,128]{2,1,0:T(8,128)(2,1)S(1)}, bf16[16,32,128]{2,1,0:T(8,128)(2,1)S(1)}, u32[]{:S(2)}, u32[]{:S(2)}) collective-permute-start(bf16[16,32,128]{2,1,0:T(8,128)(2,1)S(1)} %get-tuple-element.40), channel_id=1, source_target_pairs={{0,2},{2,0},{4,8},{6,10},{8,4},{10,6},{12,14},{14,12},{1,3},{3,1},... | collective-permute-start | bytes 393224 | tf_op jit(solution)/shard_map/ppermute | solution.py:474
  9.7 1.7 %collective-permute-start.3 = (bf16[16,32,128]{2,1,0:T(8,128)(2,1)S(1)}, bf16[16,32,128]{2,1,0:T(8,128)(2,1)S(1)}, u32[]{:S(2)}, u32[]{:S(2)}) collective-permute-start(bf16[16,32,128]{2,1,0:T(8,128)(2,1)S(1)} %get-tuple-element.41), channel_id=1, source_target_pairs={{0,4},{2,6},{4,0},{6,2},{8,12},{10,14},{12,8},{14,10},{1,5},{3,7},... | collective-permute-start | bytes 393224 | tf_op jit(solution)/shard_map/ppermute | solution.py:474
  11.4 2.5 %collective-permute-start.4 = (bf16[16,32,128]{2,1,0:T(8,128)(2,1)S(1)}, bf16[16,32,128]{2,1,0:T(8,128)(2,1)S(1)}, u32[]{:S(2)}, u32[]{:S(2)}) collective-permute-start(bf16[16,32,128]{2,1,0:T(8,128)(2,1)S(1)} %get-tuple-element.42), channel_id=1, source_target_pairs={{0,8},{2,10},{4,12},{6,14},{8,0},{10,2},{12,4},{14,6},{1,9},{3,11}... | collective-permute-start | bytes 393224 | tf_op jit(solution)/shard_map/ppermute | solution.py:474
  13.9 1.3 %collective-permute-start.5 = (bf16[16,32,128]{2,1,0:T(8,128)(2,1)S(1)}, bf16[16,32,128]{2,1,0:T(8,128)(2,1)S(1)}, u32[]{:S(2)}, u32[]{:S(2)}) collective-permute-start(bf16[16,32,128]{2,1,0:T(8,128)(2,1)S(1)} %get-tuple-element.43), channel_id=1, source_target_pairs={{0,10},{2,8},{4,14},{6,12},{8,2},{10,0},{12,6},{14,4},{1,11},{3,9}... | collective-permute-start | bytes 393224 | tf_op jit(solution)/shard_map/ppermute | solution.py:474
  15.2 0.3 collective-permute-start.6
  15.6 0.0 collective-permute-done.2.refs_0_
  15.6 3.6 %collective-permute-start.7 = (bf16[16,32,128]{2,1,0:T(8,128)(2,1)S(1)}, bf16[16,32,128]{2,1,0:T(8,128)(2,1)S(1)}, u32[]{:S(2)}, u32[]{:S(2)}) collective-permute-start(bf16[16,32,128]{2,1,0:T(8,128)(2,1)S(1)} %get-tuple-element.45), channel_id=1, source_target_pairs={{0,14},{2,12},{4,10},{6,8},{8,6},{10,4},{12,2},{14,0},{1,15},{3,13... | collective-permute-start | bytes 393224 | tf_op jit(solution)/shard_map/ppermute | solution.py:474
  19.1 0.0 collective-permute-done.3.refs_1_
  19.2 1.5 %collective-permute-start.8 = (bf16[16,32,128]{2,1,0:T(8,128)(2,1)S(1)}, bf16[16,32,128]{2,1,0:T(8,128)(2,1)S(1)}, u32[]{:S(2)}, u32[]{:S(2)}) collective-permute-start(bf16[16,32,128]{2,1,0:T(8,128)(2,1)S(1)} %get-tuple-element.46), channel_id=1, source_target_pairs={{0,12},{2,14},{4,6},{6,4},{8,10},{10,8},{12,0},{14,2},{1,13},{3,15... | collective-permute-start | bytes 393224 | tf_op jit(solution)/shard_map/ppermute | solution.py:474
  20.6 0.3 table.1.refs_8_
  21.0 3.4 %collective-permute-done.4.refs_2_ = bf16[16,32,128]{2,1,0:T(8,128)(2,1)S(1)} collective-permute-done((bf16[16,32,128]{2,1,0:T(8,128)(2,1)S(1)}, bf16[16,32,128]{2,1,0:T(8,128)(2,1)S(1)}, u32[]{:S(2)}, u32[]{:S(2)}) %collective-permute-start.4) | collective-permute-done | bytes 131104 | tf_op jit(solution)/shard_map/ppermute | solution.py:474
  24.4 8.9 %collective-permute-done.5.refs_3_ = bf16[16,32,128]{2,1,0:T(8,128)(2,1)S(1)} collective-permute-done((bf16[16,32,128]{2,1,0:T(8,128)(2,1)S(1)}, bf16[16,32,128]{2,1,0:T(8,128)(2,1)S(1)}, u32[]{:S(2)}, u32[]{:S(2)}) %collective-permute-start.5) | collective-permute-done | bytes 131104 | tf_op jit(solution)/shard_map/ppermute | solution.py:474
  33.3 0.0 collective-permute-done.6.refs_4_
  33.3 0.0 collective-permute-done.7.refs_5_
  33.3 0.0 collective-permute-done.8.refs_6_
  33.3 0.0 copy-done
  33.3 1.4 %peaks.1 = (f32[1,16]{1,0:T(1,128)}, f32[1,16]{1,0:T(1,128)}) custom-call(bf16[16,32,128]{2,1,0:T(8,128)(2,1)S(1)} %collective-permute-done.2.refs_0_, bf16[16,32,128]{2,1,0:T(8,128)(2,1)S(1)} %collective-permute-done.3.refs_1_, bf16[16,32,128]{2,1,0:T(8,128)(2,1)S(1)} %collective-permute-done.4.refs_2_, ...), custom_call_target="tpu_custom_call" | custom-call | tf_op jit(solution)/shard_map/peaks/pallas_call | solution.py:428
Async XLA Ops:
  3.3 2.7 %collective-permute-start.1 = (bf16[16,128,128]{2,1,0:T(8,128)(2,1)S(1)}, bf16[16,128,128]{2,1,0:T(8,128)(2,1)S(1)}, u32[]{:S(2)}, u32[]{:S(2)}) collective-permute-start(bf16[16,128,128]{2,1,0:T(8,128)(2,1)S(1)} %get-tuple-element.39), channel_id=1, source_target_pairs={{0,1},{1,0},{2,3},{3,2},{4,5},{5,4},{6,7},{7,6},{8,9},{9,8},{10,11... | collective-permute-start | bytes 1572872 | tf_op jit(solution)/shard_map/ppermute | solution.py:269
  4.6 2.0 %collective-permute-start = (bf16[16,128,128]{2,1,0:T(8,128)(2,1)S(1)}, bf16[16,128,128]{2,1,0:T(8,128)(2,1)S(1)}, u32[]{:S(2)}, u32[]{:S(2)}) collective-permute-start(bf16[16,128,128]{2,1,0:T(8,128)(2,1)S(1)} %get-tuple-element.38), channel_id=1, source_target_pairs={{0,1},{1,0},{2,3},{3,2},{4,5},{5,4},{6,7},{7,6},{8,9},{9,8},{10,11... | collective-permute-start | bytes 1572872 | tf_op jit(solution)/shard_map/ppermute | solution.py:273
  6.0 27.2 %copy-start = (f32[1,16]{1,0:T(1,128)S(1)}, f32[1,16]{1,0:T(1,128)}, u32[]{:S(2)}) copy-start(f32[1,16]{1,0:T(1,128)} %refs_9_.1) | copy-start | bytes 196
  6.9 8.7 %collective-permute-start.2 = (bf16[16,32,128]{2,1,0:T(8,128)(2,1)S(1)}, bf16[16,32,128]{2,1,0:T(8,128)(2,1)S(1)}, u32[]{:S(2)}, u32[]{:S(2)}) collective-permute-start(bf16[16,32,128]{2,1,0:T(8,128)(2,1)S(1)} %get-tuple-element.40), channel_id=1, source_target_pairs={{0,2},{2,0},{4,8},{6,10},{8,4},{10,6},{12,14},{14,12},{1,3},{3,1},... | collective-permute-start | bytes 393224 | tf_op jit(solution)/shard_map/ppermute | solution.py:474
  9.7 9.4 %collective-permute-start.3 = (bf16[16,32,128]{2,1,0:T(8,128)(2,1)S(1)}, bf16[16,32,128]{2,1,0:T(8,128)(2,1)S(1)}, u32[]{:S(2)}, u32[]{:S(2)}) collective-permute-start(bf16[16,32,128]{2,1,0:T(8,128)(2,1)S(1)} %get-tuple-element.41), channel_id=1, source_target_pairs={{0,4},{2,6},{4,0},{6,2},{8,12},{10,14},{12,8},{14,10},{1,5},{3,7},... | collective-permute-start | bytes 393224 | tf_op jit(solution)/shard_map/ppermute | solution.py:474
  11.4 13.0 %collective-permute-start.4 = (bf16[16,32,128]{2,1,0:T(8,128)(2,1)S(1)}, bf16[16,32,128]{2,1,0:T(8,128)(2,1)S(1)}, u32[]{:S(2)}, u32[]{:S(2)}) collective-permute-start(bf16[16,32,128]{2,1,0:T(8,128)(2,1)S(1)} %get-tuple-element.42), channel_id=1, source_target_pairs={{0,8},{2,10},{4,12},{6,14},{8,0},{10,2},{12,4},{14,6},{1,9},{3,11}... | collective-permute-start | bytes 393224 | tf_op jit(solution)/shard_map/ppermute | solution.py:474
  13.9 19.4 %collective-permute-start.5 = (bf16[16,32,128]{2,1,0:T(8,128)(2,1)S(1)}, bf16[16,32,128]{2,1,0:T(8,128)(2,1)S(1)}, u32[]{:S(2)}, u32[]{:S(2)}) collective-permute-start(bf16[16,32,128]{2,1,0:T(8,128)(2,1)S(1)} %get-tuple-element.43), channel_id=1, source_target_pairs={{0,10},{2,8},{4,14},{6,12},{8,2},{10,0},{12,6},{14,4},{1,11},{3,9}... | collective-permute-start | bytes 393224 | tf_op jit(solution)/shard_map/ppermute | solution.py:474
  15.2 18.0 %collective-permute-start.6 = (bf16[16,32,128]{2,1,0:T(8,128)(2,1)S(1)}, bf16[16,32,128]{2,1,0:T(8,128)(2,1)S(1)}, u32[]{:S(2)}, u32[]{:S(2)}) collective-permute-start(bf16[16,32,128]{2,1,0:T(8,128)(2,1)S(1)} %get-tuple-element.44), channel_id=1, source_target_pairs={{0,6},{2,4},{4,2},{6,0},{8,14},{10,12},{12,10},{14,8},{1,7},{3,5},... | collective-permute-start | bytes 393224 | tf_op jit(solution)/shard_map/ppermute | solution.py:474
  15.6 17.7 %collective-permute-start.7 = (bf16[16,32,128]{2,1,0:T(8,128)(2,1)S(1)}, bf16[16,32,128]{2,1,0:T(8,128)(2,1)S(1)}, u32[]{:S(2)}, u32[]{:S(2)}) collective-permute-start(bf16[16,32,128]{2,1,0:T(8,128)(2,1)S(1)} %get-tuple-element.45), channel_id=1, source_target_pairs={{0,14},{2,12},{4,10},{6,8},{8,6},{10,4},{12,2},{14,0},{1,15},{3,13... | collective-permute-start | bytes 393224 | tf_op jit(solution)/shard_map/ppermute | solution.py:474
  19.2 14.1 %collective-permute-start.8 = (bf16[16,32,128]{2,1,0:T(8,128)(2,1)S(1)}, bf16[16,32,128]{2,1,0:T(8,128)(2,1)S(1)}, u32[]{:S(2)}, u32[]{:S(2)}) collective-permute-start(bf16[16,32,128]{2,1,0:T(8,128)(2,1)S(1)} %get-tuple-element.46), channel_id=1, source_target_pairs={{0,12},{2,14},{4,6},{6,4},{8,10},{10,8},{12,0},{14,2},{1,13},{3,15... | collective-permute-start | bytes 393224 | tf_op jit(solution)/shard_map/ppermute | solution.py:474
where the time goes:
time: 34.8 us; the launch traced here: 34.7 us
  starting transfers between devices  14.4 us (41%)
  waiting for transfers between devices  12.5 us (36%)
  Pallas kernels  7.06 us (20%)
  between operations  0.7 us (2%)
    ppermute x7, starting transfers between devices, body(): lax.ppermute(parts[slot], 'freq', pairs)  13.8 us
    ppermute x7, waiting for transfers between devices, body(): lax.ppermute(parts[slot], 'freq', pairs)  12.3 us
    pallas_call x1, Pallas kernels, partials(): call(functools.partial(other_even_kernel, freq_total, slots), 'other_even...  2.66 us
    pallas_call x1, Pallas kernels, peaks(): pl.pallas_call(functools.partial(peak_kernel, freq_total, folded, sources...  1.37 us
    pallas_call x1, Pallas kernels, partials(): call(functools.partial(own_kernel, freq_total, slots), 'own', [vmem] * 5,...  1.32 us
    pallas_call x1, Pallas kernels, partials(): call(other_odd_kernel, 'other_odd', [vmem] * 8, [out, picked], work)  0.76 us
  transfers between devices with their start and end apart: 9, of which 3 were waited for; matrix products, arithmetic and copies ran while one was open for 0% of the time, Pallas kernels for 8%

commit v1 on v0

--- a/solution.py
+++ b/solution.py
@@ -50,16 +50,15 @@
 def slot_masks(slots):
     half = slots // 2
     between = (2, half, half + 1, 3, slots - 1)
-    return (0, 1, *between, slots - 2), (0, slots - 2, *between, 1)
+    return (1, *between, slots - 2, 0), (slots - 2, *between, 1, 0)
 
 
 def partner(slots, slot):
     index = lax.axis_index("freq")
     inner = ((index * 2) ^ index) & (slots // 2) != 0
-    outer_masks, inner_masks = slot_masks(slots)
     mask = jnp.zeros_like(slot)
-    for s in range(1, slots):
-        mask = jnp.where(slot == s, jnp.where(inner, inner_masks[s], outer_masks[s]), mask)
+    for s, (outer_mask, inner_mask) in enumerate(zip(*slot_masks(slots))):
+        mask = jnp.where(slot == s, jnp.where(inner, inner_mask, outer_mask), mask)
     return mask ^ index
 
 
@@ -150,27 +149,31 @@
             picks, field_ref[w, parity].reshape(2 * elements, sites), ((1,), (1,))
         ).astype(jnp.bfloat16)
         for i, ref in enumerate(picked_refs):
-            ref[w] = picked[i * FG : (i + 1) * FG]
-
-
-def store_spectra(parity, picked_ref, law_ref, k_real, k_imag, out_ref, first):
-    for w in range(W_HALF):
-        product = dot(picked_ref[w], law_ref[w], ((1,), (0,)))
-        real_part = product[:, :ROWS]
-        imag_part = product[:, ROWS:]
-        kr = k_real[:, 2 * w + parity : 2 * w + parity + 1]
-        ki = k_imag[:, 2 * w + parity : 2 * w + parity + 1]
-        out_ref[first + 2 * w] = (kr * real_part - ki * imag_part).astype(jnp.bfloat16)
-        out_ref[first + 2 * w + 1] = (kr * imag_part + ki * real_part).astype(jnp.bfloat16)
-
-
-def other_even_kernel(freq_total, slots, *refs):
+            ref[parity, w] = picked[i * FG : (i + 1) * FG]
+
+
+def store_spectra(picked_ref, law_ref, k_real, k_imag, out_refs):
+    size = out_refs[0].shape[1]
+    for parity in range(2):
+        for w in range(W_HALF):
+            product = dot(picked_ref[parity, w], law_ref[parity, w], ((1,), (0,)))
+            real_part = product[:, :ROWS]
+            imag_part = product[:, ROWS:]
+            kr = k_real[:, 2 * w + parity : 2 * w + parity + 1]
+            ki = k_imag[:, 2 * w + parity : 2 * w + parity + 1]
+            parts = (kr * real_part - ki * imag_part, kr * imag_part + ki * real_part)
+            for k, part in enumerate(parts):
+                part = part.astype(jnp.bfloat16)
+                for i, out_ref in enumerate(out_refs):
+                    out_ref[parity * W_DEV + 2 * w + k] = part[i * size : (i + 1) * size]
+
+
+def other_kernel(freq_total, slots, *refs):
     field_hbm, *small_hbm = refs[:7]
-    out_ref, own_picked_ref, field_ref, size_ref, slope_ref, *kept = refs[7:20]
-    delay_ref, channel_ref, blocks_ref, cells_ref = refs[20:24]
-    field_sem, small_sem, *scratch = refs[24:]
+    first_ref, second_ref, own_picked_ref, size_ref, slope_ref, delays_ref = refs[7:13]
+    delay_ref, channel_ref, blocks_ref, cells_ref = refs[13:17]
+    field_ref, field_sem, small_sem, picked_ref, law_ref = refs[17:]
     small = (delay_ref, channel_ref, blocks_ref, cells_ref, size_ref, slope_ref)
-    picked_ref, law_ref = scratch
     copies = [
         pltpu.make_async_copy(source, target, small_sem.at[i])
         for i, (source, target) in enumerate(zip(small_hbm, small))
@@ -195,37 +198,23 @@
     )
     factors = kirchhoff(freq_total, order, groups[0], size_ref, slope_ref)
     delays = delays_of(channel_ref, delay_ref, blocks_ref, groups, field_ref.shape[3])
+    delays_ref[...] = delays[:, ROWS:]
     even, step, odd = focal_base(freq_total, delays[:, :ROWS])
-    values = (picks, *step, *odd, *factors, delays[:, ROWS:])
-    for ref, value in zip(kept, values):
-        ref[...] = value
-    store_law(law_ref, even, step)
-
-    field_copies[0].wait()
-    pick_fields(0, picks, field_ref, (picked_ref, own_picked_ref))
-    store_spectra(0, picked_ref, law_ref, *factors, out_ref, 0)
-    field_copies[1].wait()
-
-
-def other_odd_kernel(field_ref, picks_ref, *refs):
-    step, odd, k_refs = refs[:2], refs[2:4], refs[4:6]
-    out_ref, own_picked_ref, picked_ref, law_ref = refs[6:]
-    store_law(law_ref, [ref[...] for ref in odd], [ref[...] for ref in step])
-    pick_fields(1, picks_ref[...], field_ref, (picked_ref, own_picked_ref))
-    store_spectra(1, picked_ref, law_ref, *k_refs, out_ref, 0)
+    for parity, law in enumerate((even, odd)):
+        store_law(law_ref.at[parity], law, step)
+        field_copies[parity].wait()
+        pick_fields(parity, picks, field_ref, (picked_ref, own_picked_ref))
+    store_spectra(picked_ref, law_ref, *factors, (first_ref, second_ref))
 
 
 def own_kernel(freq_total, slots, *refs):
-    picked_refs, (delays_ref, size_ref, slope_ref, out_ref, law_ref) = refs[:2], refs[2:]
+    picked_ref, delays_ref, size_ref, slope_ref, out_ref, law_ref = refs
     even, step, odd = focal_base(freq_total, delays_ref[...])
     for parity, law in enumerate((even, odd)):
         store_law(law_ref.at[parity], law, step)
     group = lax.axis_index("elem")
     factors = kirchhoff(freq_total, slot_order(slots), group, size_ref, slope_ref)
-    for parity in range(2):
-        store_spectra(
-            parity, picked_refs[parity], law_ref.at[parity], *factors, out_ref, parity * W_DEV
-        )
+    store_spectra(picked_ref, law_ref, *factors, (out_ref,))
 
 
 def call(kernel, name, in_specs, out_shape, scratch):
@@ -247,69 +236,55 @@
     vmem = pl.BlockSpec(memory_space=pltpu.VMEM)
     hbm = pl.BlockSpec(memory_space=pltpu.HBM)
     pinned = [pltpu.with_memory_space_constraint(a, pltpu.HBM) for a in (field, *small)]
-    out = jax.ShapeDtypeStruct((W_DEV, FG, ROWS), jnp.bfloat16)
-    picked = jax.ShapeDtypeStruct((W_HALF, FG, 2 * elements), jnp.bfloat16)
-    law = (W_HALF, 2 * elements, 2 * ROWS)
-    base = [jax.ShapeDtypeStruct((elements, ROWS), jnp.float32)] * 2
-    factors = [jax.ShapeDtypeStruct((FG, FG), jnp.float32)] * 2
-    kept = [jax.ShapeDtypeStruct((2 * FG, sites), jnp.bfloat16), *base, *base, *factors]
-    copied = [jax.ShapeDtypeStruct(a.shape, a.dtype) for a in (field, *small[4:])]
-    work = [pltpu.VMEM(picked.shape, picked.dtype), pltpu.VMEM(law, jnp.bfloat16)]
-    even, even_picked, field, size, slope, *kept, delays = call(
-        functools.partial(other_even_kernel, freq_total, slots),
-        "other_even",
+    out = jax.ShapeDtypeStruct((2 * W_DEV, FG, ROWS), jnp.bfloat16)
+    half = jax.ShapeDtypeStruct((2 * W_DEV, FG // 2, ROWS), jnp.bfloat16)
+    picked = jax.ShapeDtypeStruct((2, W_HALF, FG, 2 * elements), jnp.bfloat16)
+    law = pltpu.VMEM((2, W_HALF, 2 * elements, 2 * ROWS), jnp.bfloat16)
+    copied = [jax.ShapeDtypeStruct(a.shape, a.dtype) for a in small[4:]]
+    delays = jax.ShapeDtypeStruct((elements, ROWS), jnp.float32)
+    first, second, own_picked, size, slope, delays = call(
+        functools.partial(other_kernel, freq_total, slots),
+        "other",
         [hbm] * len(pinned),
-        [out, picked, *copied, *kept, base[0]],
+        [half, half, picked, *copied, delays],
         [
             pltpu.SMEM(a.shape, a.dtype) if a.ndim == 1 else pltpu.VMEM(a.shape, a.dtype)
             for a in small[:4]
         ]
-        + [pltpu.SemaphoreType.DMA((2,)), pltpu.SemaphoreType.DMA((len(small),)), *work],
+        + [
+            pltpu.VMEM(field.shape, field.dtype),
+            pltpu.SemaphoreType.DMA((2,)),
+            pltpu.SemaphoreType.DMA((len(small),)),
+            pltpu.VMEM(picked.shape, picked.dtype),
+            law,
+        ],
     )(*pinned)
-    even = lax.ppermute(even, "elem", swap)
-    odd, odd_picked = call(
-        other_odd_kernel, "other_odd", [vmem] * 8, [out, picked], work
-    )(field, *kept)
-    odd = lax.ppermute(odd, "elem", swap)
+    first = lax.ppermute(first, "elem", swap)
+    second = lax.ppermute(second, "elem", swap)
     (own,) = call(
-        functools.partial(own_kernel, freq_total, slots),
-        "own",
-        [vmem] * 5,
-        [jax.ShapeDtypeStruct((2 * W_DEV, FG, ROWS), jnp.bfloat16)],
-        [pltpu.VMEM((2, *law), jnp.bfloat16)],
-    )(even_picked, odd_picked, delays, size, slope)
-    return own, even, odd
-
-
-def total(own_ref, moved_ref, parity, rows):
-    own = own_ref[parity * W_DEV : (parity + 1) * W_DEV, rows]
-    both = own.astype(jnp.float32) + moved_ref[:, rows].astype(jnp.float32)
-    return jnp.swapaxes(both, 0, 1).astype(jnp.bfloat16)
-
-
-def add_even_kernel(size, own_ref, even_ref, held_ref):
-    for first in range(0, held_ref.shape[0], size):
-        rows = pl.ds(first, size)
-        held_ref[rows] = total(own_ref, even_ref, 0, rows)
-
-
-def add_odd_kernel(own_ref, odd_ref, held_ref, *refs):
+        functools.partial(own_kernel, freq_total, slots), "own", [vmem] * 4, [out], [law]
+    )(own_picked, delays, size, slope)
+    return own, first, second
+
+
+def add_kernel(first, own_ref, moved_ref, *refs):
     size = refs[0].shape[0]
     for slot, ref in enumerate(refs):
-        rows = pl.ds(slot * size, size)
-        ref[:, :W_DEV] = held_ref[rows]
-        ref[:, W_DEV:] = total(own_ref, odd_ref, 1, rows)
-
-
-def add(own, even, odd, slots):
+        own = own_ref[:, pl.ds(first + slot * size, size)].astype(jnp.float32)
+        both = own + moved_ref[:, pl.ds(slot * size, size)].astype(jnp.float32)
+        ref[...] = jnp.swapaxes(both, 0, 1).astype(jnp.bfloat16)
+
+
+def add(own, first, second, slots):
     vmem = pl.BlockSpec(memory_space=pltpu.VMEM)
     planes, flaws, rows = own.shape
-    size = flaws // slots
-    shape = jax.ShapeDtypeStruct((flaws, planes // 2, rows), own.dtype)
-    kernel = functools.partial(add_even_kernel, min(size, 16))
-    (held,) = call(kernel, "add_even", [vmem] * 2, [shape], [])(own, even)
-    shapes = [jax.ShapeDtypeStruct((size, planes, rows), own.dtype)] * slots
-    return call(add_odd_kernel, "add_odd", [vmem] * 3, shapes, [])(own, odd, held)
+    count = max(1, slots // 2)
+    shape = jax.ShapeDtypeStruct((flaws // 2 // count, planes, rows), own.dtype)
+    parts = []
+    for name, start, moved in (("add_first", 0, first), ("add_second", flaws // 2, second)):
+        kernel = functools.partial(add_kernel, start)
+        parts += call(kernel, name, [vmem] * 2, [shape] * count, [])(own, moved)
+    return parts
 
 
 def table_kernel(freq_total, slots, table_ref):
@@ -471,12 +446,15 @@
         spectra = []
         for slot, masks in enumerate(zip(*slot_masks(slots))):
             pairs = [(a, a ^ masks[((2 * a) ^ a) & half != 0]) for a in range(slots)]
-            spectra.append(lax.ppermute(parts[slot], "freq", pairs) if slot else parts[slot])
-        spectra = [*spectra[1:], spectra[0]]
-        sources = [((slot - 1) % slots, 0) for slot in range(slots)]
+            own = slot == slots - 1
+            spectra.append(parts[slot] if own else lax.ppermute(parts[slot], "freq", pairs))
+        order = (*range(half, slots - 1), *range(half), slots - 1)
+        spectra = [spectra[slot] for slot in order]
+        sources = [(order.index(slot), 0) for slot in range(slots)]
     else:
+        whole = jnp.concatenate(parts, axis=0)
         spectra = [
-            lax.all_to_all(parts[0], "freq", split_axis=0, concat_axis=0, tiled=True)
+            lax.all_to_all(whole, "freq", split_axis=0, concat_axis=0, tiled=True)
         ]
         sources = [(0, s * (FG // freq_count)) for s in range(freq_count)]
     return tuple(peaks(spectra, sources, twiddles, noise_level, freq_total, folded))

time: 34.8 us -> 34.4 us (0.989)
  starting transfers between devices: 14.4 us -> 13.8 us
    ppermute x7, starting transfers between devices: 13.8 us -> 13.2 us  [body(): lax.ppermute(parts[slot], 'freq', pairs)]
    pallas_call x5 -> x4, Pallas kernels: 5.38 us -> 5.36 us  [the longest x1 3.41 us: partials(): call(functools.partial(other_kernel, freq_total, slots), 'other', [hbm] *...]
  transfers between devices with their start and end apart: 9 -> 9, of which waited for: 3 -> 3; matrix products, arithmetic and copies ran while one was open for 0% -> 0% of each run, Pallas kernels for 8% -> 7%
where the time goes in v1:
time: 34.4 us; the launch traced here: 34.2 us
  starting transfers between devices  13.8 us (40%)
  waiting for transfers between devices  12.6 us (37%)
  Pallas kernels  7.05 us (20%)
  between operations  0.69 us (2%)
    ppermute x7, starting transfers between devices, body(): lax.ppermute(parts[slot], 'freq', pairs)  13.2 us
    ppermute x7, waiting for transfers between devices, body(): lax.ppermute(parts[slot], 'freq', pairs)  12.5 us
    pallas_call x1, Pallas kernels, partials(): call(functools.partial(other_kernel, freq_total, slots), 'other', [hbm] *...  3.41 us
    pallas_call x1, Pallas kernels, peaks(): pl.pallas_call(functools.partial(peak_kernel, freq_total, folded, sources...  1.38 us
    pallas_call x1, Pallas kernels, partials(): call(functools.partial(own_kernel, freq_total, slots), 'own', [vmem] * 4,...  1.29 us
  transfers between devices with their start and end apart: 9, of which 3 were waited for; matrix products, arithmetic and copies ran while one was open for 0% of the time, Pallas kernels for 7%

profile of v1, /device:TPU:0, one launch (start us, length us, event | category | flops | bytes accessed | tf_op | source)
XLA Modules:
  0.0 34.2 jit_solution(3381487644277911880)
XLA Ops:
  0.6 3.4 %other.1 = (bf16[32,64,128]{2,1,0:T(8,128)(2,1)S(1)}, bf16[32,64,128]{2,1,0:T(8,128)(2,1)S(1)}, bf16[2,8,128,256]{3,2,1,0:T(8,128)(2,1)S(1)}, f32[2,128]{1,0:T(2...) custom-call(bf16[8,2,2,128,256]{4,3,2,1,0:T(8,128)(2,1)} %bitcast.3, f32[256,256]{1,0:T(8,128)} %refs_1_.1, ...), custom_call_target="tpu_custom_call" | custom-call | flops 1000 | bytes 1000 | tf_op jit(solution)/shard_map/other/pallas_call | solution.py:245
  4.0 0.5 %collective-permute-start.4 = (bf16[32,64,128]{2,1,0:T(8,128)(2,1)S(1)}, bf16[32,64,128]{2,1,0:T(8,128)(2,1)S(1)}, u32[]{:S(2)}, u32[]{:S(2)}) collective-permute-start(bf16[32,64,128]{2,1,0:T(8,128)(2,1)S(1)} %get-tuple-element.24), channel_id=1, source_target_pairs={{0,1},{1,0},{2,3},{3,2},{4,5},{5,4},{6,7},{7,6},{8,9},{9,8},{10,11... | collective-permute-start | bytes 1572872 | tf_op jit(solution)/shard_map/ppermute | solution.py:262
  4.6 0.1 collective-permute-start
  4.6 1.3 %own.1.own_ref = bf16[32,128,128]{2,1,0:T(8,128)(2,1)S(1)} custom-call(bf16[2,8,128,256]{3,2,1,0:T(8,128)(2,1)S(1)} %get-tuple-element.16.refs_0_, f32[128,128]{1,0:T(8,128)S(1)} %get-tuple-element.17.refs_1_, f32[2,128]{1,0:T(2,128)S(1)} %get-tuple-element.18.refs_2_, f32[2,128]{1,0:T(2,128)S(1)} %get-tuple-element.19.refs_3_), custom_call_target="tpu_custom_call" | custom-call | flops 1000 | bytes 1000 | tf_op jit(solution)/shard_map/own/pallas_call | solution.py:264
  5.9 0.0 copy-start
  6.0 0.2 collective-permute-done.4.moved_ref
  6.1 0.3 add_first.1
  6.4 2.9 %collective-permute-start.5 = (bf16[16,32,128]{2,1,0:T(8,128)(2,1)S(1)}, bf16[16,32,128]{2,1,0:T(8,128)(2,1)S(1)}, u32[]{:S(2)}, u32[]{:S(2)}) collective-permute-start(bf16[16,32,128]{2,1,0:T(8,128)(2,1)S(1)} %get-tuple-element.25), channel_id=1, source_target_pairs={{0,2},{2,0},{4,8},{6,10},{8,4},{10,6},{12,14},{14,12},{1,3},{3,1},... | collective-permute-start | bytes 393224 | tf_op jit(solution)/shard_map/ppermute | solution.py:450
  9.4 1.7 %collective-permute-start.6 = (bf16[16,32,128]{2,1,0:T(8,128)(2,1)S(1)}, bf16[16,32,128]{2,1,0:T(8,128)(2,1)S(1)}, u32[]{:S(2)}, u32[]{:S(2)}) collective-permute-start(bf16[16,32,128]{2,1,0:T(8,128)(2,1)S(1)} %get-tuple-element.26), channel_id=1, source_target_pairs={{0,4},{2,6},{4,0},{6,2},{8,12},{10,14},{12,8},{14,10},{1,5},{3,7},... | collective-permute-start | bytes 393224 | tf_op jit(solution)/shard_map/ppermute | solution.py:450
  11.0 2.5 %collective-permute-start.7 = (bf16[16,32,128]{2,1,0:T(8,128)(2,1)S(1)}, bf16[16,32,128]{2,1,0:T(8,128)(2,1)S(1)}, u32[]{:S(2)}, u32[]{:S(2)}) collective-permute-start(bf16[16,32,128]{2,1,0:T(8,128)(2,1)S(1)} %get-tuple-element.27), channel_id=1, source_target_pairs={{0,8},{2,10},{4,12},{6,14},{8,0},{10,2},{12,4},{14,6},{1,9},{3,11}... | collective-permute-start | bytes 393224 | tf_op jit(solution)/shard_map/ppermute | solution.py:450
  13.5 1.3 %collective-permute-start.8 = (bf16[16,32,128]{2,1,0:T(8,128)(2,1)S(1)}, bf16[16,32,128]{2,1,0:T(8,128)(2,1)S(1)}, u32[]{:S(2)}, u32[]{:S(2)}) collective-permute-start(bf16[16,32,128]{2,1,0:T(8,128)(2,1)S(1)} %get-tuple-element.28), channel_id=1, source_target_pairs={{0,10},{2,8},{4,14},{6,12},{8,2},{10,0},{12,6},{14,4},{1,11},{3,9}... | collective-permute-start | bytes 393224 | tf_op jit(solution)/shard_map/ppermute | solution.py:450
  14.9 0.0 collective-permute-done.moved_ref
  14.9 0.3 add_second.1
  15.2 0.4 %collective-permute-start.1 = (bf16[16,32,128]{2,1,0:T(8,128)(2,1)S(1)}, bf16[16,32,128]{2,1,0:T(8,128)(2,1)S(1)}, u32[]{:S(2)}, u32[]{:S(2)}) collective-permute-start(bf16[16,32,128]{2,1,0:T(8,128)(2,1)S(1)} %get-tuple-element.21), channel_id=1, source_target_pairs={{0,6},{2,4},{4,2},{6,0},{8,14},{10,12},{12,10},{14,8},{1,7},{3,5},... | collective-permute-start | bytes 393224 | tf_op jit(solution)/shard_map/ppermute | solution.py:450
  15.6 0.0 collective-permute-done.5.refs_3_
  15.6 3.6 %collective-permute-start.2 = (bf16[16,32,128]{2,1,0:T(8,128)(2,1)S(1)}, bf16[16,32,128]{2,1,0:T(8,128)(2,1)S(1)}, u32[]{:S(2)}, u32[]{:S(2)}) collective-permute-start(bf16[16,32,128]{2,1,0:T(8,128)(2,1)S(1)} %get-tuple-element.22), channel_id=1, source_target_pairs={{0,14},{2,12},{4,10},{6,8},{8,6},{10,4},{12,2},{14,0},{1,15},{3,13... | collective-permute-start | bytes 393224 | tf_op jit(solution)/shard_map/ppermute | solution.py:450
  19.2 0.0 collective-permute-done.6.refs_4_
  19.2 0.8 %collective-permute-start.3 = (bf16[16,32,128]{2,1,0:T(8,128)(2,1)S(1)}, bf16[16,32,128]{2,1,0:T(8,128)(2,1)S(1)}, u32[]{:S(2)}, u32[]{:S(2)}) collective-permute-start(bf16[16,32,128]{2,1,0:T(8,128)(2,1)S(1)} %get-tuple-element.23), channel_id=1, source_target_pairs={{0,12},{2,14},{4,6},{6,4},{8,10},{10,8},{12,0},{14,2},{1,13},{3,15... | collective-permute-start | bytes 393224 | tf_op jit(solution)/shard_map/ppermute | solution.py:450
  20.0 0.3 table.1.refs_8_
  20.3 3.7 %collective-permute-done.7.refs_5_ = bf16[16,32,128]{2,1,0:T(8,128)(2,1)S(1)} collective-permute-done((bf16[16,32,128]{2,1,0:T(8,128)(2,1)S(1)}, bf16[16,32,128]{2,1,0:T(8,128)(2,1)S(1)}, u32[]{:S(2)}, u32[]{:S(2)}) %collective-permute-start.7) | collective-permute-done | bytes 131104 | tf_op jit(solution)/shard_map/ppermute | solution.py:450
  24.0 8.8 %collective-permute-done.8.refs_6_ = bf16[16,32,128]{2,1,0:T(8,128)(2,1)S(1)} collective-permute-done((bf16[16,32,128]{2,1,0:T(8,128)(2,1)S(1)}, bf16[16,32,128]{2,1,0:T(8,128)(2,1)S(1)}, u32[]{:S(2)}, u32[]{:S(2)}) %collective-permute-start.8) | collective-permute-done | bytes 131104 | tf_op jit(solution)/shard_map/ppermute | solution.py:450
  32.8 0.0 collective-permute-done.1.refs_0_
  32.8 0.0 collective-permute-done.2.refs_1_
  32.8 0.0 collective-permute-done.3.refs_2_
  32.8 0.0 copy-done
  32.8 1.4 %peaks.1 = (f32[1,16]{1,0:T(1,128)}, f32[1,16]{1,0:T(1,128)}) custom-call(bf16[16,32,128]{2,1,0:T(8,128)(2,1)S(1)} %collective-permute-done.1.refs_0_, bf16[16,32,128]{2,1,0:T(8,128)(2,1)S(1)} %collective-permute-done.2.refs_1_, bf16[16,32,128]{2,1,0:T(8,128)(2,1)S(1)} %collective-permute-done.3.refs_2_, ...), custom_call_target="tpu_custom_call" | custom-call | tf_op jit(solution)/shard_map/peaks/pallas_call | solution.py:403
Async XLA Ops:
  4.0 2.1 %collective-permute-start.4 = (bf16[32,64,128]{2,1,0:T(8,128)(2,1)S(1)}, bf16[32,64,128]{2,1,0:T(8,128)(2,1)S(1)}, u32[]{:S(2)}, u32[]{:S(2)}) collective-permute-start(bf16[32,64,128]{2,1,0:T(8,128)(2,1)S(1)} %get-tuple-element.24), channel_id=1, source_target_pairs={{0,1},{1,0},{2,3},{3,2},{4,5},{5,4},{6,7},{7,6},{8,9},{9,8},{10,11... | collective-permute-start | bytes 1572872 | tf_op jit(solution)/shard_map/ppermute | solution.py:262
  4.6 10.3 %collective-permute-start = (bf16[32,64,128]{2,1,0:T(8,128)(2,1)S(1)}, bf16[32,64,128]{2,1,0:T(8,128)(2,1)S(1)}, u32[]{:S(2)}, u32[]{:S(2)}) collective-permute-start(bf16[32,64,128]{2,1,0:T(8,128)(2,1)S(1)} %get-tuple-element.20), channel_id=1, source_target_pairs={{0,1},{1,0},{2,3},{3,2},{4,5},{5,4},{6,7},{7,6},{8,9},{9,8},{10,11... | collective-permute-start | bytes 1572872 | tf_op jit(solution)/shard_map/ppermute | solution.py:263
  5.9 26.9 %copy-start = (f32[1,16]{1,0:T(1,128)S(1)}, f32[1,16]{1,0:T(1,128)}, u32[]{:S(2)}) copy-start(f32[1,16]{1,0:T(1,128)} %refs_9_.1) | copy-start | bytes 196
  6.4 9.2 %collective-permute-start.5 = (bf16[16,32,128]{2,1,0:T(8,128)(2,1)S(1)}, bf16[16,32,128]{2,1,0:T(8,128)(2,1)S(1)}, u32[]{:S(2)}, u32[]{:S(2)}) collective-permute-start(bf16[16,32,128]{2,1,0:T(8,128)(2,1)S(1)} %get-tuple-element.25), channel_id=1, source_target_pairs={{0,2},{2,0},{4,8},{6,10},{8,4},{10,6},{12,14},{14,12},{1,3},{3,1},... | collective-permute-start | bytes 393224 | tf_op jit(solution)/shard_map/ppermute | solution.py:450
  9.4 9.8 %collective-permute-start.6 = (bf16[16,32,128]{2,1,0:T(8,128)(2,1)S(1)}, bf16[16,32,128]{2,1,0:T(8,128)(2,1)S(1)}, u32[]{:S(2)}, u32[]{:S(2)}) collective-permute-start(bf16[16,32,128]{2,1,0:T(8,128)(2,1)S(1)} %get-tuple-element.26), channel_id=1, source_target_pairs={{0,4},{2,6},{4,0},{6,2},{8,12},{10,14},{12,8},{14,10},{1,5},{3,7},... | collective-permute-start | bytes 393224 | tf_op jit(solution)/shard_map/ppermute | solution.py:450
  11.0 13.0 %collective-permute-start.7 = (bf16[16,32,128]{2,1,0:T(8,128)(2,1)S(1)}, bf16[16,32,128]{2,1,0:T(8,128)(2,1)S(1)}, u32[]{:S(2)}, u32[]{:S(2)}) collective-permute-start(bf16[16,32,128]{2,1,0:T(8,128)(2,1)S(1)} %get-tuple-element.27), channel_id=1, source_target_pairs={{0,8},{2,10},{4,12},{6,14},{8,0},{10,2},{12,4},{14,6},{1,9},{3,11}... | collective-permute-start | bytes 393224 | tf_op jit(solution)/shard_map/ppermute | solution.py:450
  13.5 19.3 %collective-permute-start.8 = (bf16[16,32,128]{2,1,0:T(8,128)(2,1)S(1)}, bf16[16,32,128]{2,1,0:T(8,128)(2,1)S(1)}, u32[]{:S(2)}, u32[]{:S(2)}) collective-permute-start(bf16[16,32,128]{2,1,0:T(8,128)(2,1)S(1)} %get-tuple-element.28), channel_id=1, source_target_pairs={{0,10},{2,8},{4,14},{6,12},{8,2},{10,0},{12,6},{14,4},{1,11},{3,9}... | collective-permute-start | bytes 393224 | tf_op jit(solution)/shard_map/ppermute | solution.py:450
  15.2 17.6 %collective-permute-start.1 = (bf16[16,32,128]{2,1,0:T(8,128)(2,1)S(1)}, bf16[16,32,128]{2,1,0:T(8,128)(2,1)S(1)}, u32[]{:S(2)}, u32[]{:S(2)}) collective-permute-start(bf16[16,32,128]{2,1,0:T(8,128)(2,1)S(1)} %get-tuple-element.21), channel_id=1, source_target_pairs={{0,6},{2,4},{4,2},{6,0},{8,14},{10,12},{12,10},{14,8},{1,7},{3,5},... | collective-permute-start | bytes 393224 | tf_op jit(solution)/shard_map/ppermute | solution.py:450
  15.6 17.2 %collective-permute-start.2 = (bf16[16,32,128]{2,1,0:T(8,128)(2,1)S(1)}, bf16[16,32,128]{2,1,0:T(8,128)(2,1)S(1)}, u32[]{:S(2)}, u32[]{:S(2)}) collective-permute-start(bf16[16,32,128]{2,1,0:T(8,128)(2,1)S(1)} %get-tuple-element.22), channel_id=1, source_target_pairs={{0,14},{2,12},{4,10},{6,8},{8,6},{10,4},{12,2},{14,0},{1,15},{3,13... | collective-permute-start | bytes 393224 | tf_op jit(solution)/shard_map/ppermute | solution.py:450
  19.2 13.6 %collective-permute-start.3 = (bf16[16,32,128]{2,1,0:T(8,128)(2,1)S(1)}, bf16[16,32,128]{2,1,0:T(8,128)(2,1)S(1)}, u32[]{:S(2)}, u32[]{:S(2)}) collective-permute-start(bf16[16,32,128]{2,1,0:T(8,128)(2,1)S(1)} %get-tuple-element.23), channel_id=1, source_target_pairs={{0,12},{2,14},{4,6},{6,4},{8,10},{10,8},{12,0},{14,2},{1,13},{3,15... | collective-permute-start | bytes 393224 | tf_op jit(solution)/shard_map/ppermute | solution.py:450

commit v2 on v1

--- a/solution.py
+++ b/solution.py
@@ -131,6 +131,8 @@
 
 def store_law(law_ref, law, step):
     elements = law_ref.shape[1] // 2
+    double = 2.0 * step[0]
+    following = turned(law, step)
     for w in range(W_HALF):
         c = law[0].astype(jnp.bfloat16)
         s = law[1].astype(jnp.bfloat16)
@@ -138,8 +140,7 @@
         law_ref[w, :elements, ROWS:] = -s
         law_ref[w, elements:, :ROWS] = s
         law_ref[w, elements:, ROWS:] = c
-        if w < W_HALF - 1:
-            law = turned(law, step)
+        law, following = following, [double * x - y for x, y in zip(following, law)]
 
 
 def pick_fields(parity, picks, field_ref, picked_refs):
@@ -186,11 +187,11 @@
         )
         for parity in range(2)
     ]
-    for copy in field_copies:
-        copy.start()
+    field_copies[0].start()
     order = slot_order(slots)
     for copy in copies:
         copy.wait()
+    field_copies[1].start()
     group = lax.axis_index("elem")
     groups = (1 - group, group)
     picks = jnp.concatenate(

time: 34.4 us -> 34.2 us (level)
  no operation moved by 1% of the time
where the time goes in v2:
time: 34.2 us; the launch traced here: 34.1 us
  starting transfers between devices  13.8 us (40%)
  waiting for transfers between devices  12.7 us (37%)
  Pallas kernels  6.89 us (20%)
  between operations  0.69 us (2%)
    ppermute x7, starting transfers between devices, body(): lax.ppermute(parts[slot], 'freq', pairs)  13.2 us
    ppermute x7, waiting for transfers between devices, body(): lax.ppermute(parts[slot], 'freq', pairs)  12.5 us
    pallas_call x1, Pallas kernels, partials(): call(functools.partial(other_kernel, freq_total, slots), 'other', [hbm] *...  3.28 us
    pallas_call x1, Pallas kernels, peaks(): pl.pallas_call(functools.partial(peak_kernel, freq_total, folded, sources...  1.38 us
    pallas_call x1, Pallas kernels, partials(): call(functools.partial(own_kernel, freq_total, slots), 'own', [vmem] * 4,...  1.26 us
  transfers between devices with their start and end apart: 9, of which 3 were waited for; matrix products, arithmetic and copies ran while one was open for 0% of the time, Pallas kernels for 7%

profile of v2, /device:TPU:0, one launch (start us, length us, event | category | flops | bytes accessed | tf_op | source)
XLA Modules:
  0.0 34.1 jit_solution(6888935045465842568)
XLA Ops:
  0.6 3.3 %other.1 = (bf16[32,64,128]{2,1,0:T(8,128)(2,1)S(1)}, bf16[32,64,128]{2,1,0:T(8,128)(2,1)S(1)}, bf16[2,8,128,256]{3,2,1,0:T(8,128)(2,1)S(1)}, f32[2,128]{1,0:T(2...) custom-call(bf16[8,2,2,128,256]{4,3,2,1,0:T(8,128)(2,1)} %bitcast.3, f32[256,256]{1,0:T(8,128)} %refs_1_.1, ...), custom_call_target="tpu_custom_call" | custom-call | flops 1000 | bytes 1000 | tf_op jit(solution)/shard_map/other/pallas_call | solution.py:246
  3.9 0.5 %collective-permute-start.4 = (bf16[32,64,128]{2,1,0:T(8,128)(2,1)S(1)}, bf16[32,64,128]{2,1,0:T(8,128)(2,1)S(1)}, u32[]{:S(2)}, u32[]{:S(2)}) collective-permute-start(bf16[32,64,128]{2,1,0:T(8,128)(2,1)S(1)} %get-tuple-element.24), channel_id=1, source_target_pairs={{0,1},{1,0},{2,3},{3,2},{4,5},{5,4},{6,7},{7,6},{8,9},{9,8},{10,11... | collective-permute-start | bytes 1572872 | tf_op jit(solution)/shard_map/ppermute | solution.py:263
  4.4 0.1 collective-permute-start
  4.5 1.3 %own.1.own_ref = bf16[32,128,128]{2,1,0:T(8,128)(2,1)S(1)} custom-call(bf16[2,8,128,256]{3,2,1,0:T(8,128)(2,1)S(1)} %get-tuple-element.16.refs_0_, f32[128,128]{1,0:T(8,128)S(1)} %get-tuple-element.17.refs_1_, f32[2,128]{1,0:T(2,128)S(1)} %get-tuple-element.18.refs_2_, f32[2,128]{1,0:T(2,128)S(1)} %get-tuple-element.19.refs_3_), custom_call_target="tpu_custom_call" | custom-call | flops 1000 | bytes 1000 | tf_op jit(solution)/shard_map/own/pallas_call | solution.py:265
  5.8 0.0 copy-start
  5.8 0.2 collective-permute-done.4.moved_ref
  6.0 0.3 add_first.1
  6.3 2.9 %collective-permute-start.5 = (bf16[16,32,128]{2,1,0:T(8,128)(2,1)S(1)}, bf16[16,32,128]{2,1,0:T(8,128)(2,1)S(1)}, u32[]{:S(2)}, u32[]{:S(2)}) collective-permute-start(bf16[16,32,128]{2,1,0:T(8,128)(2,1)S(1)} %get-tuple-element.25), channel_id=1, source_target_pairs={{0,2},{2,0},{4,8},{6,10},{8,4},{10,6},{12,14},{14,12},{1,3},{3,1},... | collective-permute-start | bytes 393224 | tf_op jit(solution)/shard_map/ppermute | solution.py:451
  9.2 1.7 %collective-permute-start.6 = (bf16[16,32,128]{2,1,0:T(8,128)(2,1)S(1)}, bf16[16,32,128]{2,1,0:T(8,128)(2,1)S(1)}, u32[]{:S(2)}, u32[]{:S(2)}) collective-permute-start(bf16[16,32,128]{2,1,0:T(8,128)(2,1)S(1)} %get-tuple-element.26), channel_id=1, source_target_pairs={{0,4},{2,6},{4,0},{6,2},{8,12},{10,14},{12,8},{14,10},{1,5},{3,7},... | collective-permute-start | bytes 393224 | tf_op jit(solution)/shard_map/ppermute | solution.py:451
  10.9 2.5 %collective-permute-start.7 = (bf16[16,32,128]{2,1,0:T(8,128)(2,1)S(1)}, bf16[16,32,128]{2,1,0:T(8,128)(2,1)S(1)}, u32[]{:S(2)}, u32[]{:S(2)}) collective-permute-start(bf16[16,32,128]{2,1,0:T(8,128)(2,1)S(1)} %get-tuple-element.27), channel_id=1, source_target_pairs={{0,8},{2,10},{4,12},{6,14},{8,0},{10,2},{12,4},{14,6},{1,9},{3,11}... | collective-permute-start | bytes 393224 | tf_op jit(solution)/shard_map/ppermute | solution.py:451
  13.4 1.3 %collective-permute-start.8 = (bf16[16,32,128]{2,1,0:T(8,128)(2,1)S(1)}, bf16[16,32,128]{2,1,0:T(8,128)(2,1)S(1)}, u32[]{:S(2)}, u32[]{:S(2)}) collective-permute-start(bf16[16,32,128]{2,1,0:T(8,128)(2,1)S(1)} %get-tuple-element.28), channel_id=1, source_target_pairs={{0,10},{2,8},{4,14},{6,12},{8,2},{10,0},{12,6},{14,4},{1,11},{3,9}... | collective-permute-start | bytes 393224 | tf_op jit(solution)/shard_map/ppermute | solution.py:451
  14.8 0.0 collective-permute-done.moved_ref
  14.8 0.3 add_second.1
  15.1 0.4 %collective-permute-start.1 = (bf16[16,32,128]{2,1,0:T(8,128)(2,1)S(1)}, bf16[16,32,128]{2,1,0:T(8,128)(2,1)S(1)}, u32[]{:S(2)}, u32[]{:S(2)}) collective-permute-start(bf16[16,32,128]{2,1,0:T(8,128)(2,1)S(1)} %get-tuple-element.21), channel_id=1, source_target_pairs={{0,6},{2,4},{4,2},{6,0},{8,14},{10,12},{12,10},{14,8},{1,7},{3,5},... | collective-permute-start | bytes 393224 | tf_op jit(solution)/shard_map/ppermute | solution.py:451
  15.5 0.0 collective-permute-done.5.refs_3_
  15.5 3.6 %collective-permute-start.2 = (bf16[16,32,128]{2,1,0:T(8,128)(2,1)S(1)}, bf16[16,32,128]{2,1,0:T(8,128)(2,1)S(1)}, u32[]{:S(2)}, u32[]{:S(2)}) collective-permute-start(bf16[16,32,128]{2,1,0:T(8,128)(2,1)S(1)} %get-tuple-element.22), channel_id=1, source_target_pairs={{0,14},{2,12},{4,10},{6,8},{8,6},{10,4},{12,2},{14,0},{1,15},{3,13... | collective-permute-start | bytes 393224 | tf_op jit(solution)/shard_map/ppermute | solution.py:451
  19.1 0.0 collective-permute-done.6.refs_4_
  19.1 0.8 %collective-permute-start.3 = (bf16[16,32,128]{2,1,0:T(8,128)(2,1)S(1)}, bf16[16,32,128]{2,1,0:T(8,128)(2,1)S(1)}, u32[]{:S(2)}, u32[]{:S(2)}) collective-permute-start(bf16[16,32,128]{2,1,0:T(8,128)(2,1)S(1)} %get-tuple-element.23), channel_id=1, source_target_pairs={{0,12},{2,14},{4,6},{6,4},{8,10},{10,8},{12,0},{14,2},{1,13},{3,15... | collective-permute-start | bytes 393224 | tf_op jit(solution)/shard_map/ppermute | solution.py:451
  19.9 0.3 table.1.refs_8_
  20.2 3.7 %collective-permute-done.7.refs_5_ = bf16[16,32,128]{2,1,0:T(8,128)(2,1)S(1)} collective-permute-done((bf16[16,32,128]{2,1,0:T(8,128)(2,1)S(1)}, bf16[16,32,128]{2,1,0:T(8,128)(2,1)S(1)}, u32[]{:S(2)}, u32[]{:S(2)}) %collective-permute-start.7) | collective-permute-done | bytes 131104 | tf_op jit(solution)/shard_map/ppermute | solution.py:451
  23.9 8.8 %collective-permute-done.8.refs_6_ = bf16[16,32,128]{2,1,0:T(8,128)(2,1)S(1)} collective-permute-done((bf16[16,32,128]{2,1,0:T(8,128)(2,1)S(1)}, bf16[16,32,128]{2,1,0:T(8,128)(2,1)S(1)}, u32[]{:S(2)}, u32[]{:S(2)}) %collective-permute-start.8) | collective-permute-done | bytes 131104 | tf_op jit(solution)/shard_map/ppermute | solution.py:451
  32.7 0.0 collective-permute-done.1.refs_0_
  32.7 0.0 collective-permute-done.2.refs_1_
  32.7 0.0 collective-permute-done.3.refs_2_
  32.7 0.0 copy-done
  32.7 1.4 %peaks.1 = (f32[1,16]{1,0:T(1,128)}, f32[1,16]{1,0:T(1,128)}) custom-call(bf16[16,32,128]{2,1,0:T(8,128)(2,1)S(1)} %collective-permute-done.1.refs_0_, bf16[16,32,128]{2,1,0:T(8,128)(2,1)S(1)} %collective-permute-done.2.refs_1_, bf16[16,32,128]{2,1,0:T(8,128)(2,1)S(1)} %collective-permute-done.3.refs_2_, ...), custom_call_target="tpu_custom_call" | custom-call | tf_op jit(solution)/shard_map/peaks/pallas_call | solution.py:404
Async XLA Ops:
  3.9 2.1 %collective-permute-start.4 = (bf16[32,64,128]{2,1,0:T(8,128)(2,1)S(1)}, bf16[32,64,128]{2,1,0:T(8,128)(2,1)S(1)}, u32[]{:S(2)}, u32[]{:S(2)}) collective-permute-start(bf16[32,64,128]{2,1,0:T(8,128)(2,1)S(1)} %get-tuple-element.24), channel_id=1, source_target_pairs={{0,1},{1,0},{2,3},{3,2},{4,5},{5,4},{6,7},{7,6},{8,9},{9,8},{10,11... | collective-permute-start | bytes 1572872 | tf_op jit(solution)/shard_map/ppermute | solution.py:263
  4.4 10.3 %collective-permute-start = (bf16[32,64,128]{2,1,0:T(8,128)(2,1)S(1)}, bf16[32,64,128]{2,1,0:T(8,128)(2,1)S(1)}, u32[]{:S(2)}, u32[]{:S(2)}) collective-permute-start(bf16[32,64,128]{2,1,0:T(8,128)(2,1)S(1)} %get-tuple-element.20), channel_id=1, source_target_pairs={{0,1},{1,0},{2,3},{3,2},{4,5},{5,4},{6,7},{7,6},{8,9},{9,8},{10,11... | collective-permute-start | bytes 1572872 | tf_op jit(solution)/shard_map/ppermute | solution.py:264
  5.8 26.9 %copy-start = (f32[1,16]{1,0:T(1,128)S(1)}, f32[1,16]{1,0:T(1,128)}, u32[]{:S(2)}) copy-start(f32[1,16]{1,0:T(1,128)} %refs_9_.1) | copy-start | bytes 196
  6.3 9.2 %collective-permute-start.5 = (bf16[16,32,128]{2,1,0:T(8,128)(2,1)S(1)}, bf16[16,32,128]{2,1,0:T(8,128)(2,1)S(1)}, u32[]{:S(2)}, u32[]{:S(2)}) collective-permute-start(bf16[16,32,128]{2,1,0:T(8,128)(2,1)S(1)} %get-tuple-element.25), channel_id=1, source_target_pairs={{0,2},{2,0},{4,8},{6,10},{8,4},{10,6},{12,14},{14,12},{1,3},{3,1},... | collective-permute-start | bytes 393224 | tf_op jit(solution)/shard_map/ppermute | solution.py:451
  9.2 9.8 %collective-permute-start.6 = (bf16[16,32,128]{2,1,0:T(8,128)(2,1)S(1)}, bf16[16,32,128]{2,1,0:T(8,128)(2,1)S(1)}, u32[]{:S(2)}, u32[]{:S(2)}) collective-permute-start(bf16[16,32,128]{2,1,0:T(8,128)(2,1)S(1)} %get-tuple-element.26), channel_id=1, source_target_pairs={{0,4},{2,6},{4,0},{6,2},{8,12},{10,14},{12,8},{14,10},{1,5},{3,7},... | collective-permute-start | bytes 393224 | tf_op jit(solution)/shard_map/ppermute | solution.py:451
  10.9 13.0 %collective-permute-start.7 = (bf16[16,32,128]{2,1,0:T(8,128)(2,1)S(1)}, bf16[16,32,128]{2,1,0:T(8,128)(2,1)S(1)}, u32[]{:S(2)}, u32[]{:S(2)}) collective-permute-start(bf16[16,32,128]{2,1,0:T(8,128)(2,1)S(1)} %get-tuple-element.27), channel_id=1, source_target_pairs={{0,8},{2,10},{4,12},{6,14},{8,0},{10,2},{12,4},{14,6},{1,9},{3,11}... | collective-permute-start | bytes 393224 | tf_op jit(solution)/shard_map/ppermute | solution.py:451
  13.4 19.3 %collective-permute-start.8 = (bf16[16,32,128]{2,1,0:T(8,128)(2,1)S(1)}, bf16[16,32,128]{2,1,0:T(8,128)(2,1)S(1)}, u32[]{:S(2)}, u32[]{:S(2)}) collective-permute-start(bf16[16,32,128]{2,1,0:T(8,128)(2,1)S(1)} %get-tuple-element.28), channel_id=1, source_target_pairs={{0,10},{2,8},{4,14},{6,12},{8,2},{10,0},{12,6},{14,4},{1,11},{3,9}... | collective-permute-start | bytes 393224 | tf_op jit(solution)/shard_map/ppermute | solution.py:451
  15.1 17.6 %collective-permute-start.1 = (bf16[16,32,128]{2,1,0:T(8,128)(2,1)S(1)}, bf16[16,32,128]{2,1,0:T(8,128)(2,1)S(1)}, u32[]{:S(2)}, u32[]{:S(2)}) collective-permute-start(bf16[16,32,128]{2,1,0:T(8,128)(2,1)S(1)} %get-tuple-element.21), channel_id=1, source_target_pairs={{0,6},{2,4},{4,2},{6,0},{8,14},{10,12},{12,10},{14,8},{1,7},{3,5},... | collective-permute-start | bytes 393224 | tf_op jit(solution)/shard_map/ppermute | solution.py:451
  15.5 17.2 %collective-permute-start.2 = (bf16[16,32,128]{2,1,0:T(8,128)(2,1)S(1)}, bf16[16,32,128]{2,1,0:T(8,128)(2,1)S(1)}, u32[]{:S(2)}, u32[]{:S(2)}) collective-permute-start(bf16[16,32,128]{2,1,0:T(8,128)(2,1)S(1)} %get-tuple-element.22), channel_id=1, source_target_pairs={{0,14},{2,12},{4,10},{6,8},{8,6},{10,4},{12,2},{14,0},{1,15},{3,13... | collective-permute-start | bytes 393224 | tf_op jit(solution)/shard_map/ppermute | solution.py:451
  19.1 13.6 %collective-permute-start.3 = (bf16[16,32,128]{2,1,0:T(8,128)(2,1)S(1)}, bf16[16,32,128]{2,1,0:T(8,128)(2,1)S(1)}, u32[]{:S(2)}, u32[]{:S(2)}) collective-permute-start(bf16[16,32,128]{2,1,0:T(8,128)(2,1)S(1)} %get-tuple-element.23), channel_id=1, source_target_pairs={{0,12},{2,14},{4,6},{6,4},{8,10},{10,8},{12,0},{14,2},{1,13},{3,15... | collective-permute-start | bytes 393224 | tf_op jit(solution)/shard_map/ppermute | solution.py:451

commit v3 on v2

--- a/solution.py
+++ b/solution.py
@@ -14,6 +14,7 @@
 NB = 4
 SB = 32
 T_CAP = 1024
+FIRST_SLOTS = 3
 
 EDGE = 0.6
 STEEP = 3.0
@@ -154,7 +155,6 @@
 
 
 def store_spectra(picked_ref, law_ref, k_real, k_imag, out_refs):
-    size = out_refs[0].shape[1]
     for parity in range(2):
         for w in range(W_HALF):
             product = dot(picked_ref[parity, w], law_ref[parity, w], ((1,), (0,)))
@@ -165,8 +165,11 @@
             parts = (kr * real_part - ki * imag_part, kr * imag_part + ki * real_part)
             for k, part in enumerate(parts):
                 part = part.astype(jnp.bfloat16)
-                for i, out_ref in enumerate(out_refs):
-                    out_ref[parity * W_DEV + 2 * w + k] = part[i * size : (i + 1) * size]
+                first = 0
+                for out_ref in out_refs:
+                    last = first + out_ref.shape[1]
+                    out_ref[parity * W_DEV + 2 * w + k] = part[first:last]
+                    first = last
 
 
 def other_kernel(freq_total, slots, *refs):
@@ -238,7 +241,11 @@
     hbm = pl.BlockSpec(memory_space=pltpu.HBM)
     pinned = [pltpu.with_memory_space_constraint(a, pltpu.HBM) for a in (field, *small)]
     out = jax.ShapeDtypeStruct((2 * W_DEV, FG, ROWS), jnp.bfloat16)
-    half = jax.ShapeDtypeStruct((2 * W_DEV, FG // 2, ROWS), jnp.bfloat16)
+    flaws = FG // 2 if slots == 1 else FG // slots * FIRST_SLOTS
+    halves = [
+        jax.ShapeDtypeStruct((2 * W_DEV, count, ROWS), jnp.bfloat16)
+        for count in (flaws, FG - flaws)
+    ]
     picked = jax.ShapeDtypeStruct((2, W_HALF, FG, 2 * elements), jnp.bfloat16)
     law = pltpu.VMEM((2, W_HALF, 2 * elements, 2 * ROWS), jnp.bfloat16)
     copied = [jax.ShapeDtypeStruct(a.shape, a.dtype) for a in small[4:]]
@@ -247,7 +254,7 @@
         functools.partial(other_kernel, freq_total, slots),
         "other",
         [hbm] * len(pinned),
-        [half, half, picked, *copied, delays],
+        [*halves, picked, *copied, delays],
         [
             pltpu.SMEM(a.shape, a.dtype) if a.ndim == 1 else pltpu.VMEM(a.shape, a.dtype)
             for a in small[:4]
@@ -279,12 +286,16 @@
 def add(own, first, second, slots):
     vmem = pl.BlockSpec(memory_space=pltpu.VMEM)
     planes, flaws, rows = own.shape
-    count = max(1, slots // 2)
-    shape = jax.ShapeDtypeStruct((flaws // 2 // count, planes, rows), own.dtype)
+    size = min(flaws // slots, first.shape[1])
+    shape = jax.ShapeDtypeStruct((size, planes, rows), own.dtype)
     parts = []
-    for name, start, moved in (("add_first", 0, first), ("add_second", flaws // 2, second)):
+    for name, start, moved in (
+        ("add_first", 0, first),
+        ("add_second", first.shape[1], second),
+    ):
         kernel = functools.partial(add_kernel, start)
-        parts += call(kernel, name, [vmem] * 2, [shape] * count, [])(own, moved)
+        shapes = [shape] * (moved.shape[1] // size)
+        parts += call(kernel, name, [vmem] * 2, shapes, [])(own, moved)
     return parts
 
 
@@ -449,7 +460,7 @@
             pairs = [(a, a ^ masks[((2 * a) ^ a) & half != 0]) for a in range(slots)]
             own = slot == slots - 1
             spectra.append(parts[slot] if own else lax.ppermute(parts[slot], "freq", pairs))
-        order = (*range(half, slots - 1), *range(half), slots - 1)
+        order = (*range(FIRST_SLOTS, slots - 1), *range(FIRST_SLOTS), slots - 1)
         spectra = [spectra[slot] for slot in order]
         sources = [(order.index(slot), 0) for slot in range(slots)]
     else:

time: 34.2 us -> 34.9 us (1.020)
  waiting for transfers between devices: 12.7 us -> 13.4 us
    ppermute x1, waiting for transfers between devices: 0.18 us -> 0.93 us  [partials(): first = lax.ppermute(first, 'elem', swap)]
    ppermute x1, starting transfers between devices: 0.52 us -> 0.08 us  [partials(): first = lax.ppermute(first, 'elem', swap)]
    ppermute x1, starting transfers between devices: 0.08 us -> 0.52 us  [partials(): second = lax.ppermute(second, 'elem', swap)]
  transfers between devices with their start and end apart: 9 -> 9, of which waited for: 3 -> 3; matrix products, arithmetic and copies ran while one was open for 0% -> 0% of each run, Pallas kernels for 7% -> 6%
where the time goes in v3:
time: 34.9 us; the launch traced here: 34.7 us
  starting transfers between devices  13.8 us (40%)
  waiting for transfers between devices  13.4 us (38%)
  Pallas kernels  6.82 us (20%)
  between operations  0.69 us (2%)
    ppermute x7, starting transfers between devices, body(): lax.ppermute(parts[slot], 'freq', pairs)  13.2 us
    ppermute x7, waiting for transfers between devices, body(): lax.ppermute(parts[slot], 'freq', pairs)  12.5 us
    pallas_call x1, Pallas kernels, partials(): call(functools.partial(other_kernel, freq_total, slots), 'other', [hbm] *...  3.28 us
    pallas_call x1, Pallas kernels, peaks(): pl.pallas_call(functools.partial(peak_kernel, freq_total, folded, sources...  1.38 us
    pallas_call x1, Pallas kernels, partials(): call(functools.partial(own_kernel, freq_total, slots), 'own', [vmem] * 4,...  1.26 us
    ppermute x1, waiting for transfers between devices, partials(): first = lax.ppermute(first, 'elem', swap)  0.93 us
  transfers between devices with their start and end apart: 9, of which 3 were waited for; matrix products, arithmetic and copies ran while one was open for 0% of the time, Pallas kernels for 6%

profile of v3, /device:TPU:0, one launch (start us, length us, event | category | flops | bytes accessed | tf_op | source)
XLA Modules:
  0.0 34.7 jit_solution(17353942299884740686)
XLA Ops:
  0.6 3.3 %other.1 = (bf16[32,48,128]{2,1,0:T(8,128)(2,1)S(1)}, bf16[32,80,128]{2,1,0:T(8,128)(2,1)S(1)}, bf16[2,8,128,256]{3,2,1,0:T(8,128)(2,1)S(1)}, f32[2,128]{1,0:T(2...) custom-call(bf16[8,2,2,128,256]{4,3,2,1,0:T(8,128)(2,1)} %bitcast.3, f32[256,256]{1,0:T(8,128)} %refs_1_.1, ...), custom_call_target="tpu_custom_call" | custom-call | flops 1000 | bytes 1000 | tf_op jit(solution)/shard_map/other/pallas_call | solution.py:253
  3.9 0.5 %collective-permute-start = (bf16[32,80,128]{2,1,0:T(8,128)(2,1)S(1)}, bf16[32,80,128]{2,1,0:T(8,128)(2,1)S(1)}, u32[]{:S(2)}, u32[]{:S(2)}) collective-permute-start(bf16[32,80,128]{2,1,0:T(8,128)(2,1)S(1)} %get-tuple-element.20), channel_id=1, source_target_pairs={{0,1},{1,0},{2,3},{3,2},{4,5},{5,4},{6,7},{7,6},{8,9},{9,8},{10,11... | collective-permute-start | bytes 1966088 | tf_op jit(solution)/shard_map/ppermute | solution.py:271
  4.4 0.1 collective-permute-start.5
  4.5 1.3 %own.1.own_ref = bf16[32,128,128]{2,1,0:T(8,128)(2,1)S(1)} custom-call(bf16[2,8,128,256]{3,2,1,0:T(8,128)(2,1)S(1)} %get-tuple-element.16.refs_0_, f32[128,128]{1,0:T(8,128)S(1)} %get-tuple-element.17.refs_1_, f32[2,128]{1,0:T(2,128)S(1)} %get-tuple-element.18.refs_2_, f32[2,128]{1,0:T(2,128)S(1)} %get-tuple-element.19.refs_3_), custom_call_target="tpu_custom_call" | custom-call | flops 1000 | bytes 1000 | tf_op jit(solution)/shard_map/own/pallas_call | solution.py:272
  5.8 0.0 copy-start
  5.8 0.9 %collective-permute-done.5.moved_ref = bf16[32,48,128]{2,1,0:T(8,128)(2,1)S(1)} collective-permute-done((bf16[32,48,128]{2,1,0:T(8,128)(2,1)S(1)}, bf16[32,48,128]{2,1,0:T(8,128)(2,1)S(1)}, u32[]{:S(2)}, u32[]{:S(2)}) %collective-permute-start.5) | collective-permute-done | bytes 393248 | tf_op jit(solution)/shard_map/ppermute | solution.py:270
  6.7 0.2 add_first.1
  7.0 2.9 %collective-permute-start.6 = (bf16[16,32,128]{2,1,0:T(8,128)(2,1)S(1)}, bf16[16,32,128]{2,1,0:T(8,128)(2,1)S(1)}, u32[]{:S(2)}, u32[]{:S(2)}) collective-permute-start(bf16[16,32,128]{2,1,0:T(8,128)(2,1)S(1)} %get-tuple-element.26), channel_id=1, source_target_pairs={{0,2},{2,0},{4,8},{6,10},{8,4},{10,6},{12,14},{14,12},{1,3},{3,1},... | collective-permute-start | bytes 393224 | tf_op jit(solution)/shard_map/ppermute | solution.py:462
  9.9 1.7 %collective-permute-start.7 = (bf16[16,32,128]{2,1,0:T(8,128)(2,1)S(1)}, bf16[16,32,128]{2,1,0:T(8,128)(2,1)S(1)}, u32[]{:S(2)}, u32[]{:S(2)}) collective-permute-start(bf16[16,32,128]{2,1,0:T(8,128)(2,1)S(1)} %get-tuple-element.27), channel_id=1, source_target_pairs={{0,4},{2,6},{4,0},{6,2},{8,12},{10,14},{12,8},{14,10},{1,5},{3,7},... | collective-permute-start | bytes 393224 | tf_op jit(solution)/shard_map/ppermute | solution.py:462
  11.5 2.5 %collective-permute-start.8 = (bf16[16,32,128]{2,1,0:T(8,128)(2,1)S(1)}, bf16[16,32,128]{2,1,0:T(8,128)(2,1)S(1)}, u32[]{:S(2)}, u32[]{:S(2)}) collective-permute-start(bf16[16,32,128]{2,1,0:T(8,128)(2,1)S(1)} %get-tuple-element.28), channel_id=1, source_target_pairs={{0,8},{2,10},{4,12},{6,14},{8,0},{10,2},{12,4},{14,6},{1,9},{3,11}... | collective-permute-start | bytes 393224 | tf_op jit(solution)/shard_map/ppermute | solution.py:462
  14.0 0.0 collective-permute-done.moved_ref
  14.1 0.4 %add_second.1 = (bf16[16,32,128]{2,1,0:T(8,128)(2,1)S(1)}, bf16[16,32,128]{2,1,0:T(8,128)(2,1)S(1)}, bf16[16,32,128]{2,1,0:T(8,128)(2,1)S(1)}, bf16[16,32,128]{2,1,0:T(8,128)(2,1)S(1)}, bf16[16,32,128]{2,1,0:T(8,128)(2,1)S(1)}) custom-call(bf16[32,128,128]{2,1,0:T(8,128)(2,1)S(1)} %own.1.own_ref, bf16[32,80,128]{2,1,0:T(8,128)(2,1)S(1)} %collective-permute-done.moved_ref), custom_call_target="tpu_custom_call" | custom-call | flops 1000 | bytes 1000 | tf_op jit(solution)/shard_map/add_second/pallas_call | solution.py:298
  14.4 1.4 %collective-permute-start.1 = (bf16[16,32,128]{2,1,0:T(8,128)(2,1)S(1)}, bf16[16,32,128]{2,1,0:T(8,128)(2,1)S(1)}, u32[]{:S(2)}, u32[]{:S(2)}) collective-permute-start(bf16[16,32,128]{2,1,0:T(8,128)(2,1)S(1)} %get-tuple-element.21), channel_id=1, source_target_pairs={{0,10},{2,8},{4,14},{6,12},{8,2},{10,0},{12,6},{14,4},{1,11},{3,9}... | collective-permute-start | bytes 393224 | tf_op jit(solution)/shard_map/ppermute | solution.py:462
  15.8 0.3 collective-permute-start.2
  16.2 0.0 collective-permute-done.6.refs_4_
  16.2 3.6 %collective-permute-start.3 = (bf16[16,32,128]{2,1,0:T(8,128)(2,1)S(1)}, bf16[16,32,128]{2,1,0:T(8,128)(2,1)S(1)}, u32[]{:S(2)}, u32[]{:S(2)}) collective-permute-start(bf16[16,32,128]{2,1,0:T(8,128)(2,1)S(1)} %get-tuple-element.23), channel_id=1, source_target_pairs={{0,14},{2,12},{4,10},{6,8},{8,6},{10,4},{12,2},{14,0},{1,15},{3,13... | collective-permute-start | bytes 393224 | tf_op jit(solution)/shard_map/ppermute | solution.py:462
  19.8 0.0 collective-permute-done.7.refs_5_
  19.8 0.8 %collective-permute-start.4 = (bf16[16,32,128]{2,1,0:T(8,128)(2,1)S(1)}, bf16[16,32,128]{2,1,0:T(8,128)(2,1)S(1)}, u32[]{:S(2)}, u32[]{:S(2)}) collective-permute-start(bf16[16,32,128]{2,1,0:T(8,128)(2,1)S(1)} %get-tuple-element.24), channel_id=1, source_target_pairs={{0,12},{2,14},{4,6},{6,4},{8,10},{10,8},{12,0},{14,2},{1,13},{3,15... | collective-permute-start | bytes 393224 | tf_op jit(solution)/shard_map/ppermute | solution.py:462
  20.6 0.3 table.1.refs_8_
  20.9 3.6 %collective-permute-done.8.refs_6_ = bf16[16,32,128]{2,1,0:T(8,128)(2,1)S(1)} collective-permute-done((bf16[16,32,128]{2,1,0:T(8,128)(2,1)S(1)}, bf16[16,32,128]{2,1,0:T(8,128)(2,1)S(1)}, u32[]{:S(2)}, u32[]{:S(2)}) %collective-permute-start.8) | collective-permute-done | bytes 131104 | tf_op jit(solution)/shard_map/ppermute | solution.py:462
  24.5 8.9 %collective-permute-done.1.refs_0_ = bf16[16,32,128]{2,1,0:T(8,128)(2,1)S(1)} collective-permute-done((bf16[16,32,128]{2,1,0:T(8,128)(2,1)S(1)}, bf16[16,32,128]{2,1,0:T(8,128)(2,1)S(1)}, u32[]{:S(2)}, u32[]{:S(2)}) %collective-permute-start.1) | collective-permute-done | bytes 131104 | tf_op jit(solution)/shard_map/ppermute | solution.py:462
  33.3 0.0 collective-permute-done.2.refs_1_
  33.3 0.0 collective-permute-done.3.refs_2_
  33.3 0.0 collective-permute-done.4.refs_3_
  33.3 0.0 copy-done
  33.4 1.4 %peaks.1 = (f32[1,16]{1,0:T(1,128)}, f32[1,16]{1,0:T(1,128)}) custom-call(bf16[16,32,128]{2,1,0:T(8,128)(2,1)S(1)} %collective-permute-done.1.refs_0_, bf16[16,32,128]{2,1,0:T(8,128)(2,1)S(1)} %collective-permute-done.2.refs_1_, bf16[16,32,128]{2,1,0:T(8,128)(2,1)S(1)} %collective-permute-done.3.refs_2_, ...), custom_call_target="tpu_custom_call" | custom-call | tf_op jit(solution)/shard_map/peaks/pallas_call | solution.py:415
Async XLA Ops:
  3.9 10.1 %collective-permute-start = (bf16[32,80,128]{2,1,0:T(8,128)(2,1)S(1)}, bf16[32,80,128]{2,1,0:T(8,128)(2,1)S(1)}, u32[]{:S(2)}, u32[]{:S(2)}) collective-permute-start(bf16[32,80,128]{2,1,0:T(8,128)(2,1)S(1)} %get-tuple-element.20), channel_id=1, source_target_pairs={{0,1},{1,0},{2,3},{3,2},{4,5},{5,4},{6,7},{7,6},{8,9},{9,8},{10,11... | collective-permute-start | bytes 1966088 | tf_op jit(solution)/shard_map/ppermute | solution.py:271
  4.4 2.3 %collective-permute-start.5 = (bf16[32,48,128]{2,1,0:T(8,128)(2,1)S(1)}, bf16[32,48,128]{2,1,0:T(8,128)(2,1)S(1)}, u32[]{:S(2)}, u32[]{:S(2)}) collective-permute-start(bf16[32,48,128]{2,1,0:T(8,128)(2,1)S(1)} %get-tuple-element.25), channel_id=1, source_target_pairs={{0,1},{1,0},{2,3},{3,2},{4,5},{5,4},{6,7},{7,6},{8,9},{9,8},{10,11... | collective-permute-start | bytes 1179656 | tf_op jit(solution)/shard_map/ppermute | solution.py:270
  5.8 27.6 %copy-start = (f32[1,16]{1,0:T(1,128)S(1)}, f32[1,16]{1,0:T(1,128)}, u32[]{:S(2)}) copy-start(f32[1,16]{1,0:T(1,128)} %refs_9_.1) | copy-start | bytes 196
  7.0 9.2 %collective-permute-start.6 = (bf16[16,32,128]{2,1,0:T(8,128)(2,1)S(1)}, bf16[16,32,128]{2,1,0:T(8,128)(2,1)S(1)}, u32[]{:S(2)}, u32[]{:S(2)}) collective-permute-start(bf16[16,32,128]{2,1,0:T(8,128)(2,1)S(1)} %get-tuple-element.26), channel_id=1, source_target_pairs={{0,2},{2,0},{4,8},{6,10},{8,4},{10,6},{12,14},{14,12},{1,3},{3,1},... | collective-permute-start | bytes 393224 | tf_op jit(solution)/shard_map/ppermute | solution.py:462
  9.9 9.9 %collective-permute-start.7 = (bf16[16,32,128]{2,1,0:T(8,128)(2,1)S(1)}, bf16[16,32,128]{2,1,0:T(8,128)(2,1)S(1)}, u32[]{:S(2)}, u32[]{:S(2)}) collective-permute-start(bf16[16,32,128]{2,1,0:T(8,128)(2,1)S(1)} %get-tuple-element.27), channel_id=1, source_target_pairs={{0,4},{2,6},{4,0},{6,2},{8,12},{10,14},{12,8},{14,10},{1,5},{3,7},... | collective-permute-start | bytes 393224 | tf_op jit(solution)/shard_map/ppermute | solution.py:462
  11.5 12.9 %collective-permute-start.8 = (bf16[16,32,128]{2,1,0:T(8,128)(2,1)S(1)}, bf16[16,32,128]{2,1,0:T(8,128)(2,1)S(1)}, u32[]{:S(2)}, u32[]{:S(2)}) collective-permute-start(bf16[16,32,128]{2,1,0:T(8,128)(2,1)S(1)} %get-tuple-element.28), channel_id=1, source_target_pairs={{0,8},{2,10},{4,12},{6,14},{8,0},{10,2},{12,4},{14,6},{1,9},{3,11}... | collective-permute-start | bytes 393224 | tf_op jit(solution)/shard_map/ppermute | solution.py:462
  14.4 18.9 %collective-permute-start.1 = (bf16[16,32,128]{2,1,0:T(8,128)(2,1)S(1)}, bf16[16,32,128]{2,1,0:T(8,128)(2,1)S(1)}, u32[]{:S(2)}, u32[]{:S(2)}) collective-permute-start(bf16[16,32,128]{2,1,0:T(8,128)(2,1)S(1)} %get-tuple-element.21), channel_id=1, source_target_pairs={{0,10},{2,8},{4,14},{6,12},{8,2},{10,0},{12,6},{14,4},{1,11},{3,9}... | collective-permute-start | bytes 393224 | tf_op jit(solution)/shard_map/ppermute | solution.py:462
  15.8 17.5 %collective-permute-start.2 = (bf16[16,32,128]{2,1,0:T(8,128)(2,1)S(1)}, bf16[16,32,128]{2,1,0:T(8,128)(2,1)S(1)}, u32[]{:S(2)}, u32[]{:S(2)}) collective-permute-start(bf16[16,32,128]{2,1,0:T(8,128)(2,1)S(1)} %get-tuple-element.22), channel_id=1, source_target_pairs={{0,6},{2,4},{4,2},{6,0},{8,14},{10,12},{12,10},{14,8},{1,7},{3,5},... | collective-permute-start | bytes 393224 | tf_op jit(solution)/shard_map/ppermute | solution.py:462
  16.2 17.2 %collective-permute-start.3 = (bf16[16,32,128]{2,1,0:T(8,128)(2,1)S(1)}, bf16[16,32,128]{2,1,0:T(8,128)(2,1)S(1)}, u32[]{:S(2)}, u32[]{:S(2)}) collective-permute-start(bf16[16,32,128]{2,1,0:T(8,128)(2,1)S(1)} %get-tuple-element.23), channel_id=1, source_target_pairs={{0,14},{2,12},{4,10},{6,8},{8,6},{10,4},{12,2},{14,0},{1,15},{3,13... | collective-permute-start | bytes 393224 | tf_op jit(solution)/shard_map/ppermute | solution.py:462
  19.8 13.6 %collective-permute-start.4 = (bf16[16,32,128]{2,1,0:T(8,128)(2,1)S(1)}, bf16[16,32,128]{2,1,0:T(8,128)(2,1)S(1)}, u32[]{:S(2)}, u32[]{:S(2)}) collective-permute-start(bf16[16,32,128]{2,1,0:T(8,128)(2,1)S(1)} %get-tuple-element.24), channel_id=1, source_target_pairs={{0,12},{2,14},{4,6},{6,4},{8,10},{10,8},{12,0},{14,2},{1,13},{3,15... | collective-permute-start | bytes 393224 | tf_op jit(solution)/shard_map/ppermute | solution.py:462

commit v4 on v3

--- a/solution.py
+++ b/solution.py
@@ -268,14 +268,16 @@
         ],
     )(*pinned)
     first = lax.ppermute(first, "elem", swap)
-    second = lax.ppermute(second, "elem", swap)
     (own,) = call(
         functools.partial(own_kernel, freq_total, slots), "own", [vmem] * 4, [out], [law]
     )(own_picked, delays, size, slope)
     return own, first, second
 
 
-def add_kernel(first, own_ref, moved_ref, *refs):
+def add_kernel(first, passed, own_ref, moved_ref, *refs):
+    if passed:
+        source_ref, *refs, target_ref = refs
+        target_ref[...] = source_ref[...]
     size = refs[0].shape[0]
     for slot, ref in enumerate(refs):
         own = own_ref[:, pl.ds(first + slot * size, size)].astype(jnp.float32)
@@ -283,20 +285,23 @@
         ref[...] = jnp.swapaxes(both, 0, 1).astype(jnp.bfloat16)
 
 
-def add(own, first, second, slots):
+def add(own, first, second, swap, slots):
     vmem = pl.BlockSpec(memory_space=pltpu.VMEM)
     planes, flaws, rows = own.shape
     size = min(flaws // slots, first.shape[1])
     shape = jax.ShapeDtypeStruct((size, planes, rows), own.dtype)
-    parts = []
-    for name, start, moved in (
-        ("add_first", 0, first),
-        ("add_second", first.shape[1], second),
-    ):
-        kernel = functools.partial(add_kernel, start)
-        shapes = [shape] * (moved.shape[1] // size)
-        parts += call(kernel, name, [vmem] * 2, shapes, [])(own, moved)
-    return parts
+    early = first.shape[1]
+    *parts, second = call(
+        functools.partial(add_kernel, 0, 1),
+        "add_first",
+        [vmem] * 3,
+        [shape] * (early // size) + [jax.ShapeDtypeStruct(second.shape, second.dtype)],
+        [],
+    )(own, first, second)
+    second = lax.ppermute(second, "elem", swap)
+    kernel = functools.partial(add_kernel, early, 0)
+    shapes = [shape] * ((flaws - early) // size)
+    return parts + [*call(kernel, "add_second", [vmem] * 2, shapes, [])(own, second)]
 
 
 def table_kernel(freq_total, slots, table_ref):
@@ -452,7 +457,7 @@
     times = sample_count // 2 if folded else sample_count
     twiddles = table(freq_total, slots, times, min(128, times))
     field = beam_field.reshape(W_HALF, 2, *beam_field.shape[1:])
-    parts = add(*partials(field, small, swap, freq_total, slots), slots)
+    parts = add(*partials(field, small, swap, freq_total, slots), swap, slots)
     if direct:
         half = slots // 2
         spectra = []

time: 34.9 us -> 34.3 us (0.983)
  waiting for transfers between devices: 13.4 us -> 12.7 us
    ppermute x1, waiting for transfers between devices: 0.93 us -> 0.07 us  [partials(): first = lax.ppermute(first, 'elem', swap)]
    ppermute x1, starting transfers between devices: 0.08 us -> 0.52 us  [partials(): first = lax.ppermute(first, 'elem', swap)]
where the time goes in v4:
time: 34.3 us; the launch traced here: 34.2 us
  starting transfers between devices  13.9 us (41%)
  waiting for transfers between devices  12.7 us (37%)
  Pallas kernels  6.86 us (20%)
  between operations  0.69 us (2%)
    ppermute x7, starting transfers between devices, body(): lax.ppermute(parts[slot], 'freq', pairs)  13 us
    ppermute x7, waiting for transfers between devices, body(): lax.ppermute(parts[slot], 'freq', pairs)  12.6 us
    pallas_call x1, Pallas kernels, partials(): call(functools.partial(other_kernel, freq_total, slots), 'other', [hbm] *...  3.28 us
    pallas_call x1, Pallas kernels, peaks(): pl.pallas_call(functools.partial(peak_kernel, freq_total, folded, sources...  1.37 us
    pallas_call x1, Pallas kernels, partials(): call(functools.partial(own_kernel, freq_total, slots), 'own', [vmem] * 4,...  1.26 us
  transfers between devices with their start and end apart: 9, of which 3 were waited for; matrix products, arithmetic and copies ran while one was open for 0% of the time, Pallas kernels for 6%

profile of v4, /device:TPU:0, one launch (start us, length us, event | category | flops | bytes accessed | tf_op | source)
XLA Modules:
  0.0 34.2 jit_solution(6737110074968556354)
XLA Ops:
  0.6 3.3 %other.1 = (bf16[32,48,128]{2,1,0:T(8,128)(2,1)S(1)}, bf16[32,80,128]{2,1,0:T(8,128)(2,1)S(1)}, bf16[2,8,128,256]{3,2,1,0:T(8,128)(2,1)S(1)}, f32[2,128]{1,0:T(2...) custom-call(bf16[8,2,2,128,256]{4,3,2,1,0:T(8,128)(2,1)} %bitcast.3, f32[256,256]{1,0:T(8,128)} %refs_1_.1, ...), custom_call_target="tpu_custom_call" | custom-call | flops 1000 | bytes 1000 | tf_op jit(solution)/shard_map/other/pallas_call | solution.py:253
  3.9 0.5 %collective-permute-start = (bf16[32,48,128]{2,1,0:T(8,128)(2,1)S(1)}, bf16[32,48,128]{2,1,0:T(8,128)(2,1)S(1)}, u32[]{:S(2)}, u32[]{:S(2)}) collective-permute-start(bf16[32,48,128]{2,1,0:T(8,128)(2,1)S(1)} %get-tuple-element.21), channel_id=1, source_target_pairs={{0,1},{1,0},{2,3},{3,2},{4,5},{5,4},{6,7},{7,6},{8,9},{9,8},{10,11... | collective-permute-start | bytes 1179656 | tf_op jit(solution)/shard_map/ppermute | solution.py:270
  4.4 1.3 %own.1.own_ref = bf16[32,128,128]{2,1,0:T(8,128)(2,1)S(1)} custom-call(bf16[2,8,128,256]{3,2,1,0:T(8,128)(2,1)S(1)} %get-tuple-element.17.refs_0_, f32[128,128]{1,0:T(8,128)S(1)} %get-tuple-element.18.refs_1_, f32[2,128]{1,0:T(2,128)S(1)} %get-tuple-element.19.refs_2_, f32[2,128]{1,0:T(2,128)S(1)} %get-tuple-element.20.refs_3_), custom_call_target="tpu_custom_call" | custom-call | flops 1000 | bytes 1000 | tf_op jit(solution)/shard_map/own/pallas_call | solution.py:271
  5.7 0.0 copy-start
  5.7 0.1 collective-permute-done.moved_ref
  5.8 0.3 add_first.1
  6.1 0.4 %collective-permute-start.1 = (bf16[32,80,128]{2,1,0:T(8,128)(2,1)S(1)}, bf16[32,80,128]{2,1,0:T(8,128)(2,1)S(1)}, u32[]{:S(2)}, u32[]{:S(2)}) collective-permute-start(bf16[32,80,128]{2,1,0:T(8,128)(2,1)S(1)} %get-tuple-element.23), channel_id=1, source_target_pairs={{0,1},{1,0},{2,3},{3,2},{4,5},{5,4},{6,7},{7,6},{8,9},{9,8},{10,11... | collective-permute-start | bytes 1966088 | tf_op jit(solution)/shard_map/ppermute | solution.py:301
  6.5 2.6 %collective-permute-start.6 = (bf16[16,32,128]{2,1,0:T(8,128)(2,1)S(1)}, bf16[16,32,128]{2,1,0:T(8,128)(2,1)S(1)}, u32[]{:S(2)}, u32[]{:S(2)}) collective-permute-start(bf16[16,32,128]{2,1,0:T(8,128)(2,1)S(1)} %get-tuple-element.28), channel_id=1, source_target_pairs={{0,2},{2,0},{4,8},{6,10},{8,4},{10,6},{12,14},{14,12},{1,3},{3,1},... | collective-permute-start | bytes 393224 | tf_op jit(solution)/shard_map/ppermute | solution.py:467
  9.1 1.7 %collective-permute-start.7 = (bf16[16,32,128]{2,1,0:T(8,128)(2,1)S(1)}, bf16[16,32,128]{2,1,0:T(8,128)(2,1)S(1)}, u32[]{:S(2)}, u32[]{:S(2)}) collective-permute-start(bf16[16,32,128]{2,1,0:T(8,128)(2,1)S(1)} %get-tuple-element.29), channel_id=1, source_target_pairs={{0,4},{2,6},{4,0},{6,2},{8,12},{10,14},{12,8},{14,10},{1,5},{3,7},... | collective-permute-start | bytes 393224 | tf_op jit(solution)/shard_map/ppermute | solution.py:467
  10.8 2.5 %collective-permute-start.8 = (bf16[16,32,128]{2,1,0:T(8,128)(2,1)S(1)}, bf16[16,32,128]{2,1,0:T(8,128)(2,1)S(1)}, u32[]{:S(2)}, u32[]{:S(2)}) collective-permute-start(bf16[16,32,128]{2,1,0:T(8,128)(2,1)S(1)} %get-tuple-element.30), channel_id=1, source_target_pairs={{0,8},{2,10},{4,12},{6,14},{8,0},{10,2},{12,4},{14,6},{1,9},{3,11}... | collective-permute-start | bytes 393224 | tf_op jit(solution)/shard_map/ppermute | solution.py:467
  13.3 0.0 collective-permute-done.1.moved_ref
  13.3 0.4 %add_second.1 = (bf16[16,32,128]{2,1,0:T(8,128)(2,1)S(1)}, bf16[16,32,128]{2,1,0:T(8,128)(2,1)S(1)}, bf16[16,32,128]{2,1,0:T(8,128)(2,1)S(1)}, bf16[16,32,128]{2,1,0:T(8,128)(2,1)S(1)}, bf16[16,32,128]{2,1,0:T(8,128)(2,1)S(1)}) custom-call(bf16[32,128,128]{2,1,0:T(8,128)(2,1)S(1)} %own.1.own_ref, bf16[32,80,128]{2,1,0:T(8,128)(2,1)S(1)} %collective-permute-done.1.moved_ref), custom_call_target="tpu_custom_call" | custom-call | flops 1000 | bytes 1000 | tf_op jit(solution)/shard_map/add_second/pallas_call | solution.py:304
  13.7 1.4 %collective-permute-start.2 = (bf16[16,32,128]{2,1,0:T(8,128)(2,1)S(1)}, bf16[16,32,128]{2,1,0:T(8,128)(2,1)S(1)}, u32[]{:S(2)}, u32[]{:S(2)}) collective-permute-start(bf16[16,32,128]{2,1,0:T(8,128)(2,1)S(1)} %get-tuple-element.24), channel_id=1, source_target_pairs={{0,10},{2,8},{4,14},{6,12},{8,2},{10,0},{12,6},{14,4},{1,11},{3,9}... | collective-permute-start | bytes 393224 | tf_op jit(solution)/shard_map/ppermute | solution.py:467
  15.1 0.3 collective-permute-start.3
  15.4 0.0 collective-permute-done.6.refs_4_
  15.4 3.6 %collective-permute-start.4 = (bf16[16,32,128]{2,1,0:T(8,128)(2,1)S(1)}, bf16[16,32,128]{2,1,0:T(8,128)(2,1)S(1)}, u32[]{:S(2)}, u32[]{:S(2)}) collective-permute-start(bf16[16,32,128]{2,1,0:T(8,128)(2,1)S(1)} %get-tuple-element.26), channel_id=1, source_target_pairs={{0,14},{2,12},{4,10},{6,8},{8,6},{10,4},{12,2},{14,0},{1,15},{3,13... | collective-permute-start | bytes 393224 | tf_op jit(solution)/shard_map/ppermute | solution.py:467
  19.0 0.0 collective-permute-done.7.refs_5_
  19.0 0.8 %collective-permute-start.5 = (bf16[16,32,128]{2,1,0:T(8,128)(2,1)S(1)}, bf16[16,32,128]{2,1,0:T(8,128)(2,1)S(1)}, u32[]{:S(2)}, u32[]{:S(2)}) collective-permute-start(bf16[16,32,128]{2,1,0:T(8,128)(2,1)S(1)} %get-tuple-element.27), channel_id=1, source_target_pairs={{0,12},{2,14},{4,6},{6,4},{8,10},{10,8},{12,0},{14,2},{1,13},{3,15... | collective-permute-start | bytes 393224 | tf_op jit(solution)/shard_map/ppermute | solution.py:467
  19.9 0.3 table.1.refs_8_
  20.2 3.6 %collective-permute-done.8.refs_6_ = bf16[16,32,128]{2,1,0:T(8,128)(2,1)S(1)} collective-permute-done((bf16[16,32,128]{2,1,0:T(8,128)(2,1)S(1)}, bf16[16,32,128]{2,1,0:T(8,128)(2,1)S(1)}, u32[]{:S(2)}, u32[]{:S(2)}) %collective-permute-start.8) | collective-permute-done | bytes 131104 | tf_op jit(solution)/shard_map/ppermute | solution.py:467
  23.8 9.0 %collective-permute-done.2.refs_0_ = bf16[16,32,128]{2,1,0:T(8,128)(2,1)S(1)} collective-permute-done((bf16[16,32,128]{2,1,0:T(8,128)(2,1)S(1)}, bf16[16,32,128]{2,1,0:T(8,128)(2,1)S(1)}, u32[]{:S(2)}, u32[]{:S(2)}) %collective-permute-start.2) | collective-permute-done | bytes 131104 | tf_op jit(solution)/shard_map/ppermute | solution.py:467
  32.8 0.0 collective-permute-done.3.refs_1_
  32.8 0.0 collective-permute-done.4.refs_2_
  32.8 0.0 collective-permute-done.5.refs_3_
  32.8 0.0 copy-done
  32.8 1.4 %peaks.1 = (f32[1,16]{1,0:T(1,128)}, f32[1,16]{1,0:T(1,128)}) custom-call(bf16[16,32,128]{2,1,0:T(8,128)(2,1)S(1)} %collective-permute-done.2.refs_0_, bf16[16,32,128]{2,1,0:T(8,128)(2,1)S(1)} %collective-permute-done.3.refs_1_, bf16[16,32,128]{2,1,0:T(8,128)(2,1)S(1)} %collective-permute-done.4.refs_2_, ...), custom_call_target="tpu_custom_call" | custom-call | tf_op jit(solution)/shard_map/peaks/pallas_call | solution.py:420
Async XLA Ops:
  3.9 1.9 %collective-permute-start = (bf16[32,48,128]{2,1,0:T(8,128)(2,1)S(1)}, bf16[32,48,128]{2,1,0:T(8,128)(2,1)S(1)}, u32[]{:S(2)}, u32[]{:S(2)}) collective-permute-start(bf16[32,48,128]{2,1,0:T(8,128)(2,1)S(1)} %get-tuple-element.21), channel_id=1, source_target_pairs={{0,1},{1,0},{2,3},{3,2},{4,5},{5,4},{6,7},{7,6},{8,9},{9,8},{10,11... | collective-permute-start | bytes 1179656 | tf_op jit(solution)/shard_map/ppermute | solution.py:270
  5.7 27.1 %copy-start = (f32[1,16]{1,0:T(1,128)S(1)}, f32[1,16]{1,0:T(1,128)}, u32[]{:S(2)}) copy-start(f32[1,16]{1,0:T(1,128)} %refs_9_.1) | copy-start | bytes 196
  6.1 7.2 %collective-permute-start.1 = (bf16[32,80,128]{2,1,0:T(8,128)(2,1)S(1)}, bf16[32,80,128]{2,1,0:T(8,128)(2,1)S(1)}, u32[]{:S(2)}, u32[]{:S(2)}) collective-permute-start(bf16[32,80,128]{2,1,0:T(8,128)(2,1)S(1)} %get-tuple-element.23), channel_id=1, source_target_pairs={{0,1},{1,0},{2,3},{3,2},{4,5},{5,4},{6,7},{7,6},{8,9},{9,8},{10,11... | collective-permute-start | bytes 1966088 | tf_op jit(solution)/shard_map/ppermute | solution.py:301
  6.5 8.9 %collective-permute-start.6 = (bf16[16,32,128]{2,1,0:T(8,128)(2,1)S(1)}, bf16[16,32,128]{2,1,0:T(8,128)(2,1)S(1)}, u32[]{:S(2)}, u32[]{:S(2)}) collective-permute-start(bf16[16,32,128]{2,1,0:T(8,128)(2,1)S(1)} %get-tuple-element.28), channel_id=1, source_target_pairs={{0,2},{2,0},{4,8},{6,10},{8,4},{10,6},{12,14},{14,12},{1,3},{3,1},... | collective-permute-start | bytes 393224 | tf_op jit(solution)/shard_map/ppermute | solution.py:467
  9.1 9.9 %collective-permute-start.7 = (bf16[16,32,128]{2,1,0:T(8,128)(2,1)S(1)}, bf16[16,32,128]{2,1,0:T(8,128)(2,1)S(1)}, u32[]{:S(2)}, u32[]{:S(2)}) collective-permute-start(bf16[16,32,128]{2,1,0:T(8,128)(2,1)S(1)} %get-tuple-element.29), channel_id=1, source_target_pairs={{0,4},{2,6},{4,0},{6,2},{8,12},{10,14},{12,8},{14,10},{1,5},{3,7},... | collective-permute-start | bytes 393224 | tf_op jit(solution)/shard_map/ppermute | solution.py:467
  10.8 13.0 %collective-permute-start.8 = (bf16[16,32,128]{2,1,0:T(8,128)(2,1)S(1)}, bf16[16,32,128]{2,1,0:T(8,128)(2,1)S(1)}, u32[]{:S(2)}, u32[]{:S(2)}) collective-permute-start(bf16[16,32,128]{2,1,0:T(8,128)(2,1)S(1)} %get-tuple-element.30), channel_id=1, source_target_pairs={{0,8},{2,10},{4,12},{6,14},{8,0},{10,2},{12,4},{14,6},{1,9},{3,11}... | collective-permute-start | bytes 393224 | tf_op jit(solution)/shard_map/ppermute | solution.py:467
  13.7 19.1 %collective-permute-start.2 = (bf16[16,32,128]{2,1,0:T(8,128)(2,1)S(1)}, bf16[16,32,128]{2,1,0:T(8,128)(2,1)S(1)}, u32[]{:S(2)}, u32[]{:S(2)}) collective-permute-start(bf16[16,32,128]{2,1,0:T(8,128)(2,1)S(1)} %get-tuple-element.24), channel_id=1, source_target_pairs={{0,10},{2,8},{4,14},{6,12},{8,2},{10,0},{12,6},{14,4},{1,11},{3,9}... | collective-permute-start | bytes 393224 | tf_op jit(solution)/shard_map/ppermute | solution.py:467
  15.1 17.7 %collective-permute-start.3 = (bf16[16,32,128]{2,1,0:T(8,128)(2,1)S(1)}, bf16[16,32,128]{2,1,0:T(8,128)(2,1)S(1)}, u32[]{:S(2)}, u32[]{:S(2)}) collective-permute-start(bf16[16,32,128]{2,1,0:T(8,128)(2,1)S(1)} %get-tuple-element.25), channel_id=1, source_target_pairs={{0,6},{2,4},{4,2},{6,0},{8,14},{10,12},{12,10},{14,8},{1,7},{3,5},... | collective-permute-start | bytes 393224 | tf_op jit(solution)/shard_map/ppermute | solution.py:467
  15.4 17.4 %collective-permute-start.4 = (bf16[16,32,128]{2,1,0:T(8,128)(2,1)S(1)}, bf16[16,32,128]{2,1,0:T(8,128)(2,1)S(1)}, u32[]{:S(2)}, u32[]{:S(2)}) collective-permute-start(bf16[16,32,128]{2,1,0:T(8,128)(2,1)S(1)} %get-tuple-element.26), channel_id=1, source_target_pairs={{0,14},{2,12},{4,10},{6,8},{8,6},{10,4},{12,2},{14,0},{1,15},{3,13... | collective-permute-start | bytes 393224 | tf_op jit(solution)/shard_map/ppermute | solution.py:467
  19.0 13.8 %collective-permute-start.5 = (bf16[16,32,128]{2,1,0:T(8,128)(2,1)S(1)}, bf16[16,32,128]{2,1,0:T(8,128)(2,1)S(1)}, u32[]{:S(2)}, u32[]{:S(2)}) collective-permute-start(bf16[16,32,128]{2,1,0:T(8,128)(2,1)S(1)} %get-tuple-element.27), channel_id=1, source_target_pairs={{0,12},{2,14},{4,6},{6,4},{8,10},{10,8},{12,0},{14,2},{1,13},{3,15... | collective-permute-start | bytes 393224 | tf_op jit(solution)/shard_map/ppermute | solution.py:467

commit v5 on v2

--- a/solution.py
+++ b/solution.py
@@ -145,12 +145,14 @@
 
 def pick_fields(parity, picks, field_ref, picked_refs):
     elements, sites = field_ref.shape[3:]
-    for w in range(W_HALF):
-        picked = dot(
-            picks, field_ref[w, parity].reshape(2 * elements, sites), ((1,), (1,))
-        ).astype(jnp.bfloat16)
-        for i, ref in enumerate(picked_refs):
-            ref[parity, w] = picked[i * FG : (i + 1) * FG]
+    width = 2
+    for w in range(0, W_HALF, width):
+        rows = field_ref[w : w + width, parity].reshape(width * 2 * elements, sites)
+        picked = dot(picks, rows, ((1,), (1,))).astype(jnp.bfloat16)
+        for k in range(width):
+            columns = slice(k * 2 * elements, (k + 1) * 2 * elements)
+            for i, ref in enumerate(picked_refs):
+                ref[parity, w + k] = picked[i * FG : (i + 1) * FG, columns]
 
 
 def store_spectra(picked_ref, law_ref, k_real, k_imag, out_refs):
@@ -340,7 +342,7 @@
     def _():
         best_ref[...] = jnp.zeros_like(best_ref)
 
-    width = min(2, columns)
+    width = min(4, columns)
     for first in range(0, columns, width):
         parts = []
         for parity in range(2):

time: 34.2 us -> 34.3 us (level)
  no operation moved by 1% of the time
where the time goes in v5:
time: 34.3 us; the launch traced here: 34.1 us
  starting transfers between devices  13.8 us (40%)
  waiting for transfers between devices  12.7 us (37%)
  Pallas kernels  6.94 us (20%)
  between operations  0.69 us (2%)
    ppermute x7, starting transfers between devices, body(): lax.ppermute(parts[slot], 'freq', pairs)  13.2 us
    ppermute x7, waiting for transfers between devices, body(): lax.ppermute(parts[slot], 'freq', pairs)  12.5 us
    pallas_call x1, Pallas kernels, partials(): call(functools.partial(other_kernel, freq_total, slots), 'other', [hbm] *...  3.28 us
    pallas_call x1, Pallas kernels, peaks(): pl.pallas_call(functools.partial(peak_kernel, freq_total, folded, sources...  1.42 us
    pallas_call x1, Pallas kernels, partials(): call(functools.partial(own_kernel, freq_total, slots), 'own', [vmem] * 4,...  1.26 us
  transfers between devices with their start and end apart: 9, of which 3 were waited for; matrix products, arithmetic and copies ran while one was open for 0% of the time, Pallas kernels for 7%

profile of v5, /device:TPU:0, one launch (start us, length us, event | category | flops | bytes accessed | tf_op | source)
XLA Modules:
  0.0 34.1 jit_solution(1358036728902800698)
XLA Ops:
  0.6 3.3 %other.1 = (bf16[32,64,128]{2,1,0:T(8,128)(2,1)S(1)}, bf16[32,64,128]{2,1,0:T(8,128)(2,1)S(1)}, bf16[2,8,128,256]{3,2,1,0:T(8,128)(2,1)S(1)}, f32[2,128]{1,0:T(2...) custom-call(bf16[8,2,2,128,256]{4,3,2,1,0:T(8,128)(2,1)} %bitcast.3, f32[256,256]{1,0:T(8,128)} %refs_1_.1, ...), custom_call_target="tpu_custom_call" | custom-call | flops 1000 | bytes 1000 | tf_op jit(solution)/shard_map/other/pallas_call | solution.py:248
  3.9 0.5 %collective-permute-start.4 = (bf16[32,64,128]{2,1,0:T(8,128)(2,1)S(1)}, bf16[32,64,128]{2,1,0:T(8,128)(2,1)S(1)}, u32[]{:S(2)}, u32[]{:S(2)}) collective-permute-start(bf16[32,64,128]{2,1,0:T(8,128)(2,1)S(1)} %get-tuple-element.24), channel_id=1, source_target_pairs={{0,1},{1,0},{2,3},{3,2},{4,5},{5,4},{6,7},{7,6},{8,9},{9,8},{10,11... | collective-permute-start | bytes 1572872 | tf_op jit(solution)/shard_map/ppermute | solution.py:265
  4.4 0.1 collective-permute-start
  4.5 1.3 %own.1.own_ref = bf16[32,128,128]{2,1,0:T(8,128)(2,1)S(1)} custom-call(bf16[2,8,128,256]{3,2,1,0:T(8,128)(2,1)S(1)} %get-tuple-element.16.refs_0_, f32[128,128]{1,0:T(8,128)S(1)} %get-tuple-element.17.refs_1_, f32[2,128]{1,0:T(2,128)S(1)} %get-tuple-element.18.refs_2_, f32[2,128]{1,0:T(2,128)S(1)} %get-tuple-element.19.refs_3_), custom_call_target="tpu_custom_call" | custom-call | flops 1000 | bytes 1000 | tf_op jit(solution)/shard_map/own/pallas_call | solution.py:267
  5.8 0.0 copy-start
  5.8 0.2 collective-permute-done.4.moved_ref
  6.0 0.3 add_first.1
  6.3 2.9 %collective-permute-start.5 = (bf16[16,32,128]{2,1,0:T(8,128)(2,1)S(1)}, bf16[16,32,128]{2,1,0:T(8,128)(2,1)S(1)}, u32[]{:S(2)}, u32[]{:S(2)}) collective-permute-start(bf16[16,32,128]{2,1,0:T(8,128)(2,1)S(1)} %get-tuple-element.25), channel_id=1, source_target_pairs={{0,2},{2,0},{4,8},{6,10},{8,4},{10,6},{12,14},{14,12},{1,3},{3,1},... | collective-permute-start | bytes 393224 | tf_op jit(solution)/shard_map/ppermute | solution.py:453
  9.2 1.7 %collective-permute-start.6 = (bf16[16,32,128]{2,1,0:T(8,128)(2,1)S(1)}, bf16[16,32,128]{2,1,0:T(8,128)(2,1)S(1)}, u32[]{:S(2)}, u32[]{:S(2)}) collective-permute-start(bf16[16,32,128]{2,1,0:T(8,128)(2,1)S(1)} %get-tuple-element.26), channel_id=1, source_target_pairs={{0,4},{2,6},{4,0},{6,2},{8,12},{10,14},{12,8},{14,10},{1,5},{3,7},... | collective-permute-start | bytes 393224 | tf_op jit(solution)/shard_map/ppermute | solution.py:453
  10.9 2.5 %collective-permute-start.7 = (bf16[16,32,128]{2,1,0:T(8,128)(2,1)S(1)}, bf16[16,32,128]{2,1,0:T(8,128)(2,1)S(1)}, u32[]{:S(2)}, u32[]{:S(2)}) collective-permute-start(bf16[16,32,128]{2,1,0:T(8,128)(2,1)S(1)} %get-tuple-element.27), channel_id=1, source_target_pairs={{0,8},{2,10},{4,12},{6,14},{8,0},{10,2},{12,4},{14,6},{1,9},{3,11}... | collective-permute-start | bytes 393224 | tf_op jit(solution)/shard_map/ppermute | solution.py:453
  13.4 1.3 %collective-permute-start.8 = (bf16[16,32,128]{2,1,0:T(8,128)(2,1)S(1)}, bf16[16,32,128]{2,1,0:T(8,128)(2,1)S(1)}, u32[]{:S(2)}, u32[]{:S(2)}) collective-permute-start(bf16[16,32,128]{2,1,0:T(8,128)(2,1)S(1)} %get-tuple-element.28), channel_id=1, source_target_pairs={{0,10},{2,8},{4,14},{6,12},{8,2},{10,0},{12,6},{14,4},{1,11},{3,9}... | collective-permute-start | bytes 393224 | tf_op jit(solution)/shard_map/ppermute | solution.py:453
  14.8 0.0 collective-permute-done.moved_ref
  14.8 0.3 add_second.1
  15.1 0.4 %collective-permute-start.1 = (bf16[16,32,128]{2,1,0:T(8,128)(2,1)S(1)}, bf16[16,32,128]{2,1,0:T(8,128)(2,1)S(1)}, u32[]{:S(2)}, u32[]{:S(2)}) collective-permute-start(bf16[16,32,128]{2,1,0:T(8,128)(2,1)S(1)} %get-tuple-element.21), channel_id=1, source_target_pairs={{0,6},{2,4},{4,2},{6,0},{8,14},{10,12},{12,10},{14,8},{1,7},{3,5},... | collective-permute-start | bytes 393224 | tf_op jit(solution)/shard_map/ppermute | solution.py:453
  15.5 0.0 collective-permute-done.5.refs_3_
  15.5 3.6 %collective-permute-start.2 = (bf16[16,32,128]{2,1,0:T(8,128)(2,1)S(1)}, bf16[16,32,128]{2,1,0:T(8,128)(2,1)S(1)}, u32[]{:S(2)}, u32[]{:S(2)}) collective-permute-start(bf16[16,32,128]{2,1,0:T(8,128)(2,1)S(1)} %get-tuple-element.22), channel_id=1, source_target_pairs={{0,14},{2,12},{4,10},{6,8},{8,6},{10,4},{12,2},{14,0},{1,15},{3,13... | collective-permute-start | bytes 393224 | tf_op jit(solution)/shard_map/ppermute | solution.py:453
  19.1 0.0 collective-permute-done.6.refs_4_
  19.1 0.8 %collective-permute-start.3 = (bf16[16,32,128]{2,1,0:T(8,128)(2,1)S(1)}, bf16[16,32,128]{2,1,0:T(8,128)(2,1)S(1)}, u32[]{:S(2)}, u32[]{:S(2)}) collective-permute-start(bf16[16,32,128]{2,1,0:T(8,128)(2,1)S(1)} %get-tuple-element.23), channel_id=1, source_target_pairs={{0,12},{2,14},{4,6},{6,4},{8,10},{10,8},{12,0},{14,2},{1,13},{3,15... | collective-permute-start | bytes 393224 | tf_op jit(solution)/shard_map/ppermute | solution.py:453
  19.9 0.3 table.1.refs_8_
  20.2 3.7 %collective-permute-done.7.refs_5_ = bf16[16,32,128]{2,1,0:T(8,128)(2,1)S(1)} collective-permute-done((bf16[16,32,128]{2,1,0:T(8,128)(2,1)S(1)}, bf16[16,32,128]{2,1,0:T(8,128)(2,1)S(1)}, u32[]{:S(2)}, u32[]{:S(2)}) %collective-permute-start.7) | collective-permute-done | bytes 131104 | tf_op jit(solution)/shard_map/ppermute | solution.py:453
  23.9 8.8 %collective-permute-done.8.refs_6_ = bf16[16,32,128]{2,1,0:T(8,128)(2,1)S(1)} collective-permute-done((bf16[16,32,128]{2,1,0:T(8,128)(2,1)S(1)}, bf16[16,32,128]{2,1,0:T(8,128)(2,1)S(1)}, u32[]{:S(2)}, u32[]{:S(2)}) %collective-permute-start.8) | collective-permute-done | bytes 131104 | tf_op jit(solution)/shard_map/ppermute | solution.py:453
  32.7 0.0 collective-permute-done.1.refs_0_
  32.7 0.0 collective-permute-done.2.refs_1_
  32.7 0.0 collective-permute-done.3.refs_2_
  32.7 0.0 copy-done
  32.7 1.4 %peaks.1 = (f32[1,16]{1,0:T(1,128)}, f32[1,16]{1,0:T(1,128)}) custom-call(bf16[16,32,128]{2,1,0:T(8,128)(2,1)S(1)} %collective-permute-done.1.refs_0_, bf16[16,32,128]{2,1,0:T(8,128)(2,1)S(1)} %collective-permute-done.2.refs_1_, bf16[16,32,128]{2,1,0:T(8,128)(2,1)S(1)} %collective-permute-done.3.refs_2_, ...), custom_call_target="tpu_custom_call" | custom-call | tf_op jit(solution)/shard_map/peaks/pallas_call | solution.py:406
Async XLA Ops:
  3.9 2.1 %collective-permute-start.4 = (bf16[32,64,128]{2,1,0:T(8,128)(2,1)S(1)}, bf16[32,64,128]{2,1,0:T(8,128)(2,1)S(1)}, u32[]{:S(2)}, u32[]{:S(2)}) collective-permute-start(bf16[32,64,128]{2,1,0:T(8,128)(2,1)S(1)} %get-tuple-element.24), channel_id=1, source_target_pairs={{0,1},{1,0},{2,3},{3,2},{4,5},{5,4},{6,7},{7,6},{8,9},{9,8},{10,11... | collective-permute-start | bytes 1572872 | tf_op jit(solution)/shard_map/ppermute | solution.py:265
  4.4 10.3 %collective-permute-start = (bf16[32,64,128]{2,1,0:T(8,128)(2,1)S(1)}, bf16[32,64,128]{2,1,0:T(8,128)(2,1)S(1)}, u32[]{:S(2)}, u32[]{:S(2)}) collective-permute-start(bf16[32,64,128]{2,1,0:T(8,128)(2,1)S(1)} %get-tuple-element.20), channel_id=1, source_target_pairs={{0,1},{1,0},{2,3},{3,2},{4,5},{5,4},{6,7},{7,6},{8,9},{9,8},{10,11... | collective-permute-start | bytes 1572872 | tf_op jit(solution)/shard_map/ppermute | solution.py:266
  5.8 26.9 %copy-start = (f32[1,16]{1,0:T(1,128)S(1)}, f32[1,16]{1,0:T(1,128)}, u32[]{:S(2)}) copy-start(f32[1,16]{1,0:T(1,128)} %refs_9_.1) | copy-start | bytes 196
  6.3 9.2 %collective-permute-start.5 = (bf16[16,32,128]{2,1,0:T(8,128)(2,1)S(1)}, bf16[16,32,128]{2,1,0:T(8,128)(2,1)S(1)}, u32[]{:S(2)}, u32[]{:S(2)}) collective-permute-start(bf16[16,32,128]{2,1,0:T(8,128)(2,1)S(1)} %get-tuple-element.25), channel_id=1, source_target_pairs={{0,2},{2,0},{4,8},{6,10},{8,4},{10,6},{12,14},{14,12},{1,3},{3,1},... | collective-permute-start | bytes 393224 | tf_op jit(solution)/shard_map/ppermute | solution.py:453
  9.2 9.8 %collective-permute-start.6 = (bf16[16,32,128]{2,1,0:T(8,128)(2,1)S(1)}, bf16[16,32,128]{2,1,0:T(8,128)(2,1)S(1)}, u32[]{:S(2)}, u32[]{:S(2)}) collective-permute-start(bf16[16,32,128]{2,1,0:T(8,128)(2,1)S(1)} %get-tuple-element.26), channel_id=1, source_target_pairs={{0,4},{2,6},{4,0},{6,2},{8,12},{10,14},{12,8},{14,10},{1,5},{3,7},... | collective-permute-start | bytes 393224 | tf_op jit(solution)/shard_map/ppermute | solution.py:453
  10.9 13.0 %collective-permute-start.7 = (bf16[16,32,128]{2,1,0:T(8,128)(2,1)S(1)}, bf16[16,32,128]{2,1,0:T(8,128)(2,1)S(1)}, u32[]{:S(2)}, u32[]{:S(2)}) collective-permute-start(bf16[16,32,128]{2,1,0:T(8,128)(2,1)S(1)} %get-tuple-element.27), channel_id=1, source_target_pairs={{0,8},{2,10},{4,12},{6,14},{8,0},{10,2},{12,4},{14,6},{1,9},{3,11}... | collective-permute-start | bytes 393224 | tf_op jit(solution)/shard_map/ppermute | solution.py:453
  13.4 19.3 %collective-permute-start.8 = (bf16[16,32,128]{2,1,0:T(8,128)(2,1)S(1)}, bf16[16,32,128]{2,1,0:T(8,128)(2,1)S(1)}, u32[]{:S(2)}, u32[]{:S(2)}) collective-permute-start(bf16[16,32,128]{2,1,0:T(8,128)(2,1)S(1)} %get-tuple-element.28), channel_id=1, source_target_pairs={{0,10},{2,8},{4,14},{6,12},{8,2},{10,0},{12,6},{14,4},{1,11},{3,9}... | collective-permute-start | bytes 393224 | tf_op jit(solution)/shard_map/ppermute | solution.py:453
  15.1 17.6 %collective-permute-start.1 = (bf16[16,32,128]{2,1,0:T(8,128)(2,1)S(1)}, bf16[16,32,128]{2,1,0:T(8,128)(2,1)S(1)}, u32[]{:S(2)}, u32[]{:S(2)}) collective-permute-start(bf16[16,32,128]{2,1,0:T(8,128)(2,1)S(1)} %get-tuple-element.21), channel_id=1, source_target_pairs={{0,6},{2,4},{4,2},{6,0},{8,14},{10,12},{12,10},{14,8},{1,7},{3,5},... | collective-permute-start | bytes 393224 | tf_op jit(solution)/shard_map/ppermute | solution.py:453
  15.5 17.2 %collective-permute-start.2 = (bf16[16,32,128]{2,1,0:T(8,128)(2,1)S(1)}, bf16[16,32,128]{2,1,0:T(8,128)(2,1)S(1)}, u32[]{:S(2)}, u32[]{:S(2)}) collective-permute-start(bf16[16,32,128]{2,1,0:T(8,128)(2,1)S(1)} %get-tuple-element.22), channel_id=1, source_target_pairs={{0,14},{2,12},{4,10},{6,8},{8,6},{10,4},{12,2},{14,0},{1,15},{3,13... | collective-permute-start | bytes 393224 | tf_op jit(solution)/shard_map/ppermute | solution.py:453
  19.1 13.6 %collective-permute-start.3 = (bf16[16,32,128]{2,1,0:T(8,128)(2,1)S(1)}, bf16[16,32,128]{2,1,0:T(8,128)(2,1)S(1)}, u32[]{:S(2)}, u32[]{:S(2)}) collective-permute-start(bf16[16,32,128]{2,1,0:T(8,128)(2,1)S(1)} %get-tuple-element.23), channel_id=1, source_target_pairs={{0,12},{2,14},{4,6},{6,4},{8,10},{10,8},{12,0},{14,2},{1,13},{3,15... | collective-permute-start | bytes 393224 | tf_op jit(solution)/shard_map/ppermute | solution.py:453

commit v6 on v2

--- a/solution.py
+++ b/solution.py
@@ -49,7 +49,7 @@
 
 def slot_masks(slots):
     half = slots // 2
-    between = (2, half, half + 1, 3, slots - 1)
+    between = (2, half + 1, half, 3, slots - 1)
     return (1, *between, slots - 2, 0), (slots - 2, *between, 1, 0)
 
 

time: 34.2 us -> 34.4 us (level)
  no operation moved by 1% of the time
where the time goes in v6:
time: 34.4 us; the launch traced here: 34.2 us
  starting transfers between devices  13.8 us (40%)
  waiting for transfers between devices  12.8 us (37%)
  Pallas kernels  6.89 us (20%)
  between operations  0.69 us (2%)
    ppermute x7, starting transfers between devices, body(): lax.ppermute(parts[slot], 'freq', pairs)  13.2 us
    ppermute x7, waiting for transfers between devices, body(): lax.ppermute(parts[slot], 'freq', pairs)  12.6 us
    pallas_call x1, Pallas kernels, partials(): call(functools.partial(other_kernel, freq_total, slots), 'other', [hbm] *...  3.28 us
    pallas_call x1, Pallas kernels, peaks(): pl.pallas_call(functools.partial(peak_kernel, freq_total, folded, sources...  1.38 us
    pallas_call x1, Pallas kernels, partials(): call(functools.partial(own_kernel, freq_total, slots), 'own', [vmem] * 4,...  1.26 us
  transfers between devices with their start and end apart: 9, of which 3 were waited for; matrix products, arithmetic and copies ran while one was open for 0% of the time, Pallas kernels for 7%

profile of v6, /device:TPU:0, one launch (start us, length us, event | category | flops | bytes accessed | tf_op | source)
XLA Modules:
  0.0 34.2 jit_solution(13554433214146061003)
XLA Ops:
  0.6 3.3 %other.1 = (bf16[32,64,128]{2,1,0:T(8,128)(2,1)S(1)}, bf16[32,64,128]{2,1,0:T(8,128)(2,1)S(1)}, bf16[2,8,128,256]{3,2,1,0:T(8,128)(2,1)S(1)}, f32[2,128]{1,0:T(2...) custom-call(bf16[8,2,2,128,256]{4,3,2,1,0:T(8,128)(2,1)} %bitcast.3, f32[256,256]{1,0:T(8,128)} %refs_1_.1, ...), custom_call_target="tpu_custom_call" | custom-call | flops 1000 | bytes 1000 | tf_op jit(solution)/shard_map/other/pallas_call | solution.py:246
  3.9 0.5 %collective-permute-start.4 = (bf16[32,64,128]{2,1,0:T(8,128)(2,1)S(1)}, bf16[32,64,128]{2,1,0:T(8,128)(2,1)S(1)}, u32[]{:S(2)}, u32[]{:S(2)}) collective-permute-start(bf16[32,64,128]{2,1,0:T(8,128)(2,1)S(1)} %get-tuple-element.24), channel_id=1, source_target_pairs={{0,1},{1,0},{2,3},{3,2},{4,5},{5,4},{6,7},{7,6},{8,9},{9,8},{10,11... | collective-permute-start | bytes 1572872 | tf_op jit(solution)/shard_map/ppermute | solution.py:263
  4.4 0.1 collective-permute-start
  4.5 1.3 %own.1.own_ref = bf16[32,128,128]{2,1,0:T(8,128)(2,1)S(1)} custom-call(bf16[2,8,128,256]{3,2,1,0:T(8,128)(2,1)S(1)} %get-tuple-element.16.refs_0_, f32[128,128]{1,0:T(8,128)S(1)} %get-tuple-element.17.refs_1_, f32[2,128]{1,0:T(2,128)S(1)} %get-tuple-element.18.refs_2_, f32[2,128]{1,0:T(2,128)S(1)} %get-tuple-element.19.refs_3_), custom_call_target="tpu_custom_call" | custom-call | flops 1000 | bytes 1000 | tf_op jit(solution)/shard_map/own/pallas_call | solution.py:265
  5.8 0.0 copy-start
  5.8 0.2 collective-permute-done.4.moved_ref
  6.0 0.3 add_first.1
  6.3 2.9 %collective-permute-start.5 = (bf16[16,32,128]{2,1,0:T(8,128)(2,1)S(1)}, bf16[16,32,128]{2,1,0:T(8,128)(2,1)S(1)}, u32[]{:S(2)}, u32[]{:S(2)}) collective-permute-start(bf16[16,32,128]{2,1,0:T(8,128)(2,1)S(1)} %get-tuple-element.25), channel_id=1, source_target_pairs={{0,2},{2,0},{4,8},{6,10},{8,4},{10,6},{12,14},{14,12},{1,3},{3,1},... | collective-permute-start | bytes 393224 | tf_op jit(solution)/shard_map/ppermute | solution.py:451
  9.2 1.7 %collective-permute-start.6 = (bf16[16,32,128]{2,1,0:T(8,128)(2,1)S(1)}, bf16[16,32,128]{2,1,0:T(8,128)(2,1)S(1)}, u32[]{:S(2)}, u32[]{:S(2)}) collective-permute-start(bf16[16,32,128]{2,1,0:T(8,128)(2,1)S(1)} %get-tuple-element.26), channel_id=1, source_target_pairs={{0,4},{2,6},{4,0},{6,2},{8,12},{10,14},{12,8},{14,10},{1,5},{3,7},... | collective-permute-start | bytes 393224 | tf_op jit(solution)/shard_map/ppermute | solution.py:451
  10.9 2.5 %collective-permute-start.7 = (bf16[16,32,128]{2,1,0:T(8,128)(2,1)S(1)}, bf16[16,32,128]{2,1,0:T(8,128)(2,1)S(1)}, u32[]{:S(2)}, u32[]{:S(2)}) collective-permute-start(bf16[16,32,128]{2,1,0:T(8,128)(2,1)S(1)} %get-tuple-element.27), channel_id=1, source_target_pairs={{0,10},{2,8},{4,14},{6,12},{8,2},{10,0},{12,6},{14,4},{1,11},{3,9}... | collective-permute-start | bytes 393224 | tf_op jit(solution)/shard_map/ppermute | solution.py:451
  13.4 1.4 %collective-permute-start.8 = (bf16[16,32,128]{2,1,0:T(8,128)(2,1)S(1)}, bf16[16,32,128]{2,1,0:T(8,128)(2,1)S(1)}, u32[]{:S(2)}, u32[]{:S(2)}) collective-permute-start(bf16[16,32,128]{2,1,0:T(8,128)(2,1)S(1)} %get-tuple-element.28), channel_id=1, source_target_pairs={{0,8},{2,10},{4,12},{6,14},{8,0},{10,2},{12,4},{14,6},{1,9},{3,11}... | collective-permute-start | bytes 393224 | tf_op jit(solution)/shard_map/ppermute | solution.py:451
  14.8 0.0 collective-permute-done.moved_ref
  14.8 0.3 add_second.1
  15.1 0.4 %collective-permute-start.1 = (bf16[16,32,128]{2,1,0:T(8,128)(2,1)S(1)}, bf16[16,32,128]{2,1,0:T(8,128)(2,1)S(1)}, u32[]{:S(2)}, u32[]{:S(2)}) collective-permute-start(bf16[16,32,128]{2,1,0:T(8,128)(2,1)S(1)} %get-tuple-element.21), channel_id=1, source_target_pairs={{0,6},{2,4},{4,2},{6,0},{8,14},{10,12},{12,10},{14,8},{1,7},{3,5},... | collective-permute-start | bytes 393224 | tf_op jit(solution)/shard_map/ppermute | solution.py:451
  15.5 0.0 collective-permute-done.5.refs_3_
  15.5 3.6 %collective-permute-start.2 = (bf16[16,32,128]{2,1,0:T(8,128)(2,1)S(1)}, bf16[16,32,128]{2,1,0:T(8,128)(2,1)S(1)}, u32[]{:S(2)}, u32[]{:S(2)}) collective-permute-start(bf16[16,32,128]{2,1,0:T(8,128)(2,1)S(1)} %get-tuple-element.22), channel_id=1, source_target_pairs={{0,14},{2,12},{4,10},{6,8},{8,6},{10,4},{12,2},{14,0},{1,15},{3,13... | collective-permute-start | bytes 393224 | tf_op jit(solution)/shard_map/ppermute | solution.py:451
  19.1 0.0 collective-permute-done.6.refs_4_
  19.1 0.8 %collective-permute-start.3 = (bf16[16,32,128]{2,1,0:T(8,128)(2,1)S(1)}, bf16[16,32,128]{2,1,0:T(8,128)(2,1)S(1)}, u32[]{:S(2)}, u32[]{:S(2)}) collective-permute-start(bf16[16,32,128]{2,1,0:T(8,128)(2,1)S(1)} %get-tuple-element.23), channel_id=1, source_target_pairs={{0,12},{2,14},{4,6},{6,4},{8,10},{10,8},{12,0},{14,2},{1,13},{3,15... | collective-permute-start | bytes 393224 | tf_op jit(solution)/shard_map/ppermute | solution.py:451
  19.9 0.3 table.1.refs_8_
  20.2 4.5 %collective-permute-done.7.refs_5_ = bf16[16,32,128]{2,1,0:T(8,128)(2,1)S(1)} collective-permute-done((bf16[16,32,128]{2,1,0:T(8,128)(2,1)S(1)}, bf16[16,32,128]{2,1,0:T(8,128)(2,1)S(1)}, u32[]{:S(2)}, u32[]{:S(2)}) %collective-permute-start.7) | collective-permute-done | bytes 131104 | tf_op jit(solution)/shard_map/ppermute | solution.py:451
  24.7 8.1 %collective-permute-done.8.refs_6_ = bf16[16,32,128]{2,1,0:T(8,128)(2,1)S(1)} collective-permute-done((bf16[16,32,128]{2,1,0:T(8,128)(2,1)S(1)}, bf16[16,32,128]{2,1,0:T(8,128)(2,1)S(1)}, u32[]{:S(2)}, u32[]{:S(2)}) %collective-permute-start.8) | collective-permute-done | bytes 131104 | tf_op jit(solution)/shard_map/ppermute | solution.py:451
  32.8 0.0 collective-permute-done.1.refs_0_
  32.8 0.0 collective-permute-done.2.refs_1_
  32.8 0.0 collective-permute-done.3.refs_2_
  32.8 0.0 copy-done
  32.9 1.4 %peaks.1 = (f32[1,16]{1,0:T(1,128)}, f32[1,16]{1,0:T(1,128)}) custom-call(bf16[16,32,128]{2,1,0:T(8,128)(2,1)S(1)} %collective-permute-done.1.refs_0_, bf16[16,32,128]{2,1,0:T(8,128)(2,1)S(1)} %collective-permute-done.2.refs_1_, bf16[16,32,128]{2,1,0:T(8,128)(2,1)S(1)} %collective-permute-done.3.refs_2_, ...), custom_call_target="tpu_custom_call" | custom-call | tf_op jit(solution)/shard_map/peaks/pallas_call | solution.py:404
Async XLA Ops:
  3.9 2.1 %collective-permute-start.4 = (bf16[32,64,128]{2,1,0:T(8,128)(2,1)S(1)}, bf16[32,64,128]{2,1,0:T(8,128)(2,1)S(1)}, u32[]{:S(2)}, u32[]{:S(2)}) collective-permute-start(bf16[32,64,128]{2,1,0:T(8,128)(2,1)S(1)} %get-tuple-element.24), channel_id=1, source_target_pairs={{0,1},{1,0},{2,3},{3,2},{4,5},{5,4},{6,7},{7,6},{8,9},{9,8},{10,11... | collective-permute-start | bytes 1572872 | tf_op jit(solution)/shard_map/ppermute | solution.py:263
  4.4 10.3 %collective-permute-start = (bf16[32,64,128]{2,1,0:T(8,128)(2,1)S(1)}, bf16[32,64,128]{2,1,0:T(8,128)(2,1)S(1)}, u32[]{:S(2)}, u32[]{:S(2)}) collective-permute-start(bf16[32,64,128]{2,1,0:T(8,128)(2,1)S(1)} %get-tuple-element.20), channel_id=1, source_target_pairs={{0,1},{1,0},{2,3},{3,2},{4,5},{5,4},{6,7},{7,6},{8,9},{9,8},{10,11... | collective-permute-start | bytes 1572872 | tf_op jit(solution)/shard_map/ppermute | solution.py:264
  5.8 27.1 %copy-start = (f32[1,16]{1,0:T(1,128)S(1)}, f32[1,16]{1,0:T(1,128)}, u32[]{:S(2)}) copy-start(f32[1,16]{1,0:T(1,128)} %refs_9_.1) | copy-start | bytes 196
  6.3 9.2 %collective-permute-start.5 = (bf16[16,32,128]{2,1,0:T(8,128)(2,1)S(1)}, bf16[16,32,128]{2,1,0:T(8,128)(2,1)S(1)}, u32[]{:S(2)}, u32[]{:S(2)}) collective-permute-start(bf16[16,32,128]{2,1,0:T(8,128)(2,1)S(1)} %get-tuple-element.25), channel_id=1, source_target_pairs={{0,2},{2,0},{4,8},{6,10},{8,4},{10,6},{12,14},{14,12},{1,3},{3,1},... | collective-permute-start | bytes 393224 | tf_op jit(solution)/shard_map/ppermute | solution.py:451
  9.2 9.8 %collective-permute-start.6 = (bf16[16,32,128]{2,1,0:T(8,128)(2,1)S(1)}, bf16[16,32,128]{2,1,0:T(8,128)(2,1)S(1)}, u32[]{:S(2)}, u32[]{:S(2)}) collective-permute-start(bf16[16,32,128]{2,1,0:T(8,128)(2,1)S(1)} %get-tuple-element.26), channel_id=1, source_target_pairs={{0,4},{2,6},{4,0},{6,2},{8,12},{10,14},{12,8},{14,10},{1,5},{3,7},... | collective-permute-start | bytes 393224 | tf_op jit(solution)/shard_map/ppermute | solution.py:451
  10.9 13.8 %collective-permute-start.7 = (bf16[16,32,128]{2,1,0:T(8,128)(2,1)S(1)}, bf16[16,32,128]{2,1,0:T(8,128)(2,1)S(1)}, u32[]{:S(2)}, u32[]{:S(2)}) collective-permute-start(bf16[16,32,128]{2,1,0:T(8,128)(2,1)S(1)} %get-tuple-element.27), channel_id=1, source_target_pairs={{0,10},{2,8},{4,14},{6,12},{8,2},{10,0},{12,6},{14,4},{1,11},{3,9}... | collective-permute-start | bytes 393224 | tf_op jit(solution)/shard_map/ppermute | solution.py:451
  13.4 19.5 %collective-permute-start.8 = (bf16[16,32,128]{2,1,0:T(8,128)(2,1)S(1)}, bf16[16,32,128]{2,1,0:T(8,128)(2,1)S(1)}, u32[]{:S(2)}, u32[]{:S(2)}) collective-permute-start(bf16[16,32,128]{2,1,0:T(8,128)(2,1)S(1)} %get-tuple-element.28), channel_id=1, source_target_pairs={{0,8},{2,10},{4,12},{6,14},{8,0},{10,2},{12,4},{14,6},{1,9},{3,11}... | collective-permute-start | bytes 393224 | tf_op jit(solution)/shard_map/ppermute | solution.py:451
  15.1 17.7 %collective-permute-start.1 = (bf16[16,32,128]{2,1,0:T(8,128)(2,1)S(1)}, bf16[16,32,128]{2,1,0:T(8,128)(2,1)S(1)}, u32[]{:S(2)}, u32[]{:S(2)}) collective-permute-start(bf16[16,32,128]{2,1,0:T(8,128)(2,1)S(1)} %get-tuple-element.21), channel_id=1, source_target_pairs={{0,6},{2,4},{4,2},{6,0},{8,14},{10,12},{12,10},{14,8},{1,7},{3,5},... | collective-permute-start | bytes 393224 | tf_op jit(solution)/shard_map/ppermute | solution.py:451
  15.5 17.3 %collective-permute-start.2 = (bf16[16,32,128]{2,1,0:T(8,128)(2,1)S(1)}, bf16[16,32,128]{2,1,0:T(8,128)(2,1)S(1)}, u32[]{:S(2)}, u32[]{:S(2)}) collective-permute-start(bf16[16,32,128]{2,1,0:T(8,128)(2,1)S(1)} %get-tuple-element.22), channel_id=1, source_target_pairs={{0,14},{2,12},{4,10},{6,8},{8,6},{10,4},{12,2},{14,0},{1,15},{3,13... | collective-permute-start | bytes 393224 | tf_op jit(solution)/shard_map/ppermute | solution.py:451
  19.1 13.8 %collective-permute-start.3 = (bf16[16,32,128]{2,1,0:T(8,128)(2,1)S(1)}, bf16[16,32,128]{2,1,0:T(8,128)(2,1)S(1)}, u32[]{:S(2)}, u32[]{:S(2)}) collective-permute-start(bf16[16,32,128]{2,1,0:T(8,128)(2,1)S(1)} %get-tuple-element.23), channel_id=1, source_target_pairs={{0,12},{2,14},{4,6},{6,4},{8,10},{10,8},{12,0},{14,2},{1,13},{3,15... | collective-permute-start | bytes 393224 | tf_op jit(solution)/shard_map/ppermute | solution.py:451

commit v7 on v6

--- a/solution.py
+++ b/solution.py
@@ -49,7 +49,7 @@
 
 def slot_masks(slots):
     half = slots // 2
-    between = (2, half + 1, half, 3, slots - 1)
+    between = (2, half + 1, slots - 1, 3, half)
     return (1, *between, slots - 2, 0), (slots - 2, *between, 1, 0)
 
 

time: 34.4 us -> 36.1 us (1.049)
  waiting for transfers between devices: 12.8 us -> 14.6 us
    ppermute x7, waiting for transfers between devices: 12.6 us -> 14.4 us  [body(): lax.ppermute(parts[slot], 'freq', pairs)]
  transfers between devices with their start and end apart: 9 -> 9, of which waited for: 3 -> 3; matrix products, arithmetic and copies ran while one was open for 0% -> 0% of each run, Pallas kernels for 7% -> 6%
where the time goes in v7:
time: 36.1 us; the launch traced here: 36 us
  waiting for transfers between devices  14.6 us (40%)
  starting transfers between devices  13.8 us (38%)
  Pallas kernels  6.89 us (19%)
  between operations  0.67 us (2%)
    ppermute x7, waiting for transfers between devices, body(): lax.ppermute(parts[slot], 'freq', pairs)  14.4 us
    ppermute x7, starting transfers between devices, body(): lax.ppermute(parts[slot], 'freq', pairs)  13.2 us
    pallas_call x1, Pallas kernels, partials(): call(functools.partial(other_kernel, freq_total, slots), 'other', [hbm] *...  3.28 us
    pallas_call x1, Pallas kernels, peaks(): pl.pallas_call(functools.partial(peak_kernel, freq_total, folded, sources...  1.37 us
    pallas_call x1, Pallas kernels, partials(): call(functools.partial(own_kernel, freq_total, slots), 'own', [vmem] * 4,...  1.26 us
  transfers between devices with their start and end apart: 9, of which 3 were waited for; matrix products, arithmetic and copies ran while one was open for 0% of the time, Pallas kernels for 6%

profile of v7, /device:TPU:0, one launch (start us, length us, event | category | flops | bytes accessed | tf_op | source)
XLA Modules:
  0.0 36.0 jit_solution(14940972101489838069)
XLA Ops:
  0.6 3.3 %other.1 = (bf16[32,64,128]{2,1,0:T(8,128)(2,1)S(1)}, bf16[32,64,128]{2,1,0:T(8,128)(2,1)S(1)}, bf16[2,8,128,256]{3,2,1,0:T(8,128)(2,1)S(1)}, f32[2,128]{1,0:T(2...) custom-call(bf16[8,2,2,128,256]{4,3,2,1,0:T(8,128)(2,1)} %bitcast.3, f32[256,256]{1,0:T(8,128)} %refs_1_.1, ...), custom_call_target="tpu_custom_call" | custom-call | flops 1000 | bytes 1000 | tf_op jit(solution)/shard_map/other/pallas_call | solution.py:246
  3.9 0.5 %collective-permute-start.4 = (bf16[32,64,128]{2,1,0:T(8,128)(2,1)S(1)}, bf16[32,64,128]{2,1,0:T(8,128)(2,1)S(1)}, u32[]{:S(2)}, u32[]{:S(2)}) collective-permute-start(bf16[32,64,128]{2,1,0:T(8,128)(2,1)S(1)} %get-tuple-element.24), channel_id=1, source_target_pairs={{0,1},{1,0},{2,3},{3,2},{4,5},{5,4},{6,7},{7,6},{8,9},{9,8},{10,11... | collective-permute-start | bytes 1572872 | tf_op jit(solution)/shard_map/ppermute | solution.py:263
  4.4 0.1 collective-permute-start
  4.5 1.3 %own.1.own_ref = bf16[32,128,128]{2,1,0:T(8,128)(2,1)S(1)} custom-call(bf16[2,8,128,256]{3,2,1,0:T(8,128)(2,1)S(1)} %get-tuple-element.16.refs_0_, f32[128,128]{1,0:T(8,128)S(1)} %get-tuple-element.17.refs_1_, f32[2,128]{1,0:T(2,128)S(1)} %get-tuple-element.18.refs_2_, f32[2,128]{1,0:T(2,128)S(1)} %get-tuple-element.19.refs_3_), custom_call_target="tpu_custom_call" | custom-call | flops 1000 | bytes 1000 | tf_op jit(solution)/shard_map/own/pallas_call | solution.py:265
  5.8 0.0 copy-start
  5.8 0.2 collective-permute-done.4.moved_ref
  6.0 0.3 add_first.1
  6.3 2.9 %collective-permute-start.5 = (bf16[16,32,128]{2,1,0:T(8,128)(2,1)S(1)}, bf16[16,32,128]{2,1,0:T(8,128)(2,1)S(1)}, u32[]{:S(2)}, u32[]{:S(2)}) collective-permute-start(bf16[16,32,128]{2,1,0:T(8,128)(2,1)S(1)} %get-tuple-element.25), channel_id=1, source_target_pairs={{0,2},{2,0},{4,8},{6,10},{8,4},{10,6},{12,14},{14,12},{1,3},{3,1},... | collective-permute-start | bytes 393224 | tf_op jit(solution)/shard_map/ppermute | solution.py:451
  9.2 1.7 %collective-permute-start.6 = (bf16[16,32,128]{2,1,0:T(8,128)(2,1)S(1)}, bf16[16,32,128]{2,1,0:T(8,128)(2,1)S(1)}, u32[]{:S(2)}, u32[]{:S(2)}) collective-permute-start(bf16[16,32,128]{2,1,0:T(8,128)(2,1)S(1)} %get-tuple-element.26), channel_id=1, source_target_pairs={{0,4},{2,6},{4,0},{6,2},{8,12},{10,14},{12,8},{14,10},{1,5},{3,7},... | collective-permute-start | bytes 393224 | tf_op jit(solution)/shard_map/ppermute | solution.py:451
  10.9 2.5 %collective-permute-start.7 = (bf16[16,32,128]{2,1,0:T(8,128)(2,1)S(1)}, bf16[16,32,128]{2,1,0:T(8,128)(2,1)S(1)}, u32[]{:S(2)}, u32[]{:S(2)}) collective-permute-start(bf16[16,32,128]{2,1,0:T(8,128)(2,1)S(1)} %get-tuple-element.27), channel_id=1, source_target_pairs={{0,10},{2,8},{4,14},{6,12},{8,2},{10,0},{12,6},{14,4},{1,11},{3,9}... | collective-permute-start | bytes 393224 | tf_op jit(solution)/shard_map/ppermute | solution.py:451
  13.4 1.1 %collective-permute-start.8 = (bf16[16,32,128]{2,1,0:T(8,128)(2,1)S(1)}, bf16[16,32,128]{2,1,0:T(8,128)(2,1)S(1)}, u32[]{:S(2)}, u32[]{:S(2)}) collective-permute-start(bf16[16,32,128]{2,1,0:T(8,128)(2,1)S(1)} %get-tuple-element.28), channel_id=1, source_target_pairs={{0,14},{2,12},{4,10},{6,8},{8,6},{10,4},{12,2},{14,0},{1,15},{3,13... | collective-permute-start | bytes 393224 | tf_op jit(solution)/shard_map/ppermute | solution.py:451
  14.5 0.0 collective-permute-done.moved_ref
  14.5 0.3 add_second.1
  14.9 1.8 %collective-permute-start.1 = (bf16[16,32,128]{2,1,0:T(8,128)(2,1)S(1)}, bf16[16,32,128]{2,1,0:T(8,128)(2,1)S(1)}, u32[]{:S(2)}, u32[]{:S(2)}) collective-permute-start(bf16[16,32,128]{2,1,0:T(8,128)(2,1)S(1)} %get-tuple-element.21), channel_id=1, source_target_pairs={{0,6},{2,4},{4,2},{6,0},{8,14},{10,12},{12,10},{14,8},{1,7},{3,5},... | collective-permute-start | bytes 393224 | tf_op jit(solution)/shard_map/ppermute | solution.py:451
  16.6 0.0 collective-permute-done.5.refs_3_
  16.6 2.4 %collective-permute-start.2 = (bf16[16,32,128]{2,1,0:T(8,128)(2,1)S(1)}, bf16[16,32,128]{2,1,0:T(8,128)(2,1)S(1)}, u32[]{:S(2)}, u32[]{:S(2)}) collective-permute-start(bf16[16,32,128]{2,1,0:T(8,128)(2,1)S(1)} %get-tuple-element.22), channel_id=1, source_target_pairs={{0,8},{2,10},{4,12},{6,14},{8,0},{10,2},{12,4},{14,6},{1,9},{3,11}... | collective-permute-start | bytes 393224 | tf_op jit(solution)/shard_map/ppermute | solution.py:451
  19.1 0.0 collective-permute-done.6.refs_4_
  19.1 0.8 %collective-permute-start.3 = (bf16[16,32,128]{2,1,0:T(8,128)(2,1)S(1)}, bf16[16,32,128]{2,1,0:T(8,128)(2,1)S(1)}, u32[]{:S(2)}, u32[]{:S(2)}) collective-permute-start(bf16[16,32,128]{2,1,0:T(8,128)(2,1)S(1)} %get-tuple-element.23), channel_id=1, source_target_pairs={{0,12},{2,14},{4,6},{6,4},{8,10},{10,8},{12,0},{14,2},{1,13},{3,15... | collective-permute-start | bytes 393224 | tf_op jit(solution)/shard_map/ppermute | solution.py:451
  19.9 0.3 table.1.refs_8_
  20.2 4.6 %collective-permute-done.7.refs_5_ = bf16[16,32,128]{2,1,0:T(8,128)(2,1)S(1)} collective-permute-done((bf16[16,32,128]{2,1,0:T(8,128)(2,1)S(1)}, bf16[16,32,128]{2,1,0:T(8,128)(2,1)S(1)}, u32[]{:S(2)}, u32[]{:S(2)}) %collective-permute-start.7) | collective-permute-done | bytes 131104 | tf_op jit(solution)/shard_map/ppermute | solution.py:451
  24.8 0.0 collective-permute-done.8.refs_6_
  24.8 0.0 collective-permute-done.1.refs_0_
  24.8 9.8 %collective-permute-done.2.refs_1_ = bf16[16,32,128]{2,1,0:T(8,128)(2,1)S(1)} collective-permute-done((bf16[16,32,128]{2,1,0:T(8,128)(2,1)S(1)}, bf16[16,32,128]{2,1,0:T(8,128)(2,1)S(1)}, u32[]{:S(2)}, u32[]{:S(2)}) %collective-permute-start.2) | collective-permute-done | bytes 131104 | tf_op jit(solution)/shard_map/ppermute | solution.py:451
  34.6 0.0 collective-permute-done.3.refs_2_
  34.6 0.0 copy-done
  34.6 1.4 %peaks.1 = (f32[1,16]{1,0:T(1,128)}, f32[1,16]{1,0:T(1,128)}) custom-call(bf16[16,32,128]{2,1,0:T(8,128)(2,1)S(1)} %collective-permute-done.1.refs_0_, bf16[16,32,128]{2,1,0:T(8,128)(2,1)S(1)} %collective-permute-done.2.refs_1_, bf16[16,32,128]{2,1,0:T(8,128)(2,1)S(1)} %collective-permute-done.3.refs_2_, ...), custom_call_target="tpu_custom_call" | custom-call | tf_op jit(solution)/shard_map/peaks/pallas_call | solution.py:404
Async XLA Ops:
  3.9 2.1 %collective-permute-start.4 = (bf16[32,64,128]{2,1,0:T(8,128)(2,1)S(1)}, bf16[32,64,128]{2,1,0:T(8,128)(2,1)S(1)}, u32[]{:S(2)}, u32[]{:S(2)}) collective-permute-start(bf16[32,64,128]{2,1,0:T(8,128)(2,1)S(1)} %get-tuple-element.24), channel_id=1, source_target_pairs={{0,1},{1,0},{2,3},{3,2},{4,5},{5,4},{6,7},{7,6},{8,9},{9,8},{10,11... | collective-permute-start | bytes 1572872 | tf_op jit(solution)/shard_map/ppermute | solution.py:263
  4.4 10.1 %collective-permute-start = (bf16[32,64,128]{2,1,0:T(8,128)(2,1)S(1)}, bf16[32,64,128]{2,1,0:T(8,128)(2,1)S(1)}, u32[]{:S(2)}, u32[]{:S(2)}) collective-permute-start(bf16[32,64,128]{2,1,0:T(8,128)(2,1)S(1)} %get-tuple-element.20), channel_id=1, source_target_pairs={{0,1},{1,0},{2,3},{3,2},{4,5},{5,4},{6,7},{7,6},{8,9},{9,8},{10,11... | collective-permute-start | bytes 1572872 | tf_op jit(solution)/shard_map/ppermute | solution.py:264
  5.8 28.8 %copy-start = (f32[1,16]{1,0:T(1,128)S(1)}, f32[1,16]{1,0:T(1,128)}, u32[]{:S(2)}) copy-start(f32[1,16]{1,0:T(1,128)} %refs_9_.1) | copy-start | bytes 196
  6.3 10.3 %collective-permute-start.5 = (bf16[16,32,128]{2,1,0:T(8,128)(2,1)S(1)}, bf16[16,32,128]{2,1,0:T(8,128)(2,1)S(1)}, u32[]{:S(2)}, u32[]{:S(2)}) collective-permute-start(bf16[16,32,128]{2,1,0:T(8,128)(2,1)S(1)} %get-tuple-element.25), channel_id=1, source_target_pairs={{0,2},{2,0},{4,8},{6,10},{8,4},{10,6},{12,14},{14,12},{1,3},{3,1},... | collective-permute-start | bytes 393224 | tf_op jit(solution)/shard_map/ppermute | solution.py:451
  9.2 9.8 %collective-permute-start.6 = (bf16[16,32,128]{2,1,0:T(8,128)(2,1)S(1)}, bf16[16,32,128]{2,1,0:T(8,128)(2,1)S(1)}, u32[]{:S(2)}, u32[]{:S(2)}) collective-permute-start(bf16[16,32,128]{2,1,0:T(8,128)(2,1)S(1)} %get-tuple-element.26), channel_id=1, source_target_pairs={{0,4},{2,6},{4,0},{6,2},{8,12},{10,14},{12,8},{14,10},{1,5},{3,7},... | collective-permute-start | bytes 393224 | tf_op jit(solution)/shard_map/ppermute | solution.py:451
  10.9 13.9 %collective-permute-start.7 = (bf16[16,32,128]{2,1,0:T(8,128)(2,1)S(1)}, bf16[16,32,128]{2,1,0:T(8,128)(2,1)S(1)}, u32[]{:S(2)}, u32[]{:S(2)}) collective-permute-start(bf16[16,32,128]{2,1,0:T(8,128)(2,1)S(1)} %get-tuple-element.27), channel_id=1, source_target_pairs={{0,10},{2,8},{4,14},{6,12},{8,2},{10,0},{12,6},{14,4},{1,11},{3,9}... | collective-permute-start | bytes 393224 | tf_op jit(solution)/shard_map/ppermute | solution.py:451
  13.4 11.5 %collective-permute-start.8 = (bf16[16,32,128]{2,1,0:T(8,128)(2,1)S(1)}, bf16[16,32,128]{2,1,0:T(8,128)(2,1)S(1)}, u32[]{:S(2)}, u32[]{:S(2)}) collective-permute-start(bf16[16,32,128]{2,1,0:T(8,128)(2,1)S(1)} %get-tuple-element.28), channel_id=1, source_target_pairs={{0,14},{2,12},{4,10},{6,8},{8,6},{10,4},{12,2},{14,0},{1,15},{3,13... | collective-permute-start | bytes 393224 | tf_op jit(solution)/shard_map/ppermute | solution.py:451
  14.9 10.0 %collective-permute-start.1 = (bf16[16,32,128]{2,1,0:T(8,128)(2,1)S(1)}, bf16[16,32,128]{2,1,0:T(8,128)(2,1)S(1)}, u32[]{:S(2)}, u32[]{:S(2)}) collective-permute-start(bf16[16,32,128]{2,1,0:T(8,128)(2,1)S(1)} %get-tuple-element.21), channel_id=1, source_target_pairs={{0,6},{2,4},{4,2},{6,0},{8,14},{10,12},{12,10},{14,8},{1,7},{3,5},... | collective-permute-start | bytes 393224 | tf_op jit(solution)/shard_map/ppermute | solution.py:451
  16.6 18.0 %collective-permute-start.2 = (bf16[16,32,128]{2,1,0:T(8,128)(2,1)S(1)}, bf16[16,32,128]{2,1,0:T(8,128)(2,1)S(1)}, u32[]{:S(2)}, u32[]{:S(2)}) collective-permute-start(bf16[16,32,128]{2,1,0:T(8,128)(2,1)S(1)} %get-tuple-element.22), channel_id=1, source_target_pairs={{0,8},{2,10},{4,12},{6,14},{8,0},{10,2},{12,4},{14,6},{1,9},{3,11}... | collective-permute-start | bytes 393224 | tf_op jit(solution)/shard_map/ppermute | solution.py:451
  19.1 15.5 %collective-permute-start.3 = (bf16[16,32,128]{2,1,0:T(8,128)(2,1)S(1)}, bf16[16,32,128]{2,1,0:T(8,128)(2,1)S(1)}, u32[]{:S(2)}, u32[]{:S(2)}) collective-permute-start(bf16[16,32,128]{2,1,0:T(8,128)(2,1)S(1)} %get-tuple-element.23), channel_id=1, source_target_pairs={{0,12},{2,14},{4,6},{6,4},{8,10},{10,8},{12,0},{14,2},{1,13},{3,15... | collective-permute-start | bytes 393224 | tf_op jit(solution)/shard_map/ppermute | solution.py:451

commit v8 on v7

--- a/solution.py
+++ b/solution.py
@@ -50,7 +50,7 @@
 def slot_masks(slots):
     half = slots // 2
     between = (2, half + 1, slots - 1, 3, half)
-    return (1, *between, slots - 2, 0), (slots - 2, *between, 1, 0)
+    return (slots - 2, *between, 1, 0), (1, *between, slots - 2, 0)
 
 
 def partner(slots, slot):

time: 36.1 us -> 35.7 us (0.989); the launches traced: 36 us -> 35 us
  waiting for transfers between devices: 14.6 us -> 12.3 us
  starting transfers between devices: 13.8 us -> 15.2 us
    ppermute x7, waiting for transfers between devices: 14.4 us -> 12.1 us  [body(): lax.ppermute(parts[slot], 'freq', pairs)]
    ppermute x7, starting transfers between devices: 13.2 us -> 14.6 us  [body(): lax.ppermute(parts[slot], 'freq', pairs)]
  transfers between devices with their start and end apart: 9 -> 9, of which waited for: 3 -> 6; matrix products, arithmetic and copies ran while one was open for 0% -> 0% of each run, Pallas kernels for 6% -> 6%
where the time goes in v8:
time: 35.7 us; the launch traced here: 35 us
  starting transfers between devices  15.2 us (43%)
  waiting for transfers between devices  12.3 us (34%)
  Pallas kernels  6.89 us (19%)
  between operations  0.67 us (2%)
    ppermute x7, starting transfers between devices, body(): lax.ppermute(parts[slot], 'freq', pairs)  14.6 us
    ppermute x7, waiting for transfers between devices, body(): lax.ppermute(parts[slot], 'freq', pairs)  12.1 us
    pallas_call x1, Pallas kernels, partials(): call(functools.partial(other_kernel, freq_total, slots), 'other', [hbm] *...  3.28 us
    pallas_call x1, Pallas kernels, peaks(): pl.pallas_call(functools.partial(peak_kernel, freq_total, folded, sources...  1.37 us
    pallas_call x1, Pallas kernels, partials(): call(functools.partial(own_kernel, freq_total, slots), 'own', [vmem] * 4,...  1.26 us
  transfers between devices with their start and end apart: 9, of which 6 were waited for; matrix products, arithmetic and copies ran while one was open for 0% of the time, Pallas kernels for 6%

profile of v8, /device:TPU:0, one launch (start us, length us, event | category | flops | bytes accessed | tf_op | source)
XLA Modules:
  0.0 35.0 jit_solution(11475842733972337239)
XLA Ops:
  0.6 3.3 %other.1 = (bf16[32,64,128]{2,1,0:T(8,128)(2,1)S(1)}, bf16[32,64,128]{2,1,0:T(8,128)(2,1)S(1)}, bf16[2,8,128,256]{3,2,1,0:T(8,128)(2,1)S(1)}, f32[2,128]{1,0:T(2...) custom-call(bf16[8,2,2,128,256]{4,3,2,1,0:T(8,128)(2,1)} %bitcast.3, f32[256,256]{1,0:T(8,128)} %refs_1_.1, ...), custom_call_target="tpu_custom_call" | custom-call | flops 1000 | bytes 1000 | tf_op jit(solution)/shard_map/other/pallas_call | solution.py:246
  3.9 0.5 %collective-permute-start.4 = (bf16[32,64,128]{2,1,0:T(8,128)(2,1)S(1)}, bf16[32,64,128]{2,1,0:T(8,128)(2,1)S(1)}, u32[]{:S(2)}, u32[]{:S(2)}) collective-permute-start(bf16[32,64,128]{2,1,0:T(8,128)(2,1)S(1)} %get-tuple-element.24), channel_id=1, source_target_pairs={{0,1},{1,0},{2,3},{3,2},{4,5},{5,4},{6,7},{7,6},{8,9},{9,8},{10,11... | collective-permute-start | bytes 1572872 | tf_op jit(solution)/shard_map/ppermute | solution.py:263
  4.4 0.1 collective-permute-start
  4.5 1.3 %own.1.own_ref = bf16[32,128,128]{2,1,0:T(8,128)(2,1)S(1)} custom-call(bf16[2,8,128,256]{3,2,1,0:T(8,128)(2,1)S(1)} %get-tuple-element.16.refs_0_, f32[128,128]{1,0:T(8,128)S(1)} %get-tuple-element.17.refs_1_, f32[2,128]{1,0:T(2,128)S(1)} %get-tuple-element.18.refs_2_, f32[2,128]{1,0:T(2,128)S(1)} %get-tuple-element.19.refs_3_), custom_call_target="tpu_custom_call" | custom-call | flops 1000 | bytes 1000 | tf_op jit(solution)/shard_map/own/pallas_call | solution.py:265
  5.8 0.0 copy-start
  5.8 0.2 collective-permute-done.4.moved_ref
  6.0 0.3 add_first.1
  6.3 5.0 %collective-permute-start.5 = (bf16[16,32,128]{2,1,0:T(8,128)(2,1)S(1)}, bf16[16,32,128]{2,1,0:T(8,128)(2,1)S(1)}, u32[]{:S(2)}, u32[]{:S(2)}) collective-permute-start(bf16[16,32,128]{2,1,0:T(8,128)(2,1)S(1)} %get-tuple-element.25), channel_id=1, source_target_pairs={{0,12},{2,14},{4,6},{6,4},{8,10},{10,8},{12,0},{14,2},{1,13},{3,15... | collective-permute-start | bytes 393224 | tf_op jit(solution)/shard_map/ppermute | solution.py:451
  11.3 0.0 collective-permute-start.6
  11.3 1.7 %collective-permute-start.7 = (bf16[16,32,128]{2,1,0:T(8,128)(2,1)S(1)}, bf16[16,32,128]{2,1,0:T(8,128)(2,1)S(1)}, u32[]{:S(2)}, u32[]{:S(2)}) collective-permute-start(bf16[16,32,128]{2,1,0:T(8,128)(2,1)S(1)} %get-tuple-element.27), channel_id=1, source_target_pairs={{0,10},{2,8},{4,14},{6,12},{8,2},{10,0},{12,6},{14,4},{1,11},{3,9}... | collective-permute-start | bytes 393224 | tf_op jit(solution)/shard_map/ppermute | solution.py:451
  13.1 3.6 %collective-permute-start.8 = (bf16[16,32,128]{2,1,0:T(8,128)(2,1)S(1)}, bf16[16,32,128]{2,1,0:T(8,128)(2,1)S(1)}, u32[]{:S(2)}, u32[]{:S(2)}) collective-permute-start(bf16[16,32,128]{2,1,0:T(8,128)(2,1)S(1)} %get-tuple-element.28), channel_id=1, source_target_pairs={{0,14},{2,12},{4,10},{6,8},{8,6},{10,4},{12,2},{14,0},{1,15},{3,13... | collective-permute-start | bytes 393224 | tf_op jit(solution)/shard_map/ppermute | solution.py:451
  16.6 0.0 collective-permute-done.moved_ref
  16.6 0.3 add_second.1
  17.0 0.1 collective-permute-start.1
  17.1 0.0 collective-permute-done.5.refs_3_
  17.1 1.7 %collective-permute-start.2 = (bf16[16,32,128]{2,1,0:T(8,128)(2,1)S(1)}, bf16[16,32,128]{2,1,0:T(8,128)(2,1)S(1)}, u32[]{:S(2)}, u32[]{:S(2)}) collective-permute-start(bf16[16,32,128]{2,1,0:T(8,128)(2,1)S(1)} %get-tuple-element.22), channel_id=1, source_target_pairs={{0,8},{2,10},{4,12},{6,14},{8,0},{10,2},{12,4},{14,6},{1,9},{3,11}... | collective-permute-start | bytes 393224 | tf_op jit(solution)/shard_map/ppermute | solution.py:451
  18.8 1.4 %collective-permute-done.6.refs_4_ = bf16[16,32,128]{2,1,0:T(8,128)(2,1)S(1)} collective-permute-done((bf16[16,32,128]{2,1,0:T(8,128)(2,1)S(1)}, bf16[16,32,128]{2,1,0:T(8,128)(2,1)S(1)}, u32[]{:S(2)}, u32[]{:S(2)}) %collective-permute-start.6) | collective-permute-done | bytes 131104 | tf_op jit(solution)/shard_map/ppermute | solution.py:451
  20.1 2.5 %collective-permute-start.3 = (bf16[16,32,128]{2,1,0:T(8,128)(2,1)S(1)}, bf16[16,32,128]{2,1,0:T(8,128)(2,1)S(1)}, u32[]{:S(2)}, u32[]{:S(2)}) collective-permute-start(bf16[16,32,128]{2,1,0:T(8,128)(2,1)S(1)} %get-tuple-element.23), channel_id=1, source_target_pairs={{0,2},{2,0},{4,8},{6,10},{8,4},{10,6},{12,14},{14,12},{1,3},{3,1},... | collective-permute-start | bytes 393224 | tf_op jit(solution)/shard_map/ppermute | solution.py:451
  22.6 0.3 table.1.refs_8_
  22.9 2.3 %collective-permute-done.7.refs_5_ = bf16[16,32,128]{2,1,0:T(8,128)(2,1)S(1)} collective-permute-done((bf16[16,32,128]{2,1,0:T(8,128)(2,1)S(1)}, bf16[16,32,128]{2,1,0:T(8,128)(2,1)S(1)}, u32[]{:S(2)}, u32[]{:S(2)}) %collective-permute-start.7) | collective-permute-done | bytes 131104 | tf_op jit(solution)/shard_map/ppermute | solution.py:451
  25.2 0.1 collective-permute-done.8.refs_6_
  25.3 2.1 %collective-permute-done.1.refs_0_ = bf16[16,32,128]{2,1,0:T(8,128)(2,1)S(1)} collective-permute-done((bf16[16,32,128]{2,1,0:T(8,128)(2,1)S(1)}, bf16[16,32,128]{2,1,0:T(8,128)(2,1)S(1)}, u32[]{:S(2)}, u32[]{:S(2)}) %collective-permute-start.1) | collective-permute-done | bytes 131104 | tf_op jit(solution)/shard_map/ppermute | solution.py:451
  27.4 6.2 %collective-permute-done.2.refs_1_ = bf16[16,32,128]{2,1,0:T(8,128)(2,1)S(1)} collective-permute-done((bf16[16,32,128]{2,1,0:T(8,128)(2,1)S(1)}, bf16[16,32,128]{2,1,0:T(8,128)(2,1)S(1)}, u32[]{:S(2)}, u32[]{:S(2)}) %collective-permute-start.2) | collective-permute-done | bytes 131104 | tf_op jit(solution)/shard_map/ppermute | solution.py:451
  33.7 0.0 collective-permute-done.3.refs_2_
  33.7 0.0 copy-done
  33.7 1.4 %peaks.1 = (f32[1,16]{1,0:T(1,128)}, f32[1,16]{1,0:T(1,128)}) custom-call(bf16[16,32,128]{2,1,0:T(8,128)(2,1)S(1)} %collective-permute-done.1.refs_0_, bf16[16,32,128]{2,1,0:T(8,128)(2,1)S(1)} %collective-permute-done.2.refs_1_, bf16[16,32,128]{2,1,0:T(8,128)(2,1)S(1)} %collective-permute-done.3.refs_2_, ...), custom_call_target="tpu_custom_call" | custom-call | tf_op jit(solution)/shard_map/peaks/pallas_call | solution.py:404
Async XLA Ops:
  3.9 2.1 %collective-permute-start.4 = (bf16[32,64,128]{2,1,0:T(8,128)(2,1)S(1)}, bf16[32,64,128]{2,1,0:T(8,128)(2,1)S(1)}, u32[]{:S(2)}, u32[]{:S(2)}) collective-permute-start(bf16[32,64,128]{2,1,0:T(8,128)(2,1)S(1)} %get-tuple-element.24), channel_id=1, source_target_pairs={{0,1},{1,0},{2,3},{3,2},{4,5},{5,4},{6,7},{7,6},{8,9},{9,8},{10,11... | collective-permute-start | bytes 1572872 | tf_op jit(solution)/shard_map/ppermute | solution.py:263
  4.4 12.2 %collective-permute-start = (bf16[32,64,128]{2,1,0:T(8,128)(2,1)S(1)}, bf16[32,64,128]{2,1,0:T(8,128)(2,1)S(1)}, u32[]{:S(2)}, u32[]{:S(2)}) collective-permute-start(bf16[32,64,128]{2,1,0:T(8,128)(2,1)S(1)} %get-tuple-element.20), channel_id=1, source_target_pairs={{0,1},{1,0},{2,3},{3,2},{4,5},{5,4},{6,7},{7,6},{8,9},{9,8},{10,11... | collective-permute-start | bytes 1572872 | tf_op jit(solution)/shard_map/ppermute | solution.py:264
  5.8 27.9 %copy-start = (f32[1,16]{1,0:T(1,128)S(1)}, f32[1,16]{1,0:T(1,128)}, u32[]{:S(2)}) copy-start(f32[1,16]{1,0:T(1,128)} %refs_9_.1) | copy-start | bytes 196
  6.3 10.8 %collective-permute-start.5 = (bf16[16,32,128]{2,1,0:T(8,128)(2,1)S(1)}, bf16[16,32,128]{2,1,0:T(8,128)(2,1)S(1)}, u32[]{:S(2)}, u32[]{:S(2)}) collective-permute-start(bf16[16,32,128]{2,1,0:T(8,128)(2,1)S(1)} %get-tuple-element.25), channel_id=1, source_target_pairs={{0,12},{2,14},{4,6},{6,4},{8,10},{10,8},{12,0},{14,2},{1,13},{3,15... | collective-permute-start | bytes 393224 | tf_op jit(solution)/shard_map/ppermute | solution.py:451
  11.3 8.8 %collective-permute-start.6 = (bf16[16,32,128]{2,1,0:T(8,128)(2,1)S(1)}, bf16[16,32,128]{2,1,0:T(8,128)(2,1)S(1)}, u32[]{:S(2)}, u32[]{:S(2)}) collective-permute-start(bf16[16,32,128]{2,1,0:T(8,128)(2,1)S(1)} %get-tuple-element.26), channel_id=1, source_target_pairs={{0,4},{2,6},{4,0},{6,2},{8,12},{10,14},{12,8},{14,10},{1,5},{3,7},... | collective-permute-start | bytes 393224 | tf_op jit(solution)/shard_map/ppermute | solution.py:451
  11.3 13.9 %collective-permute-start.7 = (bf16[16,32,128]{2,1,0:T(8,128)(2,1)S(1)}, bf16[16,32,128]{2,1,0:T(8,128)(2,1)S(1)}, u32[]{:S(2)}, u32[]{:S(2)}) collective-permute-start(bf16[16,32,128]{2,1,0:T(8,128)(2,1)S(1)} %get-tuple-element.27), channel_id=1, source_target_pairs={{0,10},{2,8},{4,14},{6,12},{8,2},{10,0},{12,6},{14,4},{1,11},{3,9}... | collective-permute-start | bytes 393224 | tf_op jit(solution)/shard_map/ppermute | solution.py:451
  13.1 12.3 %collective-permute-start.8 = (bf16[16,32,128]{2,1,0:T(8,128)(2,1)S(1)}, bf16[16,32,128]{2,1,0:T(8,128)(2,1)S(1)}, u32[]{:S(2)}, u32[]{:S(2)}) collective-permute-start(bf16[16,32,128]{2,1,0:T(8,128)(2,1)S(1)} %get-tuple-element.28), channel_id=1, source_target_pairs={{0,14},{2,12},{4,10},{6,8},{8,6},{10,4},{12,2},{14,0},{1,15},{3,13... | collective-permute-start | bytes 393224 | tf_op jit(solution)/shard_map/ppermute | solution.py:451
  17.0 10.4 %collective-permute-start.1 = (bf16[16,32,128]{2,1,0:T(8,128)(2,1)S(1)}, bf16[16,32,128]{2,1,0:T(8,128)(2,1)S(1)}, u32[]{:S(2)}, u32[]{:S(2)}) collective-permute-start(bf16[16,32,128]{2,1,0:T(8,128)(2,1)S(1)} %get-tuple-element.21), channel_id=1, source_target_pairs={{0,6},{2,4},{4,2},{6,0},{8,14},{10,12},{12,10},{14,8},{1,7},{3,5},... | collective-permute-start | bytes 393224 | tf_op jit(solution)/shard_map/ppermute | solution.py:451
  17.1 16.6 %collective-permute-start.2 = (bf16[16,32,128]{2,1,0:T(8,128)(2,1)S(1)}, bf16[16,32,128]{2,1,0:T(8,128)(2,1)S(1)}, u32[]{:S(2)}, u32[]{:S(2)}) collective-permute-start(bf16[16,32,128]{2,1,0:T(8,128)(2,1)S(1)} %get-tuple-element.22), channel_id=1, source_target_pairs={{0,8},{2,10},{4,12},{6,14},{8,0},{10,2},{12,4},{14,6},{1,9},{3,11}... | collective-permute-start | bytes 393224 | tf_op jit(solution)/shard_map/ppermute | solution.py:451
  20.1 13.5 %collective-permute-start.3 = (bf16[16,32,128]{2,1,0:T(8,128)(2,1)S(1)}, bf16[16,32,128]{2,1,0:T(8,128)(2,1)S(1)}, u32[]{:S(2)}, u32[]{:S(2)}) collective-permute-start(bf16[16,32,128]{2,1,0:T(8,128)(2,1)S(1)} %get-tuple-element.23), channel_id=1, source_target_pairs={{0,2},{2,0},{4,8},{6,10},{8,4},{10,6},{12,14},{14,12},{1,3},{3,1},... | collective-permute-start | bytes 393224 | tf_op jit(solution)/shard_map/ppermute | solution.py:451

commit v9 on v7

--- a/solution.py
+++ b/solution.py
@@ -49,7 +49,7 @@
 
 def slot_masks(slots):
     half = slots // 2
-    between = (2, half + 1, slots - 1, 3, half)
+    between = (2, half + 1, half, slots - 1, 3)
     return (1, *between, slots - 2, 0), (slots - 2, *between, 1, 0)
 
 

time: 36.1 us -> 34.4 us (0.953)
  waiting for transfers between devices: 14.6 us -> 13.4 us
  starting transfers between devices: 13.8 us -> 13.3 us
    ppermute x7, waiting for transfers between devices: 14.4 us -> 13.2 us  [body(): lax.ppermute(parts[slot], 'freq', pairs)]
    ppermute x7, starting transfers between devices: 13.2 us -> 12.7 us  [body(): lax.ppermute(parts[slot], 'freq', pairs)]
  transfers between devices with their start and end apart: 9 -> 9, of which waited for: 3 -> 3; matrix products, arithmetic and copies ran while one was open for 0% -> 0% of each run, Pallas kernels for 6% -> 7%
where the time goes in v9:
time: 34.4 us; the launch traced here: 34.3 us
  waiting for transfers between devices  13.4 us (39%)
  starting transfers between devices  13.3 us (39%)
  Pallas kernels  6.89 us (20%)
  between operations  0.69 us (2%)
    ppermute x7, waiting for transfers between devices, body(): lax.ppermute(parts[slot], 'freq', pairs)  13.2 us
    ppermute x7, starting transfers between devices, body(): lax.ppermute(parts[slot], 'freq', pairs)  12.7 us
    pallas_call x1, Pallas kernels, partials(): call(functools.partial(other_kernel, freq_total, slots), 'other', [hbm] *...  3.28 us
    pallas_call x1, Pallas kernels, peaks(): pl.pallas_call(functools.partial(peak_kernel, freq_total, folded, sources...  1.38 us
    pallas_call x1, Pallas kernels, partials(): call(functools.partial(own_kernel, freq_total, slots), 'own', [vmem] * 4,...  1.26 us
  transfers between devices with their start and end apart: 9, of which 3 were waited for; matrix products, arithmetic and copies ran while one was open for 0% of the time, Pallas kernels for 7%

profile of v9, /device:TPU:0, one launch (start us, length us, event | category | flops | bytes accessed | tf_op | source)
XLA Modules:
  0.0 34.3 jit_solution(17226164823555928930)
XLA Ops:
  0.6 3.3 %other.1 = (bf16[32,64,128]{2,1,0:T(8,128)(2,1)S(1)}, bf16[32,64,128]{2,1,0:T(8,128)(2,1)S(1)}, bf16[2,8,128,256]{3,2,1,0:T(8,128)(2,1)S(1)}, f32[2,128]{1,0:T(2...) custom-call(bf16[8,2,2,128,256]{4,3,2,1,0:T(8,128)(2,1)} %bitcast.3, f32[256,256]{1,0:T(8,128)} %refs_1_.1, ...), custom_call_target="tpu_custom_call" | custom-call | flops 1000 | bytes 1000 | tf_op jit(solution)/shard_map/other/pallas_call | solution.py:246
  3.9 0.5 %collective-permute-start.4 = (bf16[32,64,128]{2,1,0:T(8,128)(2,1)S(1)}, bf16[32,64,128]{2,1,0:T(8,128)(2,1)S(1)}, u32[]{:S(2)}, u32[]{:S(2)}) collective-permute-start(bf16[32,64,128]{2,1,0:T(8,128)(2,1)S(1)} %get-tuple-element.24), channel_id=1, source_target_pairs={{0,1},{1,0},{2,3},{3,2},{4,5},{5,4},{6,7},{7,6},{8,9},{9,8},{10,11... | collective-permute-start | bytes 1572872 | tf_op jit(solution)/shard_map/ppermute | solution.py:263
  4.4 0.1 collective-permute-start
  4.5 1.3 %own.1.own_ref = bf16[32,128,128]{2,1,0:T(8,128)(2,1)S(1)} custom-call(bf16[2,8,128,256]{3,2,1,0:T(8,128)(2,1)S(1)} %get-tuple-element.16.refs_0_, f32[128,128]{1,0:T(8,128)S(1)} %get-tuple-element.17.refs_1_, f32[2,128]{1,0:T(2,128)S(1)} %get-tuple-element.18.refs_2_, f32[2,128]{1,0:T(2,128)S(1)} %get-tuple-element.19.refs_3_), custom_call_target="tpu_custom_call" | custom-call | flops 1000 | bytes 1000 | tf_op jit(solution)/shard_map/own/pallas_call | solution.py:265
  5.8 0.0 copy-start
  5.8 0.2 collective-permute-done.4.moved_ref
  6.0 0.3 add_first.1
  6.3 2.9 %collective-permute-start.5 = (bf16[16,32,128]{2,1,0:T(8,128)(2,1)S(1)}, bf16[16,32,128]{2,1,0:T(8,128)(2,1)S(1)}, u32[]{:S(2)}, u32[]{:S(2)}) collective-permute-start(bf16[16,32,128]{2,1,0:T(8,128)(2,1)S(1)} %get-tuple-element.25), channel_id=1, source_target_pairs={{0,2},{2,0},{4,8},{6,10},{8,4},{10,6},{12,14},{14,12},{1,3},{3,1},... | collective-permute-start | bytes 393224 | tf_op jit(solution)/shard_map/ppermute | solution.py:451
  9.2 1.7 %collective-permute-start.6 = (bf16[16,32,128]{2,1,0:T(8,128)(2,1)S(1)}, bf16[16,32,128]{2,1,0:T(8,128)(2,1)S(1)}, u32[]{:S(2)}, u32[]{:S(2)}) collective-permute-start(bf16[16,32,128]{2,1,0:T(8,128)(2,1)S(1)} %get-tuple-element.26), channel_id=1, source_target_pairs={{0,4},{2,6},{4,0},{6,2},{8,12},{10,14},{12,8},{14,10},{1,5},{3,7},... | collective-permute-start | bytes 393224 | tf_op jit(solution)/shard_map/ppermute | solution.py:451
  10.9 2.5 %collective-permute-start.7 = (bf16[16,32,128]{2,1,0:T(8,128)(2,1)S(1)}, bf16[16,32,128]{2,1,0:T(8,128)(2,1)S(1)}, u32[]{:S(2)}, u32[]{:S(2)}) collective-permute-start(bf16[16,32,128]{2,1,0:T(8,128)(2,1)S(1)} %get-tuple-element.27), channel_id=1, source_target_pairs={{0,10},{2,8},{4,14},{6,12},{8,2},{10,0},{12,6},{14,4},{1,11},{3,9}... | collective-permute-start | bytes 393224 | tf_op jit(solution)/shard_map/ppermute | solution.py:451
  13.4 1.4 %collective-permute-start.8 = (bf16[16,32,128]{2,1,0:T(8,128)(2,1)S(1)}, bf16[16,32,128]{2,1,0:T(8,128)(2,1)S(1)}, u32[]{:S(2)}, u32[]{:S(2)}) collective-permute-start(bf16[16,32,128]{2,1,0:T(8,128)(2,1)S(1)} %get-tuple-element.28), channel_id=1, source_target_pairs={{0,8},{2,10},{4,12},{6,14},{8,0},{10,2},{12,4},{14,6},{1,9},{3,11}... | collective-permute-start | bytes 393224 | tf_op jit(solution)/shard_map/ppermute | solution.py:451
  14.8 0.0 collective-permute-done.moved_ref
  14.8 0.3 add_second.1
  15.1 2.0 %collective-permute-start.1 = (bf16[16,32,128]{2,1,0:T(8,128)(2,1)S(1)}, bf16[16,32,128]{2,1,0:T(8,128)(2,1)S(1)}, u32[]{:S(2)}, u32[]{:S(2)}) collective-permute-start(bf16[16,32,128]{2,1,0:T(8,128)(2,1)S(1)} %get-tuple-element.21), channel_id=1, source_target_pairs={{0,14},{2,12},{4,10},{6,8},{8,6},{10,4},{12,2},{14,0},{1,15},{3,13... | collective-permute-start | bytes 393224 | tf_op jit(solution)/shard_map/ppermute | solution.py:451
  17.1 0.0 collective-permute-done.5.refs_3_
  17.1 1.1 %collective-permute-start.2 = (bf16[16,32,128]{2,1,0:T(8,128)(2,1)S(1)}, bf16[16,32,128]{2,1,0:T(8,128)(2,1)S(1)}, u32[]{:S(2)}, u32[]{:S(2)}) collective-permute-start(bf16[16,32,128]{2,1,0:T(8,128)(2,1)S(1)} %get-tuple-element.22), channel_id=1, source_target_pairs={{0,6},{2,4},{4,2},{6,0},{8,14},{10,12},{12,10},{14,8},{1,7},{3,5},... | collective-permute-start | bytes 393224 | tf_op jit(solution)/shard_map/ppermute | solution.py:451
  18.2 0.0 collective-permute-done.6.refs_4_
  18.2 1.2 %collective-permute-start.3 = (bf16[16,32,128]{2,1,0:T(8,128)(2,1)S(1)}, bf16[16,32,128]{2,1,0:T(8,128)(2,1)S(1)}, u32[]{:S(2)}, u32[]{:S(2)}) collective-permute-start(bf16[16,32,128]{2,1,0:T(8,128)(2,1)S(1)} %get-tuple-element.23), channel_id=1, source_target_pairs={{0,12},{2,14},{4,6},{6,4},{8,10},{10,8},{12,0},{14,2},{1,13},{3,15... | collective-permute-start | bytes 393224 | tf_op jit(solution)/shard_map/ppermute | solution.py:451
  19.4 0.3 table.1.refs_8_
  19.7 8.0 %collective-permute-done.7.refs_5_ = bf16[16,32,128]{2,1,0:T(8,128)(2,1)S(1)} collective-permute-done((bf16[16,32,128]{2,1,0:T(8,128)(2,1)S(1)}, bf16[16,32,128]{2,1,0:T(8,128)(2,1)S(1)}, u32[]{:S(2)}, u32[]{:S(2)}) %collective-permute-start.7) | collective-permute-done | bytes 131104 | tf_op jit(solution)/shard_map/ppermute | solution.py:451
  27.7 5.2 %collective-permute-done.8.refs_6_ = bf16[16,32,128]{2,1,0:T(8,128)(2,1)S(1)} collective-permute-done((bf16[16,32,128]{2,1,0:T(8,128)(2,1)S(1)}, bf16[16,32,128]{2,1,0:T(8,128)(2,1)S(1)}, u32[]{:S(2)}, u32[]{:S(2)}) %collective-permute-start.8) | collective-permute-done | bytes 131104 | tf_op jit(solution)/shard_map/ppermute | solution.py:451
  32.9 0.0 collective-permute-done.1.refs_0_
  32.9 0.0 collective-permute-done.2.refs_1_
  32.9 0.0 collective-permute-done.3.refs_2_
  32.9 0.0 copy-done
  32.9 1.4 %peaks.1 = (f32[1,16]{1,0:T(1,128)}, f32[1,16]{1,0:T(1,128)}) custom-call(bf16[16,32,128]{2,1,0:T(8,128)(2,1)S(1)} %collective-permute-done.1.refs_0_, bf16[16,32,128]{2,1,0:T(8,128)(2,1)S(1)} %collective-permute-done.2.refs_1_, bf16[16,32,128]{2,1,0:T(8,128)(2,1)S(1)} %collective-permute-done.3.refs_2_, ...), custom_call_target="tpu_custom_call" | custom-call | tf_op jit(solution)/shard_map/peaks/pallas_call | solution.py:404
Async XLA Ops:
  3.9 2.1 %collective-permute-start.4 = (bf16[32,64,128]{2,1,0:T(8,128)(2,1)S(1)}, bf16[32,64,128]{2,1,0:T(8,128)(2,1)S(1)}, u32[]{:S(2)}, u32[]{:S(2)}) collective-permute-start(bf16[32,64,128]{2,1,0:T(8,128)(2,1)S(1)} %get-tuple-element.24), channel_id=1, source_target_pairs={{0,1},{1,0},{2,3},{3,2},{4,5},{5,4},{6,7},{7,6},{8,9},{9,8},{10,11... | collective-permute-start | bytes 1572872 | tf_op jit(solution)/shard_map/ppermute | solution.py:263
  4.4 10.3 %collective-permute-start = (bf16[32,64,128]{2,1,0:T(8,128)(2,1)S(1)}, bf16[32,64,128]{2,1,0:T(8,128)(2,1)S(1)}, u32[]{:S(2)}, u32[]{:S(2)}) collective-permute-start(bf16[32,64,128]{2,1,0:T(8,128)(2,1)S(1)} %get-tuple-element.20), channel_id=1, source_target_pairs={{0,1},{1,0},{2,3},{3,2},{4,5},{5,4},{6,7},{7,6},{8,9},{9,8},{10,11... | collective-permute-start | bytes 1572872 | tf_op jit(solution)/shard_map/ppermute | solution.py:264
  5.8 27.1 %copy-start = (f32[1,16]{1,0:T(1,128)S(1)}, f32[1,16]{1,0:T(1,128)}, u32[]{:S(2)}) copy-start(f32[1,16]{1,0:T(1,128)} %refs_9_.1) | copy-start | bytes 196
  6.3 10.8 %collective-permute-start.5 = (bf16[16,32,128]{2,1,0:T(8,128)(2,1)S(1)}, bf16[16,32,128]{2,1,0:T(8,128)(2,1)S(1)}, u32[]{:S(2)}, u32[]{:S(2)}) collective-permute-start(bf16[16,32,128]{2,1,0:T(8,128)(2,1)S(1)} %get-tuple-element.25), channel_id=1, source_target_pairs={{0,2},{2,0},{4,8},{6,10},{8,4},{10,6},{12,14},{14,12},{1,3},{3,1},... | collective-permute-start | bytes 393224 | tf_op jit(solution)/shard_map/ppermute | solution.py:451
  9.2 8.9 %collective-permute-start.6 = (bf16[16,32,128]{2,1,0:T(8,128)(2,1)S(1)}, bf16[16,32,128]{2,1,0:T(8,128)(2,1)S(1)}, u32[]{:S(2)}, u32[]{:S(2)}) collective-permute-start(bf16[16,32,128]{2,1,0:T(8,128)(2,1)S(1)} %get-tuple-element.26), channel_id=1, source_target_pairs={{0,4},{2,6},{4,0},{6,2},{8,12},{10,14},{12,8},{14,10},{1,5},{3,7},... | collective-permute-start | bytes 393224 | tf_op jit(solution)/shard_map/ppermute | solution.py:451
  10.9 16.8 %collective-permute-start.7 = (bf16[16,32,128]{2,1,0:T(8,128)(2,1)S(1)}, bf16[16,32,128]{2,1,0:T(8,128)(2,1)S(1)}, u32[]{:S(2)}, u32[]{:S(2)}) collective-permute-start(bf16[16,32,128]{2,1,0:T(8,128)(2,1)S(1)} %get-tuple-element.27), channel_id=1, source_target_pairs={{0,10},{2,8},{4,14},{6,12},{8,2},{10,0},{12,6},{14,4},{1,11},{3,9}... | collective-permute-start | bytes 393224 | tf_op jit(solution)/shard_map/ppermute | solution.py:451
  13.4 19.5 %collective-permute-start.8 = (bf16[16,32,128]{2,1,0:T(8,128)(2,1)S(1)}, bf16[16,32,128]{2,1,0:T(8,128)(2,1)S(1)}, u32[]{:S(2)}, u32[]{:S(2)}) collective-permute-start(bf16[16,32,128]{2,1,0:T(8,128)(2,1)S(1)} %get-tuple-element.28), channel_id=1, source_target_pairs={{0,8},{2,10},{4,12},{6,14},{8,0},{10,2},{12,4},{14,6},{1,9},{3,11}... | collective-permute-start | bytes 393224 | tf_op jit(solution)/shard_map/ppermute | solution.py:451
  15.1 17.8 %collective-permute-start.1 = (bf16[16,32,128]{2,1,0:T(8,128)(2,1)S(1)}, bf16[16,32,128]{2,1,0:T(8,128)(2,1)S(1)}, u32[]{:S(2)}, u32[]{:S(2)}) collective-permute-start(bf16[16,32,128]{2,1,0:T(8,128)(2,1)S(1)} %get-tuple-element.21), channel_id=1, source_target_pairs={{0,14},{2,12},{4,10},{6,8},{8,6},{10,4},{12,2},{14,0},{1,15},{3,13... | collective-permute-start | bytes 393224 | tf_op jit(solution)/shard_map/ppermute | solution.py:451
  17.1 15.8 %collective-permute-start.2 = (bf16[16,32,128]{2,1,0:T(8,128)(2,1)S(1)}, bf16[16,32,128]{2,1,0:T(8,128)(2,1)S(1)}, u32[]{:S(2)}, u32[]{:S(2)}) collective-permute-start(bf16[16,32,128]{2,1,0:T(8,128)(2,1)S(1)} %get-tuple-element.22), channel_id=1, source_target_pairs={{0,6},{2,4},{4,2},{6,0},{8,14},{10,12},{12,10},{14,8},{1,7},{3,5},... | collective-permute-start | bytes 393224 | tf_op jit(solution)/shard_map/ppermute | solution.py:451
  18.2 14.7 %collective-permute-start.3 = (bf16[16,32,128]{2,1,0:T(8,128)(2,1)S(1)}, bf16[16,32,128]{2,1,0:T(8,128)(2,1)S(1)}, u32[]{:S(2)}, u32[]{:S(2)}) collective-permute-start(bf16[16,32,128]{2,1,0:T(8,128)(2,1)S(1)} %get-tuple-element.23), channel_id=1, source_target_pairs={{0,12},{2,14},{4,6},{6,4},{8,10},{10,8},{12,0},{14,2},{1,13},{3,15... | collective-permute-start | bytes 393224 | tf_op jit(solution)/shard_map/ppermute | solution.py:451

commit v10 on v6

--- a/solution.py
+++ b/solution.py
@@ -336,7 +336,7 @@
     columns = peak_ref.shape[1]
     time_block = table_ref.shape[2] // 2
 
-    @pl.when(first_step())
+    @pl.when(first_step() and (blocks > 1 or columns < best_ref.shape[0]) if blocks == 1 else first_step())
     def _():
         best_ref[...] = jnp.zeros_like(best_ref)
 
@@ -369,9 +369,8 @@
         power = jnp.max(power, axis=0, keepdims=True)
         for k in range(width):
             row = pl.ds(first + k, 1)
-            best_ref[row, :] = jnp.maximum(
-                best_ref[row, :], power[:, k * ROWS : (k + 1) * ROWS]
-            )
+            value = power[:, k * ROWS : (k + 1) * ROWS]
+            best_ref[row, :] = value if blocks == 1 else jnp.maximum(best_ref[row, :], value)
 
     @pl.when(last_step())
     def _():

time: 34.4 us -> 34.4 us (level)
  no operation moved by 1% of the time
where the time goes in v10:
time: 34.4 us; the launch traced here: 34.2 us
  starting transfers between devices  13.8 us (40%)
  waiting for transfers between devices  12.8 us (37%)
  Pallas kernels  6.89 us (20%)
  between operations  0.69 us (2%)
    ppermute x7, starting transfers between devices, body(): lax.ppermute(parts[slot], 'freq', pairs)  13.2 us
    ppermute x7, waiting for transfers between devices, body(): lax.ppermute(parts[slot], 'freq', pairs)  12.6 us
    pallas_call x1, Pallas kernels, partials(): call(functools.partial(other_kernel, freq_total, slots), 'other', [hbm] *...  3.28 us
    pallas_call x1, Pallas kernels, peaks(): pl.pallas_call(functools.partial(peak_kernel, freq_total, folded, sources...  1.37 us
    pallas_call x1, Pallas kernels, partials(): call(functools.partial(own_kernel, freq_total, slots), 'own', [vmem] * 4,...  1.26 us
  transfers between devices with their start and end apart: 9, of which 3 were waited for; matrix products, arithmetic and copies ran while one was open for 0% of the time, Pallas kernels for 7%

profile of v10, /device:TPU:0, one launch (start us, length us, event | category | flops | bytes accessed | tf_op | source)
XLA Modules:
  0.0 34.2 jit_solution(7503446095587721541)
XLA Ops:
  0.6 3.3 %other.1 = (bf16[32,64,128]{2,1,0:T(8,128)(2,1)S(1)}, bf16[32,64,128]{2,1,0:T(8,128)(2,1)S(1)}, bf16[2,8,128,256]{3,2,1,0:T(8,128)(2,1)S(1)}, f32[2,128]{1,0:T(2...) custom-call(bf16[8,2,2,128,256]{4,3,2,1,0:T(8,128)(2,1)} %bitcast.3, f32[256,256]{1,0:T(8,128)} %refs_1_.1, ...), custom_call_target="tpu_custom_call" | custom-call | flops 1000 | bytes 1000 | tf_op jit(solution)/shard_map/other/pallas_call | solution.py:246
  3.9 0.5 %collective-permute-start.4 = (bf16[32,64,128]{2,1,0:T(8,128)(2,1)S(1)}, bf16[32,64,128]{2,1,0:T(8,128)(2,1)S(1)}, u32[]{:S(2)}, u32[]{:S(2)}) collective-permute-start(bf16[32,64,128]{2,1,0:T(8,128)(2,1)S(1)} %get-tuple-element.24), channel_id=1, source_target_pairs={{0,1},{1,0},{2,3},{3,2},{4,5},{5,4},{6,7},{7,6},{8,9},{9,8},{10,11... | collective-permute-start | bytes 1572872 | tf_op jit(solution)/shard_map/ppermute | solution.py:263
  4.4 0.1 collective-permute-start
  4.5 1.3 %own.1.own_ref = bf16[32,128,128]{2,1,0:T(8,128)(2,1)S(1)} custom-call(bf16[2,8,128,256]{3,2,1,0:T(8,128)(2,1)S(1)} %get-tuple-element.16.refs_0_, f32[128,128]{1,0:T(8,128)S(1)} %get-tuple-element.17.refs_1_, f32[2,128]{1,0:T(2,128)S(1)} %get-tuple-element.18.refs_2_, f32[2,128]{1,0:T(2,128)S(1)} %get-tuple-element.19.refs_3_), custom_call_target="tpu_custom_call" | custom-call | flops 1000 | bytes 1000 | tf_op jit(solution)/shard_map/own/pallas_call | solution.py:265
  5.8 0.0 copy-start
  5.8 0.2 collective-permute-done.4.moved_ref
  6.0 0.3 add_first.1
  6.3 2.9 %collective-permute-start.5 = (bf16[16,32,128]{2,1,0:T(8,128)(2,1)S(1)}, bf16[16,32,128]{2,1,0:T(8,128)(2,1)S(1)}, u32[]{:S(2)}, u32[]{:S(2)}) collective-permute-start(bf16[16,32,128]{2,1,0:T(8,128)(2,1)S(1)} %get-tuple-element.25), channel_id=1, source_target_pairs={{0,2},{2,0},{4,8},{6,10},{8,4},{10,6},{12,14},{14,12},{1,3},{3,1},... | collective-permute-start | bytes 393224 | tf_op jit(solution)/shard_map/ppermute | solution.py:450
  9.2 1.7 %collective-permute-start.6 = (bf16[16,32,128]{2,1,0:T(8,128)(2,1)S(1)}, bf16[16,32,128]{2,1,0:T(8,128)(2,1)S(1)}, u32[]{:S(2)}, u32[]{:S(2)}) collective-permute-start(bf16[16,32,128]{2,1,0:T(8,128)(2,1)S(1)} %get-tuple-element.26), channel_id=1, source_target_pairs={{0,4},{2,6},{4,0},{6,2},{8,12},{10,14},{12,8},{14,10},{1,5},{3,7},... | collective-permute-start | bytes 393224 | tf_op jit(solution)/shard_map/ppermute | solution.py:450
  10.9 2.5 %collective-permute-start.7 = (bf16[16,32,128]{2,1,0:T(8,128)(2,1)S(1)}, bf16[16,32,128]{2,1,0:T(8,128)(2,1)S(1)}, u32[]{:S(2)}, u32[]{:S(2)}) collective-permute-start(bf16[16,32,128]{2,1,0:T(8,128)(2,1)S(1)} %get-tuple-element.27), channel_id=1, source_target_pairs={{0,10},{2,8},{4,14},{6,12},{8,2},{10,0},{12,6},{14,4},{1,11},{3,9}... | collective-permute-start | bytes 393224 | tf_op jit(solution)/shard_map/ppermute | solution.py:450
  13.4 1.4 %collective-permute-start.8 = (bf16[16,32,128]{2,1,0:T(8,128)(2,1)S(1)}, bf16[16,32,128]{2,1,0:T(8,128)(2,1)S(1)}, u32[]{:S(2)}, u32[]{:S(2)}) collective-permute-start(bf16[16,32,128]{2,1,0:T(8,128)(2,1)S(1)} %get-tuple-element.28), channel_id=1, source_target_pairs={{0,8},{2,10},{4,12},{6,14},{8,0},{10,2},{12,4},{14,6},{1,9},{3,11}... | collective-permute-start | bytes 393224 | tf_op jit(solution)/shard_map/ppermute | solution.py:450
  14.8 0.0 collective-permute-done.moved_ref
  14.8 0.3 add_second.1
  15.1 0.4 %collective-permute-start.1 = (bf16[16,32,128]{2,1,0:T(8,128)(2,1)S(1)}, bf16[16,32,128]{2,1,0:T(8,128)(2,1)S(1)}, u32[]{:S(2)}, u32[]{:S(2)}) collective-permute-start(bf16[16,32,128]{2,1,0:T(8,128)(2,1)S(1)} %get-tuple-element.21), channel_id=1, source_target_pairs={{0,6},{2,4},{4,2},{6,0},{8,14},{10,12},{12,10},{14,8},{1,7},{3,5},... | collective-permute-start | bytes 393224 | tf_op jit(solution)/shard_map/ppermute | solution.py:450
  15.5 0.0 collective-permute-done.5.refs_3_
  15.5 3.6 %collective-permute-start.2 = (bf16[16,32,128]{2,1,0:T(8,128)(2,1)S(1)}, bf16[16,32,128]{2,1,0:T(8,128)(2,1)S(1)}, u32[]{:S(2)}, u32[]{:S(2)}) collective-permute-start(bf16[16,32,128]{2,1,0:T(8,128)(2,1)S(1)} %get-tuple-element.22), channel_id=1, source_target_pairs={{0,14},{2,12},{4,10},{6,8},{8,6},{10,4},{12,2},{14,0},{1,15},{3,13... | collective-permute-start | bytes 393224 | tf_op jit(solution)/shard_map/ppermute | solution.py:450
  19.1 0.0 collective-permute-done.6.refs_4_
  19.1 0.8 %collective-permute-start.3 = (bf16[16,32,128]{2,1,0:T(8,128)(2,1)S(1)}, bf16[16,32,128]{2,1,0:T(8,128)(2,1)S(1)}, u32[]{:S(2)}, u32[]{:S(2)}) collective-permute-start(bf16[16,32,128]{2,1,0:T(8,128)(2,1)S(1)} %get-tuple-element.23), channel_id=1, source_target_pairs={{0,12},{2,14},{4,6},{6,4},{8,10},{10,8},{12,0},{14,2},{1,13},{3,15... | collective-permute-start | bytes 393224 | tf_op jit(solution)/shard_map/ppermute | solution.py:450
  19.9 0.3 table.1.refs_8_
  20.2 4.5 %collective-permute-done.7.refs_5_ = bf16[16,32,128]{2,1,0:T(8,128)(2,1)S(1)} collective-permute-done((bf16[16,32,128]{2,1,0:T(8,128)(2,1)S(1)}, bf16[16,32,128]{2,1,0:T(8,128)(2,1)S(1)}, u32[]{:S(2)}, u32[]{:S(2)}) %collective-permute-start.7) | collective-permute-done | bytes 131104 | tf_op jit(solution)/shard_map/ppermute | solution.py:450
  24.7 8.1 %collective-permute-done.8.refs_6_ = bf16[16,32,128]{2,1,0:T(8,128)(2,1)S(1)} collective-permute-done((bf16[16,32,128]{2,1,0:T(8,128)(2,1)S(1)}, bf16[16,32,128]{2,1,0:T(8,128)(2,1)S(1)}, u32[]{:S(2)}, u32[]{:S(2)}) %collective-permute-start.8) | collective-permute-done | bytes 131104 | tf_op jit(solution)/shard_map/ppermute | solution.py:450
  32.8 0.0 collective-permute-done.1.refs_0_
  32.8 0.0 collective-permute-done.2.refs_1_
  32.8 0.0 collective-permute-done.3.refs_2_
  32.8 0.0 copy-done
  32.9 1.4 %peaks.1 = (f32[1,16]{1,0:T(1,128)}, f32[1,16]{1,0:T(1,128)}) custom-call(bf16[16,32,128]{2,1,0:T(8,128)(2,1)S(1)} %collective-permute-done.1.refs_0_, bf16[16,32,128]{2,1,0:T(8,128)(2,1)S(1)} %collective-permute-done.2.refs_1_, bf16[16,32,128]{2,1,0:T(8,128)(2,1)S(1)} %collective-permute-done.3.refs_2_, ...), custom_call_target="tpu_custom_call" | custom-call | tf_op jit(solution)/shard_map/peaks/pallas_call | solution.py:403
Async XLA Ops:
  3.9 2.1 %collective-permute-start.4 = (bf16[32,64,128]{2,1,0:T(8,128)(2,1)S(1)}, bf16[32,64,128]{2,1,0:T(8,128)(2,1)S(1)}, u32[]{:S(2)}, u32[]{:S(2)}) collective-permute-start(bf16[32,64,128]{2,1,0:T(8,128)(2,1)S(1)} %get-tuple-element.24), channel_id=1, source_target_pairs={{0,1},{1,0},{2,3},{3,2},{4,5},{5,4},{6,7},{7,6},{8,9},{9,8},{10,11... | collective-permute-start | bytes 1572872 | tf_op jit(solution)/shard_map/ppermute | solution.py:263
  4.4 10.3 %collective-permute-start = (bf16[32,64,128]{2,1,0:T(8,128)(2,1)S(1)}, bf16[32,64,128]{2,1,0:T(8,128)(2,1)S(1)}, u32[]{:S(2)}, u32[]{:S(2)}) collective-permute-start(bf16[32,64,128]{2,1,0:T(8,128)(2,1)S(1)} %get-tuple-element.20), channel_id=1, source_target_pairs={{0,1},{1,0},{2,3},{3,2},{4,5},{5,4},{6,7},{7,6},{8,9},{9,8},{10,11... | collective-permute-start | bytes 1572872 | tf_op jit(solution)/shard_map/ppermute | solution.py:264
  5.8 27.1 %copy-start = (f32[1,16]{1,0:T(1,128)S(1)}, f32[1,16]{1,0:T(1,128)}, u32[]{:S(2)}) copy-start(f32[1,16]{1,0:T(1,128)} %refs_9_.1) | copy-start | bytes 196
  6.3 9.2 %collective-permute-start.5 = (bf16[16,32,128]{2,1,0:T(8,128)(2,1)S(1)}, bf16[16,32,128]{2,1,0:T(8,128)(2,1)S(1)}, u32[]{:S(2)}, u32[]{:S(2)}) collective-permute-start(bf16[16,32,128]{2,1,0:T(8,128)(2,1)S(1)} %get-tuple-element.25), channel_id=1, source_target_pairs={{0,2},{2,0},{4,8},{6,10},{8,4},{10,6},{12,14},{14,12},{1,3},{3,1},... | collective-permute-start | bytes 393224 | tf_op jit(solution)/shard_map/ppermute | solution.py:450
  9.2 9.8 %collective-permute-start.6 = (bf16[16,32,128]{2,1,0:T(8,128)(2,1)S(1)}, bf16[16,32,128]{2,1,0:T(8,128)(2,1)S(1)}, u32[]{:S(2)}, u32[]{:S(2)}) collective-permute-start(bf16[16,32,128]{2,1,0:T(8,128)(2,1)S(1)} %get-tuple-element.26), channel_id=1, source_target_pairs={{0,4},{2,6},{4,0},{6,2},{8,12},{10,14},{12,8},{14,10},{1,5},{3,7},... | collective-permute-start | bytes 393224 | tf_op jit(solution)/shard_map/ppermute | solution.py:450
  10.9 13.8 %collective-permute-start.7 = (bf16[16,32,128]{2,1,0:T(8,128)(2,1)S(1)}, bf16[16,32,128]{2,1,0:T(8,128)(2,1)S(1)}, u32[]{:S(2)}, u32[]{:S(2)}) collective-permute-start(bf16[16,32,128]{2,1,0:T(8,128)(2,1)S(1)} %get-tuple-element.27), channel_id=1, source_target_pairs={{0,10},{2,8},{4,14},{6,12},{8,2},{10,0},{12,6},{14,4},{1,11},{3,9}... | collective-permute-start | bytes 393224 | tf_op jit(solution)/shard_map/ppermute | solution.py:450
  13.4 19.5 %collective-permute-start.8 = (bf16[16,32,128]{2,1,0:T(8,128)(2,1)S(1)}, bf16[16,32,128]{2,1,0:T(8,128)(2,1)S(1)}, u32[]{:S(2)}, u32[]{:S(2)}) collective-permute-start(bf16[16,32,128]{2,1,0:T(8,128)(2,1)S(1)} %get-tuple-element.28), channel_id=1, source_target_pairs={{0,8},{2,10},{4,12},{6,14},{8,0},{10,2},{12,4},{14,6},{1,9},{3,11}... | collective-permute-start | bytes 393224 | tf_op jit(solution)/shard_map/ppermute | solution.py:450
  15.1 17.7 %collective-permute-start.1 = (bf16[16,32,128]{2,1,0:T(8,128)(2,1)S(1)}, bf16[16,32,128]{2,1,0:T(8,128)(2,1)S(1)}, u32[]{:S(2)}, u32[]{:S(2)}) collective-permute-start(bf16[16,32,128]{2,1,0:T(8,128)(2,1)S(1)} %get-tuple-element.21), channel_id=1, source_target_pairs={{0,6},{2,4},{4,2},{6,0},{8,14},{10,12},{12,10},{14,8},{1,7},{3,5},... | collective-permute-start | bytes 393224 | tf_op jit(solution)/shard_map/ppermute | solution.py:450
  15.5 17.3 %collective-permute-start.2 = (bf16[16,32,128]{2,1,0:T(8,128)(2,1)S(1)}, bf16[16,32,128]{2,1,0:T(8,128)(2,1)S(1)}, u32[]{:S(2)}, u32[]{:S(2)}) collective-permute-start(bf16[16,32,128]{2,1,0:T(8,128)(2,1)S(1)} %get-tuple-element.22), channel_id=1, source_target_pairs={{0,14},{2,12},{4,10},{6,8},{8,6},{10,4},{12,2},{14,0},{1,15},{3,13... | collective-permute-start | bytes 393224 | tf_op jit(solution)/shard_map/ppermute | solution.py:450
  19.1 13.8 %collective-permute-start.3 = (bf16[16,32,128]{2,1,0:T(8,128)(2,1)S(1)}, bf16[16,32,128]{2,1,0:T(8,128)(2,1)S(1)}, u32[]{:S(2)}, u32[]{:S(2)}) collective-permute-start(bf16[16,32,128]{2,1,0:T(8,128)(2,1)S(1)} %get-tuple-element.23), channel_id=1, source_target_pairs={{0,12},{2,14},{4,6},{6,4},{8,10},{10,8},{12,0},{14,2},{1,13},{3,15... | collective-permute-start | bytes 393224 | tf_op jit(solution)/shard_map/ppermute | solution.py:450

commit v11 on v6

--- a/solution.py
+++ b/solution.py
@@ -187,10 +187,11 @@
         )
         for parity in range(2)
     ]
+    order = slot_order(slots)
+    for copy in copies[1:]:
+        copy.wait()
     field_copies[0].start()
-    order = slot_order(slots)
-    for copy in copies:
-        copy.wait()
+    copies[0].wait()
     field_copies[1].start()
     group = lax.axis_index("elem")
     groups = (1 - group, group)

time: 34.4 us -> 34.7 us (level)
  transfers between devices with their start and end apart: 9 -> 9, of which waited for: 3 -> 3; matrix products, arithmetic and copies ran while one was open for 0% -> 0% of each run, Pallas kernels for 7% -> 6%
where the time goes in v11:
time: 34.7 us; the launch traced here: 34.5 us
  starting transfers between devices  13.8 us (40%)
  waiting for transfers between devices  12.8 us (37%)
  Pallas kernels  7.14 us (21%)
  between operations  0.69 us (2%)
    ppermute x7, starting transfers between devices, body(): lax.ppermute(parts[slot], 'freq', pairs)  13.2 us
    ppermute x7, waiting for transfers between devices, body(): lax.ppermute(parts[slot], 'freq', pairs)  12.6 us
    pallas_call x1, Pallas kernels, partials(): call(functools.partial(other_kernel, freq_total, slots), 'other', [hbm] *...  3.53 us
    pallas_call x1, Pallas kernels, peaks(): pl.pallas_call(functools.partial(peak_kernel, freq_total, folded, sources...  1.38 us
    pallas_call x1, Pallas kernels, partials(): call(functools.partial(own_kernel, freq_total, slots), 'own', [vmem] * 4,...  1.26 us
  transfers between devices with their start and end apart: 9, of which 3 were waited for; matrix products, arithmetic and copies ran while one was open for 0% of the time, Pallas kernels for 6%

profile of v11, /device:TPU:0, one launch (start us, length us, event | category | flops | bytes accessed | tf_op | source)
XLA Modules:
  0.0 34.5 jit_solution(13875263748323457836)
XLA Ops:
  0.6 3.5 %other.1 = (bf16[32,64,128]{2,1,0:T(8,128)(2,1)S(1)}, bf16[32,64,128]{2,1,0:T(8,128)(2,1)S(1)}, bf16[2,8,128,256]{3,2,1,0:T(8,128)(2,1)S(1)}, f32[2,128]{1,0:T(2...) custom-call(bf16[8,2,2,128,256]{4,3,2,1,0:T(8,128)(2,1)} %bitcast.3, f32[256,256]{1,0:T(8,128)} %refs_1_.1, ...), custom_call_target="tpu_custom_call" | custom-call | flops 1000 | bytes 1000 | tf_op jit(solution)/shard_map/other/pallas_call | solution.py:247
  4.2 0.5 %collective-permute-start.4 = (bf16[32,64,128]{2,1,0:T(8,128)(2,1)S(1)}, bf16[32,64,128]{2,1,0:T(8,128)(2,1)S(1)}, u32[]{:S(2)}, u32[]{:S(2)}) collective-permute-start(bf16[32,64,128]{2,1,0:T(8,128)(2,1)S(1)} %get-tuple-element.24), channel_id=1, source_target_pairs={{0,1},{1,0},{2,3},{3,2},{4,5},{5,4},{6,7},{7,6},{8,9},{9,8},{10,11... | collective-permute-start | bytes 1572872 | tf_op jit(solution)/shard_map/ppermute | solution.py:264
  4.7 0.1 collective-permute-start
  4.8 1.3 %own.1.own_ref = bf16[32,128,128]{2,1,0:T(8,128)(2,1)S(1)} custom-call(bf16[2,8,128,256]{3,2,1,0:T(8,128)(2,1)S(1)} %get-tuple-element.16.refs_0_, f32[128,128]{1,0:T(8,128)S(1)} %get-tuple-element.17.refs_1_, f32[2,128]{1,0:T(2,128)S(1)} %get-tuple-element.18.refs_2_, f32[2,128]{1,0:T(2,128)S(1)} %get-tuple-element.19.refs_3_), custom_call_target="tpu_custom_call" | custom-call | flops 1000 | bytes 1000 | tf_op jit(solution)/shard_map/own/pallas_call | solution.py:266
  6.0 0.0 copy-start
  6.0 0.2 collective-permute-done.4.moved_ref
  6.2 0.3 add_first.1
  6.6 2.9 %collective-permute-start.5 = (bf16[16,32,128]{2,1,0:T(8,128)(2,1)S(1)}, bf16[16,32,128]{2,1,0:T(8,128)(2,1)S(1)}, u32[]{:S(2)}, u32[]{:S(2)}) collective-permute-start(bf16[16,32,128]{2,1,0:T(8,128)(2,1)S(1)} %get-tuple-element.25), channel_id=1, source_target_pairs={{0,2},{2,0},{4,8},{6,10},{8,4},{10,6},{12,14},{14,12},{1,3},{3,1},... | collective-permute-start | bytes 393224 | tf_op jit(solution)/shard_map/ppermute | solution.py:452
  9.5 1.7 %collective-permute-start.6 = (bf16[16,32,128]{2,1,0:T(8,128)(2,1)S(1)}, bf16[16,32,128]{2,1,0:T(8,128)(2,1)S(1)}, u32[]{:S(2)}, u32[]{:S(2)}) collective-permute-start(bf16[16,32,128]{2,1,0:T(8,128)(2,1)S(1)} %get-tuple-element.26), channel_id=1, source_target_pairs={{0,4},{2,6},{4,0},{6,2},{8,12},{10,14},{12,8},{14,10},{1,5},{3,7},... | collective-permute-start | bytes 393224 | tf_op jit(solution)/shard_map/ppermute | solution.py:452
  11.2 2.5 %collective-permute-start.7 = (bf16[16,32,128]{2,1,0:T(8,128)(2,1)S(1)}, bf16[16,32,128]{2,1,0:T(8,128)(2,1)S(1)}, u32[]{:S(2)}, u32[]{:S(2)}) collective-permute-start(bf16[16,32,128]{2,1,0:T(8,128)(2,1)S(1)} %get-tuple-element.27), channel_id=1, source_target_pairs={{0,10},{2,8},{4,14},{6,12},{8,2},{10,0},{12,6},{14,4},{1,11},{3,9}... | collective-permute-start | bytes 393224 | tf_op jit(solution)/shard_map/ppermute | solution.py:452
  13.6 1.4 %collective-permute-start.8 = (bf16[16,32,128]{2,1,0:T(8,128)(2,1)S(1)}, bf16[16,32,128]{2,1,0:T(8,128)(2,1)S(1)}, u32[]{:S(2)}, u32[]{:S(2)}) collective-permute-start(bf16[16,32,128]{2,1,0:T(8,128)(2,1)S(1)} %get-tuple-element.28), channel_id=1, source_target_pairs={{0,8},{2,10},{4,12},{6,14},{8,0},{10,2},{12,4},{14,6},{1,9},{3,11}... | collective-permute-start | bytes 393224 | tf_op jit(solution)/shard_map/ppermute | solution.py:452
  15.0 0.0 collective-permute-done.moved_ref
  15.0 0.3 add_second.1
  15.3 0.4 %collective-permute-start.1 = (bf16[16,32,128]{2,1,0:T(8,128)(2,1)S(1)}, bf16[16,32,128]{2,1,0:T(8,128)(2,1)S(1)}, u32[]{:S(2)}, u32[]{:S(2)}) collective-permute-start(bf16[16,32,128]{2,1,0:T(8,128)(2,1)S(1)} %get-tuple-element.21), channel_id=1, source_target_pairs={{0,6},{2,4},{4,2},{6,0},{8,14},{10,12},{12,10},{14,8},{1,7},{3,5},... | collective-permute-start | bytes 393224 | tf_op jit(solution)/shard_map/ppermute | solution.py:452
  15.8 0.0 collective-permute-done.5.refs_3_
  15.8 3.6 %collective-permute-start.2 = (bf16[16,32,128]{2,1,0:T(8,128)(2,1)S(1)}, bf16[16,32,128]{2,1,0:T(8,128)(2,1)S(1)}, u32[]{:S(2)}, u32[]{:S(2)}) collective-permute-start(bf16[16,32,128]{2,1,0:T(8,128)(2,1)S(1)} %get-tuple-element.22), channel_id=1, source_target_pairs={{0,14},{2,12},{4,10},{6,8},{8,6},{10,4},{12,2},{14,0},{1,15},{3,13... | collective-permute-start | bytes 393224 | tf_op jit(solution)/shard_map/ppermute | solution.py:452
  19.3 0.0 collective-permute-done.6.refs_4_
  19.3 0.8 %collective-permute-start.3 = (bf16[16,32,128]{2,1,0:T(8,128)(2,1)S(1)}, bf16[16,32,128]{2,1,0:T(8,128)(2,1)S(1)}, u32[]{:S(2)}, u32[]{:S(2)}) collective-permute-start(bf16[16,32,128]{2,1,0:T(8,128)(2,1)S(1)} %get-tuple-element.23), channel_id=1, source_target_pairs={{0,12},{2,14},{4,6},{6,4},{8,10},{10,8},{12,0},{14,2},{1,13},{3,15... | collective-permute-start | bytes 393224 | tf_op jit(solution)/shard_map/ppermute | solution.py:452
  20.1 0.3 table.1.refs_8_
  20.5 4.5 %collective-permute-done.7.refs_5_ = bf16[16,32,128]{2,1,0:T(8,128)(2,1)S(1)} collective-permute-done((bf16[16,32,128]{2,1,0:T(8,128)(2,1)S(1)}, bf16[16,32,128]{2,1,0:T(8,128)(2,1)S(1)}, u32[]{:S(2)}, u32[]{:S(2)}) %collective-permute-start.7) | collective-permute-done | bytes 131104 | tf_op jit(solution)/shard_map/ppermute | solution.py:452
  25.0 8.1 %collective-permute-done.8.refs_6_ = bf16[16,32,128]{2,1,0:T(8,128)(2,1)S(1)} collective-permute-done((bf16[16,32,128]{2,1,0:T(8,128)(2,1)S(1)}, bf16[16,32,128]{2,1,0:T(8,128)(2,1)S(1)}, u32[]{:S(2)}, u32[]{:S(2)}) %collective-permute-start.8) | collective-permute-done | bytes 131104 | tf_op jit(solution)/shard_map/ppermute | solution.py:452
  33.1 0.0 collective-permute-done.1.refs_0_
  33.1 0.0 collective-permute-done.2.refs_1_
  33.1 0.0 collective-permute-done.3.refs_2_
  33.1 0.0 copy-done
  33.1 1.4 %peaks.1 = (f32[1,16]{1,0:T(1,128)}, f32[1,16]{1,0:T(1,128)}) custom-call(bf16[16,32,128]{2,1,0:T(8,128)(2,1)S(1)} %collective-permute-done.1.refs_0_, bf16[16,32,128]{2,1,0:T(8,128)(2,1)S(1)} %collective-permute-done.2.refs_1_, bf16[16,32,128]{2,1,0:T(8,128)(2,1)S(1)} %collective-permute-done.3.refs_2_, ...), custom_call_target="tpu_custom_call" | custom-call | tf_op jit(solution)/shard_map/peaks/pallas_call | solution.py:405
Async XLA Ops:
  4.2 2.1 %collective-permute-start.4 = (bf16[32,64,128]{2,1,0:T(8,128)(2,1)S(1)}, bf16[32,64,128]{2,1,0:T(8,128)(2,1)S(1)}, u32[]{:S(2)}, u32[]{:S(2)}) collective-permute-start(bf16[32,64,128]{2,1,0:T(8,128)(2,1)S(1)} %get-tuple-element.24), channel_id=1, source_target_pairs={{0,1},{1,0},{2,3},{3,2},{4,5},{5,4},{6,7},{7,6},{8,9},{9,8},{10,11... | collective-permute-start | bytes 1572872 | tf_op jit(solution)/shard_map/ppermute | solution.py:264
  4.7 10.3 %collective-permute-start = (bf16[32,64,128]{2,1,0:T(8,128)(2,1)S(1)}, bf16[32,64,128]{2,1,0:T(8,128)(2,1)S(1)}, u32[]{:S(2)}, u32[]{:S(2)}) collective-permute-start(bf16[32,64,128]{2,1,0:T(8,128)(2,1)S(1)} %get-tuple-element.20), channel_id=1, source_target_pairs={{0,1},{1,0},{2,3},{3,2},{4,5},{5,4},{6,7},{7,6},{8,9},{9,8},{10,11... | collective-permute-start | bytes 1572872 | tf_op jit(solution)/shard_map/ppermute | solution.py:265
  6.0 27.1 %copy-start = (f32[1,16]{1,0:T(1,128)S(1)}, f32[1,16]{1,0:T(1,128)}, u32[]{:S(2)}) copy-start(f32[1,16]{1,0:T(1,128)} %refs_9_.1) | copy-start | bytes 196
  6.6 9.2 %collective-permute-start.5 = (bf16[16,32,128]{2,1,0:T(8,128)(2,1)S(1)}, bf16[16,32,128]{2,1,0:T(8,128)(2,1)S(1)}, u32[]{:S(2)}, u32[]{:S(2)}) collective-permute-start(bf16[16,32,128]{2,1,0:T(8,128)(2,1)S(1)} %get-tuple-element.25), channel_id=1, source_target_pairs={{0,2},{2,0},{4,8},{6,10},{8,4},{10,6},{12,14},{14,12},{1,3},{3,1},... | collective-permute-start | bytes 393224 | tf_op jit(solution)/shard_map/ppermute | solution.py:452
  9.5 9.8 %collective-permute-start.6 = (bf16[16,32,128]{2,1,0:T(8,128)(2,1)S(1)}, bf16[16,32,128]{2,1,0:T(8,128)(2,1)S(1)}, u32[]{:S(2)}, u32[]{:S(2)}) collective-permute-start(bf16[16,32,128]{2,1,0:T(8,128)(2,1)S(1)} %get-tuple-element.26), channel_id=1, source_target_pairs={{0,4},{2,6},{4,0},{6,2},{8,12},{10,14},{12,8},{14,10},{1,5},{3,7},... | collective-permute-start | bytes 393224 | tf_op jit(solution)/shard_map/ppermute | solution.py:452
  11.2 13.8 %collective-permute-start.7 = (bf16[16,32,128]{2,1,0:T(8,128)(2,1)S(1)}, bf16[16,32,128]{2,1,0:T(8,128)(2,1)S(1)}, u32[]{:S(2)}, u32[]{:S(2)}) collective-permute-start(bf16[16,32,128]{2,1,0:T(8,128)(2,1)S(1)} %get-tuple-element.27), channel_id=1, source_target_pairs={{0,10},{2,8},{4,14},{6,12},{8,2},{10,0},{12,6},{14,4},{1,11},{3,9}... | collective-permute-start | bytes 393224 | tf_op jit(solution)/shard_map/ppermute | solution.py:452
  13.6 19.5 %collective-permute-start.8 = (bf16[16,32,128]{2,1,0:T(8,128)(2,1)S(1)}, bf16[16,32,128]{2,1,0:T(8,128)(2,1)S(1)}, u32[]{:S(2)}, u32[]{:S(2)}) collective-permute-start(bf16[16,32,128]{2,1,0:T(8,128)(2,1)S(1)} %get-tuple-element.28), channel_id=1, source_target_pairs={{0,8},{2,10},{4,12},{6,14},{8,0},{10,2},{12,4},{14,6},{1,9},{3,11}... | collective-permute-start | bytes 393224 | tf_op jit(solution)/shard_map/ppermute | solution.py:452
  15.3 17.7 %collective-permute-start.1 = (bf16[16,32,128]{2,1,0:T(8,128)(2,1)S(1)}, bf16[16,32,128]{2,1,0:T(8,128)(2,1)S(1)}, u32[]{:S(2)}, u32[]{:S(2)}) collective-permute-start(bf16[16,32,128]{2,1,0:T(8,128)(2,1)S(1)} %get-tuple-element.21), channel_id=1, source_target_pairs={{0,6},{2,4},{4,2},{6,0},{8,14},{10,12},{12,10},{14,8},{1,7},{3,5},... | collective-permute-start | bytes 393224 | tf_op jit(solution)/shard_map/ppermute | solution.py:452
  15.8 17.3 %collective-permute-start.2 = (bf16[16,32,128]{2,1,0:T(8,128)(2,1)S(1)}, bf16[16,32,128]{2,1,0:T(8,128)(2,1)S(1)}, u32[]{:S(2)}, u32[]{:S(2)}) collective-permute-start(bf16[16,32,128]{2,1,0:T(8,128)(2,1)S(1)} %get-tuple-element.22), channel_id=1, source_target_pairs={{0,14},{2,12},{4,10},{6,8},{8,6},{10,4},{12,2},{14,0},{1,15},{3,13... | collective-permute-start | bytes 393224 | tf_op jit(solution)/shard_map/ppermute | solution.py:452
  19.3 13.8 %collective-permute-start.3 = (bf16[16,32,128]{2,1,0:T(8,128)(2,1)S(1)}, bf16[16,32,128]{2,1,0:T(8,128)(2,1)S(1)}, u32[]{:S(2)}, u32[]{:S(2)}) collective-permute-start(bf16[16,32,128]{2,1,0:T(8,128)(2,1)S(1)} %get-tuple-element.23), channel_id=1, source_target_pairs={{0,12},{2,14},{4,6},{6,4},{8,10},{10,8},{12,0},{14,2},{1,13},{3,15... | collective-permute-start | bytes 393224 | tf_op jit(solution)/shard_map/ppermute | solution.py:452
